TPU v7x, 256 devices: a whole 4x4x8 slice. The times are simulated.
256 devices in a mesh: freq: 16 (over y_lo, x, core), blk: 16 (over y_hi, z).
Axes of the slice: x: 4, y: 4 (y_hi: 2, y_lo: 2; y = y_hi * 2 + y_lo), z: 8, core: 2. Of those that a mesh axis runs over, the one named last changes fastest.
Arguments:
- samples: bfloat16 [16, 128, 69376], P('blk', 'freq'), may hold values from -6 to 6
- chan_list: int32 [128], replicated, may hold values from 0 to 128, as said below
Outputs:
- visibilities: bfloat16 [128, 16, 9, 2, 128, 128], P('freq', 'blk')
Inputs may be any that keep to these rules, and one draw needn't show every extreme that they name: `chan_list`: 128 distinct bins in increasing order, the first 0 and the last 128.
All inputs are finite; a program needn't handle non-finite values.
Results may differ from a plain program's by a relative error of at most 0.0065.
Values may be sent and summed in bfloat16 or wider, within the bound.
No kernel may reach another device: no remote copies, remote signals or barrier semaphores. Data moves between devices by JAX's collectives and lax.ppermute only.
A program may use at most 64 MiB of HBM per device.

v0:
```python
import jax
import jax.numpy as jnp
from jax import lax
from jax.sharding import PartitionSpec as P

POINTS = 256
TAPS = 16
CHANNELS = 128
SPECTRA = 256


def from_behind(value, axis, steps):
    count = lax.axis_size(axis)
    pairs = [(source, (source + steps) % count) for source in range(count)]
    return lax.ppermute(value, axis, pairs)


def filter_table(chan_list):
    window_len = TAPS * POINTS
    position = jnp.arange(window_len, dtype=jnp.float32)
    offset_pos = (position - window_len / 2 + 0.5) / POINTS
    taper = 0.5 - 0.5 * jnp.cos(2.0 * jnp.pi * (position + 0.5) / window_len)
    window = jnp.sin(jnp.pi * offset_pos) / (jnp.pi * offset_pos) * taper
    window = window / jnp.sqrt(jnp.sum(window * window))
    window = window.reshape(TAPS, POINTS)
    columns = jnp.arange(POINTS, dtype=jnp.int32)
    angles = (chan_list[:, None] * columns[None, :] % POINTS).astype(jnp.float32) * (
        2.0 * jnp.pi / POINTS
    )
    cosines = window[:, None, :] * jnp.cos(angles)[None, :, :]
    sine_part = -window[:, None, :] * jnp.sin(angles)[None, :, :]
    return jnp.concatenate([cosines, sine_part], axis=1).astype(jnp.bfloat16)


def correlate(turned):
    own_tile = turned[:, 0]
    chan_count = own_tile.shape[1]
    tile_rows = own_tile.shape[2]
    stacked = jnp.stack(
        [
            jnp.concatenate([own_tile[0], own_tile[1]], axis=1),
            jnp.concatenate([own_tile[1], -own_tile[0]], axis=1),
        ]
    )

    def cross_block(moving):
        product = lax.dot_general(
            stacked, moving, (((0, 3), (0, 3)), ((1,), (1,))), preferred_element_type=jnp.float32
        )
        return (
            (product * (1.0 / SPECTRA))
            .astype(jnp.bfloat16)
            .reshape(chan_count, 2, tile_rows, tile_rows)
        )

    loop_size = lax.axis_size("blk")
    offsets = loop_size // 2 + 1
    result = jnp.zeros((chan_count, offsets, 2, tile_rows, tile_rows), jnp.bfloat16)
    result = lax.dynamic_update_index_in_dim(result, cross_block(own_tile), 0, 1)

    def advance(offset_idx, state_pair):
        moving = from_behind(state_pair[0], "blk", 1)
        return (
            moving,
            lax.dynamic_update_index_in_dim(state_pair[1], cross_block(moving), offset_idx, 1),
        )

    result = lax.fori_loop(1, offsets, advance, (own_tile, result))[1]
    return result[:, None]


def body(samples, chan_list):
    filters = filter_table(chan_list)
    per_device = samples.shape[1]
    frames = samples.reshape(per_device, samples.shape[2] // POINTS, POINTS)

    def add_tap(tap_index, running):
        segment = lax.dynamic_slice_in_dim(frames, tap_index, SPECTRA, 1)
        weights = lax.dynamic_index_in_dim(filters, tap_index, 0, keepdims=False)
        return running + jnp.einsum(
            "kn,isn->kis", weights, segment, preferred_element_type=jnp.float32
        )

    running = jnp.zeros((2 * CHANNELS, per_device, SPECTRA), jnp.float32)
    voltages = lax.fori_loop(0, TAPS, add_tap, running).astype(jnp.bfloat16)
    freq_size = lax.axis_size("freq")
    sectioned = voltages.reshape(2, freq_size, CHANNELS // freq_size, per_device, SPECTRA)
    return correlate(lax.all_to_all(sectioned, "freq", split_axis=1, concat_axis=3, tiled=True))


def solution(mesh):
    in_specs = (P("blk", "freq", None), P())
    out_specs = P("freq", "blk", None, None, None, None)
    return jax.shard_map(body, mesh=mesh, in_specs=in_specs, out_specs=out_specs, check_vma=False)
```

profile of v0, /device:TPU:6, one launch (start us, length us, event | category | flops | bytes accessed | tf_op | source)
XLA Modules:
  0.0 303.9 jit_solution(16558006394165354900)
XLA Ops:
  0.0 0.7 fusion.25
  1.7 1.2 fusion.15
  3.0 0.6 multiply_convert_fusion
  3.6 1.5 pad_maximum_fusion
  5.2 28.9 %while.32 = (s32[]{:T(128)}, f32[256,8,256]{2,0,1:T(8,128)S(1)}, bf16[16,256,256]{2,1,0:T(8,128)(2,1)}, bf16[8,271,256]{2,0,1:T(8,128)(2,1)S(1)}, s32[]{:T(128)}, /*index=5*/s32[]{:T(128)}) while((s32[]{:T(128)}, f32[256,8,256]{2,0,1:T(8,128)S(1)}, bf16[16,256,256]{2,1,0:T(8,128)(2,1)}, bf16[8,271,256]{2,0,1:T(8,128)(2,1)S(1)}, ...), condition=%wide.region_2.3_spmd.clone, body=%wide.region_1.2_spmd.clone.sunk | while | flops 269484032 | bytes 7471199 | solution.py:85
  5.3 1.7 select_add_fusion.2
  7.1 1.7 select_add_fusion.2
  8.9 1.7 select_add_fusion.2
  10.7 1.7 select_add_fusion.2
  12.5 1.7 select_add_fusion.2
  14.3 1.7 select_add_fusion.2
  16.1 1.7 select_add_fusion.2
  17.9 1.7 select_add_fusion.2
  19.8 1.7 select_add_fusion.2
  21.6 1.7 select_add_fusion.2
  23.4 1.7 select_add_fusion.2
  25.2 1.7 select_add_fusion.2
  27.0 1.7 select_add_fusion.2
  28.8 1.7 select_add_fusion.2
  30.6 1.7 select_add_fusion.2
  32.4 1.7 select_add_fusion.2
  34.1 1.1 copy.37
  35.3 1.1 copy.18
  36.3 5.8 %all-to-all-start = ((bf16[2,16,8,8,256]{4,3,0,2,1:T(8,128)(2,1)}), bf16[2,16,8,8,256]{4,3,0,2,1:T(8,128)(2,1)S(1)}, u32[]{:S(2)}, u32[]{:S(2)}) async-start(bf16[2,16,8,8,256]{4,3,0,2,1:T(8,128)(2,1)} %copy.18), calls=%async_computation | async-start | bytes 2097152 | tf_op jit(solution)/shard_map/all_to_all | solution.py:88
  42.1 13.3 %all-to-all-done = bf16[2,16,8,8,256]{4,3,0,2,1:T(8,128)(2,1)S(1)} async-done(((bf16[2,16,8,8,256]{4,3,0,2,1:T(8,128)(2,1)}), bf16[2,16,8,8,256]{4,3,0,2,1:T(8,128)(2,1)S(1)}, u32[]{:S(2)}, u32[]{:S(2)}) %all-to-all-start) | async-done | bytes 1048608 | tf_op jit(solution)/shard_map/all_to_all | solution.py:88
  55.7 0.2 maximum_bitcast_fusion
  56.1 0.7 fusion.7
  56.9 3.2 %dynamic_update_slice.14 = bf16[8,9,2,128,128]{4,3,2,0,1:T(8,128)(2,1)} pad(bf16[8,1,2,128,128]{4,3,2,0,1:T(8,128)(2,1)S(1)} %bitcast.68, bf16[]{:T(256)} %constant.140.clone.1), padding=0_0x0_8x0_0x0_0x0_0 | pad | bytes 5242882 | tf_op jit(solution)/shard_map/jit(dynamic_update_index_in_dim)/dynamic_update_slice | solution.py:59
  60.1 1.1 copy_bitcast_fusion.1
  61.2 236.4 %while.31 = (s32[]{:T(128)}, bf16[2,8,128,256]{3,2,0,1:T(8,128)(2,1)}, bf16[8,9,2,128,128]{4,3,2,0,1:T(8,128)(2,1)}, bf16[2,8,256,256]{3,2,0,1:T(8,128)(2,1)S(1)}, s32[]{:T(128)}, /*index=5*/s32[]{:T(128)}, s32[]{:T(128)}) while((s32[]{:T(128)}, bf16[2,8,128,256]{3,2,0,1:T(8,128)(2,1)}, bf16[8,9,2,128,128]{4,3,2,0,1:T(8,128)(2,1)}, ...), condition=%wide.region_4.5_spmd, body=%wide.region_3.4_spmd.sunk | while | flops 268959744 | bytes 11010203 | solution.py:68
  61.2 1.9 collective-permute-start
  63.1 30.5 %collective-permute-done = bf16[2,8,128,256]{3,2,0,1:T(8,128)(2,1)S(1)} collective-permute-done((bf16[2,8,128,256]{3,2,0,1:T(8,128)(2,1)}, bf16[2,8,128,256]{3,2,0,1:T(8,128)(2,1)S(1)}, u32[]{:S(2)}, u32[]{:S(2)}) %collective-permute-start) | collective-permute-done | bytes 1048608 | tf_op jit(solution)/shard_map/while/body/eval_jaxpr/ppermute | solution.py:15
  93.6 0.7 fusion.40
  94.3 0.8 constant_dynamic-update-slice_fusion.2
  95.1 1.0 copy.57
  96.1 29.0 %collective-permute-done = bf16[2,8,128,256]{3,2,0,1:T(8,128)(2,1)S(1)} collective-permute-done((bf16[2,8,128,256]{3,2,0,1:T(8,128)(2,1)}, bf16[2,8,128,256]{3,2,0,1:T(8,128)(2,1)S(1)}, u32[]{:S(2)}, u32[]{:S(2)}) %collective-permute-start) | collective-permute-done | bytes 1048608 | tf_op jit(solution)/shard_map/while/body/eval_jaxpr/ppermute | solution.py:15
  125.0 0.7 fusion.40
  125.7 0.9 constant_dynamic-update-slice_fusion.2
  126.6 1.0 copy.57
  127.6 28.1 %collective-permute-done = bf16[2,8,128,256]{3,2,0,1:T(8,128)(2,1)S(1)} collective-permute-done((bf16[2,8,128,256]{3,2,0,1:T(8,128)(2,1)}, bf16[2,8,128,256]{3,2,0,1:T(8,128)(2,1)S(1)}, u32[]{:S(2)}, u32[]{:S(2)}) %collective-permute-start) | collective-permute-done | bytes 1048608 | tf_op jit(solution)/shard_map/while/body/eval_jaxpr/ppermute | solution.py:15
  155.7 0.7 fusion.40
  156.4 0.8 constant_dynamic-update-slice_fusion.2
  157.2 1.0 copy.57
  158.2 27.2 %collective-permute-done = bf16[2,8,128,256]{3,2,0,1:T(8,128)(2,1)S(1)} collective-permute-done((bf16[2,8,128,256]{3,2,0,1:T(8,128)(2,1)}, bf16[2,8,128,256]{3,2,0,1:T(8,128)(2,1)S(1)}, u32[]{:S(2)}, u32[]{:S(2)}) %collective-permute-start) | collective-permute-done | bytes 1048608 | tf_op jit(solution)/shard_map/while/body/eval_jaxpr/ppermute | solution.py:15
  185.4 0.7 fusion.40
  186.1 0.8 constant_dynamic-update-slice_fusion.2
  187.0 1.0 copy.57
  187.9 26.3 %collective-permute-done = bf16[2,8,128,256]{3,2,0,1:T(8,128)(2,1)S(1)} collective-permute-done((bf16[2,8,128,256]{3,2,0,1:T(8,128)(2,1)}, bf16[2,8,128,256]{3,2,0,1:T(8,128)(2,1)S(1)}, u32[]{:S(2)}, u32[]{:S(2)}) %collective-permute-start) | collective-permute-done | bytes 1048608 | tf_op jit(solution)/shard_map/while/body/eval_jaxpr/ppermute | solution.py:15
  214.2 0.7 fusion.40
  214.9 0.8 constant_dynamic-update-slice_fusion.2
  215.8 1.0 copy.57
  216.7 25.3 %collective-permute-done = bf16[2,8,128,256]{3,2,0,1:T(8,128)(2,1)S(1)} collective-permute-done((bf16[2,8,128,256]{3,2,0,1:T(8,128)(2,1)}, bf16[2,8,128,256]{3,2,0,1:T(8,128)(2,1)S(1)}, u32[]{:S(2)}, u32[]{:S(2)}) %collective-permute-start) | collective-permute-done | bytes 1048608 | tf_op jit(solution)/shard_map/while/body/eval_jaxpr/ppermute | solution.py:15
  242.1 0.7 fusion.40
  242.8 0.8 constant_dynamic-update-slice_fusion.2
  243.6 1.0 copy.57
  244.6 24.4 %collective-permute-done = bf16[2,8,128,256]{3,2,0,1:T(8,128)(2,1)S(1)} collective-permute-done((bf16[2,8,128,256]{3,2,0,1:T(8,128)(2,1)}, bf16[2,8,128,256]{3,2,0,1:T(8,128)(2,1)S(1)}, u32[]{:S(2)}, u32[]{:S(2)}) %collective-permute-start) | collective-permute-done | bytes 1048608 | tf_op jit(solution)/shard_map/while/body/eval_jaxpr/ppermute | solution.py:15
  269.0 0.7 fusion.40
  269.7 0.8 constant_dynamic-update-slice_fusion.2
  270.6 1.0 copy.57
  271.5 23.5 %collective-permute-done = bf16[2,8,128,256]{3,2,0,1:T(8,128)(2,1)S(1)} collective-permute-done((bf16[2,8,128,256]{3,2,0,1:T(8,128)(2,1)}, bf16[2,8,128,256]{3,2,0,1:T(8,128)(2,1)S(1)}, u32[]{:S(2)}, u32[]{:S(2)}) %collective-permute-start) | collective-permute-done | bytes 1048608 | tf_op jit(solution)/shard_map/while/body/eval_jaxpr/ppermute | solution.py:15
  295.0 0.7 fusion.40
  295.8 0.8 constant_dynamic-update-slice_fusion.2
  296.6 1.0 copy.57
  297.6 6.4 %copy.38 = bf16[8,9,2,128,128]{4,3,2,1,0:T(8,128)(2,1)} copy(bf16[8,9,2,128,128]{4,3,2,0,1:T(8,128)(2,1)} %get-tuple-element.195) | data formatting | bytes 9437184 | tf_op jit(solution)/shard_map/while | solution.py:68
  (33 shorter events, 2.0 us)
Async XLA Ops:
  3.6 1.6 copy-start
  36.3 19.1 %all-to-all-start = ((bf16[2,16,8,8,256]{4,3,0,2,1:T(8,128)(2,1)}), bf16[2,16,8,8,256]{4,3,0,2,1:T(8,128)(2,1)S(1)}, u32[]{:S(2)}, u32[]{:S(2)}) async-start(bf16[2,16,8,8,256]{4,3,0,2,1:T(8,128)(2,1)} %copy.18), calls=%async_computation | async-start | bytes 2097152 | tf_op jit(solution)/shard_map/all_to_all | solution.py:88
  61.2 32.4 %collective-permute-start = (bf16[2,8,128,256]{3,2,0,1:T(8,128)(2,1)}, bf16[2,8,128,256]{3,2,0,1:T(8,128)(2,1)S(1)}, u32[]{:S(2)}, u32[]{:S(2)}) collective-permute-start(bf16[2,8,128,256]{3,2,0,1:T(8,128)(2,1)} %get-tuple-element.323), channel_id=1, source_target_pairs={{0,1},{1,2},{2,3},{3,4},{4,5},{5,6},{6,7},{7,8},{8,9},{9,10},{10,1... | collective-permute-start | bytes 3145736 | tf_op jit(solution)/shard_map/while/body/eval_jaxpr/ppermute | solution.py:15
  96.1 29.0 %collective-permute-start = (bf16[2,8,128,256]{3,2,0,1:T(8,128)(2,1)}, bf16[2,8,128,256]{3,2,0,1:T(8,128)(2,1)S(1)}, u32[]{:S(2)}, u32[]{:S(2)}) collective-permute-start(bf16[2,8,128,256]{3,2,0,1:T(8,128)(2,1)} %get-tuple-element.323), channel_id=1, source_target_pairs={{0,1},{1,2},{2,3},{3,4},{4,5},{5,6},{6,7},{7,8},{8,9},{9,10},{10,1... | collective-permute-start | bytes 3145736 | tf_op jit(solution)/shard_map/while/body/eval_jaxpr/ppermute | solution.py:15
  127.6 28.1 %collective-permute-start = (bf16[2,8,128,256]{3,2,0,1:T(8,128)(2,1)}, bf16[2,8,128,256]{3,2,0,1:T(8,128)(2,1)S(1)}, u32[]{:S(2)}, u32[]{:S(2)}) collective-permute-start(bf16[2,8,128,256]{3,2,0,1:T(8,128)(2,1)} %get-tuple-element.323), channel_id=1, source_target_pairs={{0,1},{1,2},{2,3},{3,4},{4,5},{5,6},{6,7},{7,8},{8,9},{9,10},{10,1... | collective-permute-start | bytes 3145736 | tf_op jit(solution)/shard_map/while/body/eval_jaxpr/ppermute | solution.py:15
  158.2 27.2 %collective-permute-start = (bf16[2,8,128,256]{3,2,0,1:T(8,128)(2,1)}, bf16[2,8,128,256]{3,2,0,1:T(8,128)(2,1)S(1)}, u32[]{:S(2)}, u32[]{:S(2)}) collective-permute-start(bf16[2,8,128,256]{3,2,0,1:T(8,128)(2,1)} %get-tuple-element.323), channel_id=1, source_target_pairs={{0,1},{1,2},{2,3},{3,4},{4,5},{5,6},{6,7},{7,8},{8,9},{9,10},{10,1... | collective-permute-start | bytes 3145736 | tf_op jit(solution)/shard_map/while/body/eval_jaxpr/ppermute | solution.py:15
  187.9 26.3 %collective-permute-start = (bf16[2,8,128,256]{3,2,0,1:T(8,128)(2,1)}, bf16[2,8,128,256]{3,2,0,1:T(8,128)(2,1)S(1)}, u32[]{:S(2)}, u32[]{:S(2)}) collective-permute-start(bf16[2,8,128,256]{3,2,0,1:T(8,128)(2,1)} %get-tuple-element.323), channel_id=1, source_target_pairs={{0,1},{1,2},{2,3},{3,4},{4,5},{5,6},{6,7},{7,8},{8,9},{9,10},{10,1... | collective-permute-start | bytes 3145736 | tf_op jit(solution)/shard_map/while/body/eval_jaxpr/ppermute | solution.py:15
  216.7 25.4 %collective-permute-start = (bf16[2,8,128,256]{3,2,0,1:T(8,128)(2,1)}, bf16[2,8,128,256]{3,2,0,1:T(8,128)(2,1)S(1)}, u32[]{:S(2)}, u32[]{:S(2)}) collective-permute-start(bf16[2,8,128,256]{3,2,0,1:T(8,128)(2,1)} %get-tuple-element.323), channel_id=1, source_target_pairs={{0,1},{1,2},{2,3},{3,4},{4,5},{5,6},{6,7},{7,8},{8,9},{9,10},{10,1... | collective-permute-start | bytes 3145736 | tf_op jit(solution)/shard_map/while/body/eval_jaxpr/ppermute | solution.py:15
  244.6 24.4 %collective-permute-start = (bf16[2,8,128,256]{3,2,0,1:T(8,128)(2,1)}, bf16[2,8,128,256]{3,2,0,1:T(8,128)(2,1)S(1)}, u32[]{:S(2)}, u32[]{:S(2)}) collective-permute-start(bf16[2,8,128,256]{3,2,0,1:T(8,128)(2,1)} %get-tuple-element.323), channel_id=1, source_target_pairs={{0,1},{1,2},{2,3},{3,4},{4,5},{5,6},{6,7},{7,8},{8,9},{9,10},{10,1... | collective-permute-start | bytes 3145736 | tf_op jit(solution)/shard_map/while/body/eval_jaxpr/ppermute | solution.py:15
  271.5 23.5 %collective-permute-start = (bf16[2,8,128,256]{3,2,0,1:T(8,128)(2,1)}, bf16[2,8,128,256]{3,2,0,1:T(8,128)(2,1)S(1)}, u32[]{:S(2)}, u32[]{:S(2)}) collective-permute-start(bf16[2,8,128,256]{3,2,0,1:T(8,128)(2,1)} %get-tuple-element.323), channel_id=1, source_target_pairs={{0,1},{1,2},{2,3},{3,4},{4,5},{5,6},{6,7},{7,8},{8,9},{9,10},{10,1... | collective-permute-start | bytes 3145736 | tf_op jit(solution)/shard_map/while/body/eval_jaxpr/ppermute | solution.py:15
where the time goes:
time: 304 us
  waiting for transfers between devices  228 us (75%)
  matrix products  33.6 us (11%)
  local copies, waits for them, and re-layouts  28.8 us (9%)
  starting transfers between devices  7.74 us (3%)
  other arithmetic  4.81 us (2%)
    ppermute x8, waiting for transfers between devices, from_behind(): return lax.ppermute(value, axis, pairs)  214 us
    dot_general x16, matrix products, add_tap(): jnp.einsum('kn,isn->kis', weights, segment, preferred_element_type=jnp.fl...  27.3 us
    all_to_all x1, waiting for transfers between devices, body(): lax.all_to_all(sectioned, 'freq', split_axis=1, concat_axis=3, tiled=True)  13.3 us
    while x8, local copies, waits for them, and re-layouts  7.76 us
    dynamic_update_slice x8, local copies, waits for them, and re-layouts, advance(): lax.dynamic_update_index_in_dim(state_pair[1], cross_block(moving), offse...  6.71 us
    dot_general x9, matrix products, cross_block(): lax.dot_general(stacked, moving, (((0, 3), (0, 3)), ((1,), (1,))), prefer...  6.36 us
    while x1, local copies, waits for them, and re-layouts, correlate(): result = lax.fori_loop(1, offsets, advance, (own_tile, result))[1]  6.36 us
  transfers between devices with their start and end apart: 9, of which 9 were waited for; matrix products, arithmetic and copies ran while one was open for 0% of the time, Pallas kernels for 0%

commit v1 on v0

v1 whole, which is shorter than its diff:
```python
import jax
import jax.numpy as jnp
from jax import lax
from jax.sharding import PartitionSpec as P

POINTS = 256
TAPS = 16
CHANNELS = 128
SPECTRA = 256
CHUNKS = 2


def shifted(value, steps):
    count = lax.axis_size("blk")
    return lax.ppermute(value, "blk", [(b, (b + steps) % count) for b in range(count)])


def filter_tables(chan_list, freq_size):
    window_len = TAPS * POINTS
    position = jnp.arange(window_len, dtype=jnp.float32)
    offset_pos = (position - window_len / 2 + 0.5) / POINTS
    taper = 0.5 - 0.5 * jnp.cos(2.0 * jnp.pi * (position + 0.5) / window_len)
    window = jnp.sin(jnp.pi * offset_pos) / (jnp.pi * offset_pos) * taper
    window = window / jnp.sqrt(jnp.sum(window * window))
    window = window.reshape(TAPS, 1, POINTS)
    columns = jnp.arange(POINTS, dtype=jnp.int32)
    angles = (chan_list[:, None] * columns[None, :] % POINTS).astype(jnp.float32) * (
        2.0 * jnp.pi / POINTS
    )
    waves = jnp.stack([jnp.cos(angles), -jnp.sin(angles)], axis=0)
    waves = waves.reshape(2, freq_size, CHUNKS, -1, POINTS).transpose(2, 1, 0, 3, 4)
    return [
        (window * waves[chunk].reshape(1, -1, POINTS)).astype(jnp.bfloat16)
        for chunk in range(CHUNKS)
    ]


def channelize(frames, filters):
    return lax.conv_general_dilated(
        frames,
        filters,
        window_strides=(1,),
        padding="VALID",
        dimension_numbers=("NWC", "WOI", "CNW"),
        preferred_element_type=jnp.float32,
    ).astype(jnp.bfloat16)


def cross_block(stacked, moving):
    product = lax.dot_general(
        stacked, moving, (((0, 3), (0, 3)), ((1,), (1,))), preferred_element_type=jnp.float32
    )
    chan_count, _, tile = product.shape
    return (product * (1.0 / SPECTRA)).astype(jnp.bfloat16).reshape(chan_count, 2, tile, tile)


def stack_parts(own):
    return jnp.stack(
        [
            jnp.concatenate([own[0], own[1]], axis=1),
            jnp.concatenate([own[1], -own[0]], axis=1),
        ]
    )


def body(samples, chan_list):
    freq_size = lax.axis_size("freq")
    inputs = samples.shape[1]
    frames = samples.reshape(inputs, samples.shape[2] // POINTS, POINTS)
    tables = filter_tables(chan_list, freq_size)
    chans = CHANNELS // freq_size // CHUNKS

    turned = []
    for chunk in range(CHUNKS):
        voltages = channelize(frames, tables[chunk])
        sectioned = voltages.reshape(freq_size, 2, chans, inputs, SPECTRA)
        turned.append(
            lax.all_to_all(sectioned, "freq", split_axis=0, concat_axis=3, tiled=True).reshape(
                2, chans, freq_size * inputs, SPECTRA
            )
        )
    half = lax.axis_size("blk") // 2
    rows = []
    for chunk in range(CHUNKS):
        own = turned[chunk]
        stacked = stack_parts(own)
        blocks = [None] * (half + 1)
        blocks[0] = own
        ups = half // 2 if chunk % 2 == 0 else half // 2 - 1
        for offset in range(1, ups + 1):
            blocks[offset] = shifted(blocks[offset - 1], 1)
        blocks[half - 1] = shifted(own, half - 1)
        for offset in range(half - 2, ups, -1):
            blocks[offset] = shifted(blocks[offset + 1], -1)
        blocks[half] = shifted(own, half)
        rows.append(jnp.stack([cross_block(stacked, block) for block in blocks], axis=1))
    return jnp.concatenate(rows, axis=0)[:, None]


def solution(mesh):
    in_specs = (P("blk", "freq", None), P())
    out_specs = P("freq", "blk", None, None, None, None)
    return jax.shard_map(body, mesh=mesh, in_specs=in_specs, out_specs=out_specs, check_vma=False)
```

time: 304 us -> 179 us (0.59)
  waiting for transfers between devices: 228 us -> 104 us
  starting transfers between devices: 7.74 us -> 44.8 us
  local copies, waits for them, and re-layouts: 28.8 us -> 4.49 us
  matrix products: 33.6 us -> 18.9 us
    ppermute x8 -> x16, waiting for transfers between devices: 214 us -> 81 us  [shifted(): lax.ppermute(value, 'blk', [(b, (b + steps) % count) for b in range(count)])]
    ppermute x8 -> x16, starting transfers between devices: 1.94 us -> 32.7 us  [shifted(): lax.ppermute(value, 'blk', [(b, (b + steps) % count) for b in range(count)])]
    dot_general x16 -> x0, matrix products: 27.3 us -> none  [add_tap(): jnp.einsum('kn,isn->kis', weights, segment, preferred_element_type=jnp.fl...]
    while x10 -> x0, local copies, waits for them, and re-layouts: 15.2 us -> none
    all_to_all x1 -> x2, waiting for transfers between devices: 13.3 us -> 23.5 us  [body(): lax.all_to_all(sectioned, 'freq', split_axis=0, concat_axis=3, tiled=True)]
    dynamic_update_slice x9 -> x0, local copies, waits for them, and re-layouts: 9.95 us -> none  [the longest x8 6.71 us: advance(): lax.dynamic_update_index_in_dim(state_pair[1], cross_block(moving), offse...]
    conv_general_dilated x0 -> x2, matrix products: none -> 9.03 us  [channelize(): lax.conv_general_dilated(frames, filters, window_strides=(1,), padding='V...]
    all_to_all x1 -> x2, starting transfers between devices: 5.8 us -> 12.2 us  [body(): lax.all_to_all(sectioned, 'freq', split_axis=0, concat_axis=3, tiled=True)]
  transfers between devices with their start and end apart: 9 -> 18, of which waited for: 9 -> 10; matrix products, arithmetic and copies ran while one was open for 0% -> 9% of each run, Pallas kernels for 0% -> 0%
where the time goes in v1:
time: 179 us
  waiting for transfers between devices  104 us (58%)
  starting transfers between devices  44.8 us (25%)
  matrix products  18.9 us (11%)
  other arithmetic  4.95 us (3%)
  local copies, waits for them, and re-layouts  4.49 us (3%)
    ppermute x16, waiting for transfers between devices, shifted(): lax.ppermute(value, 'blk', [(b, (b + steps) % count) for b in range(count)])  81 us
    ppermute x16, starting transfers between devices, shifted(): lax.ppermute(value, 'blk', [(b, (b + steps) % count) for b in range(count)])  32.7 us
    all_to_all x2, waiting for transfers between devices, body(): lax.all_to_all(sectioned, 'freq', split_axis=0, concat_axis=3, tiled=True)  23.5 us
    all_to_all x2, starting transfers between devices, body(): lax.all_to_all(sectioned, 'freq', split_axis=0, concat_axis=3, tiled=True)  12.2 us
    dot_general x18, matrix products, cross_block(): lax.dot_general(stacked, moving, (((0, 3), (0, 3)), ((1,), (1,))), prefer...  9.9 us
    conv_general_dilated x2, matrix products, channelize(): lax.conv_general_dilated(frames, filters, window_strides=(1,), padding='V...  9.03 us
  transfers between devices with their start and end apart: 18, of which 10 were waited for; matrix products, arithmetic and copies ran while one was open for 9% of the time, Pallas kernels for 0%

profile of v1, /device:TPU:6, one launch (start us, length us, event | category | flops | bytes accessed | tf_op | source)
XLA Modules:
  0.0 178.9 jit_solution(868367390253192866)
XLA Ops:
  0.0 0.7 fusion.53
  1.4 0.1 fusion.45
  1.6 0.8 mul.177
  2.3 1.2 fusion.43
  3.6 0.1 maximum_bitcast_fusion.5
  3.7 4.5 %convolution_convert_fusion = bf16[128,8,256]{0,1,2:T(8,128)(2,1)S(1)} fusion(bf16[8,271,256]{2,0,1:T(8,128)(2,1)S(1)} %bitcast.252, f32[128,256]{1,0:T(8,128)S(1)} %mul.195, f32[16,256]{1,0:T(8,128)S(1)} %fusion.45), kind=kOutput, calls=%fused_computation.3 | convolution fusion | flops 2148794368 | bytes 1781760 | tf_op jit(solution)/shard_map/conv_general_dilated | solution.py:39
  8.3 1.4 copy.45
  9.6 5.8 %all-to-all-start.1 = ((bf16[16,2,4,8,256]{4,3,2,1,0:T(8,128)(2,1)}), bf16[16,2,4,8,256]{4,3,2,1,0:T(8,128)(2,1)S(1)}, u32[]{:S(2)}, u32[]{:S(2)}) async-start(bf16[16,2,4,8,256]{4,3,2,1,0:T(8,128)(2,1)} %bitcast.48), calls=%async_computation.1 | async-start | bytes 1048576 | tf_op jit(solution)/shard_map/all_to_all | solution.py:78
  15.5 4.5 %convolution_convert_fusion.1 = bf16[128,8,256]{0,1,2:T(8,128)(2,1)S(1)} fusion(bf16[8,271,256]{2,0,1:T(8,128)(2,1)S(1)} %bitcast.251, f32[128,256]{1,0:T(8,128)S(1)} %mul.183, f32[16,256]{1,0:T(8,128)S(1)} %fusion.45), kind=kOutput, calls=%fused_computation.4 | convolution fusion | flops 2148794368 | bytes 1781760 | tf_op jit(solution)/shard_map/conv_general_dilated | solution.py:39
  20.0 1.4 copy.31
  21.4 2.1 %all-to-all-done.1 = bf16[16,2,4,8,256]{4,3,2,1,0:T(8,128)(2,1)S(1)} async-done(((bf16[16,2,4,8,256]{4,3,2,1,0:T(8,128)(2,1)}), bf16[16,2,4,8,256]{4,3,2,1,0:T(8,128)(2,1)S(1)}, u32[]{:S(2)}, u32[]{:S(2)}) %all-to-all-start.1) | async-done | bytes 524320 | tf_op jit(solution)/shard_map/all_to_all | solution.py:78
  23.4 6.4 %all-to-all-start = ((bf16[16,2,4,8,256]{4,3,2,1,0:T(8,128)(2,1)}), bf16[16,2,4,8,256]{4,3,2,1,0:T(8,128)(2,1)S(1)}, u32[]{:S(2)}, u32[]{:S(2)}) async-start(bf16[16,2,4,8,256]{4,3,2,1,0:T(8,128)(2,1)} %bitcast.2), calls=%async_computation | async-start | bytes 1048576 | tf_op jit(solution)/shard_map/all_to_all | solution.py:78
  29.8 6.1 %collective-permute-start.11 = (bf16[2,4,128,256]{3,2,0,1:T(8,128)(2,1)S(1)}, bf16[2,4,128,256]{3,2,0,1:T(8,128)(2,1)}, u32[]{:S(2)}, u32[]{:S(2)}) collective-permute-start(bf16[2,4,128,256]{3,2,0,1:T(8,128)(2,1)S(1)} %copy_bitcast_fusion), channel_id=1, source_target_pairs={{0,7},{1,8},{2,9},{3,10},{4,11},{5,12},{6,13},{7,14},{8,15},{9,0},... | collective-permute-start | bytes 1572872 | tf_op jit(solution)/shard_map/ppermute | solution.py:15
  35.9 0.0 collective-permute-start.8
  35.9 2.9 %collective-permute-start.15 = (bf16[2,4,128,256]{3,2,0,1:T(8,128)(2,1)S(1)}, bf16[2,4,128,256]{3,2,0,1:T(8,128)(2,1)}, u32[]{:S(2)}, u32[]{:S(2)}) collective-permute-start(bf16[2,4,128,256]{3,2,0,1:T(8,128)(2,1)S(1)} %copy_bitcast_fusion), channel_id=1, source_target_pairs={{0,8},{1,9},{2,10},{3,11},{4,12},{5,13},{6,14},{7,15},{8,0},{9,1},... | collective-permute-start | bytes 1572872 | tf_op jit(solution)/shard_map/ppermute | solution.py:15
  38.8 21.4 %all-to-all-done = bf16[16,2,4,8,256]{4,3,2,1,0:T(8,128)(2,1)S(1)} async-done(((bf16[16,2,4,8,256]{4,3,2,1,0:T(8,128)(2,1)}), bf16[16,2,4,8,256]{4,3,2,1,0:T(8,128)(2,1)S(1)}, u32[]{:S(2)}, u32[]{:S(2)}) %all-to-all-start) | async-done | bytes 524320 | tf_op jit(solution)/shard_map/all_to_all | solution.py:78
  60.3 0.1 collective-permute-start.4
  60.4 4.3 %collective-permute-start = (bf16[2,4,128,256]{3,2,0,1:T(8,128)(2,1)S(1)}, bf16[2,4,128,256]{3,2,0,1:T(8,128)(2,1)S(1)}, u32[]{:S(2)}, u32[]{:S(2)}) collective-permute-start(bf16[2,4,128,256]{3,2,0,1:T(8,128)(2,1)S(1)} %copy_bitcast_fusion.1), channel_id=1, source_target_pairs={{0,1},{1,2},{2,3},{3,4},{4,5},{5,6},{6,7},{7,8},{8,9},{9,10},{10,1... | collective-permute-start | bytes 1572872 | tf_op jit(solution)/shard_map/ppermute | solution.py:15
  64.8 0.1 copy_bitcast_fusion.4
  65.0 0.1 maximum_bitcast_fusion.1
  65.1 0.4 fusion.35
  65.5 0.1 maximum_bitcast_fusion.3
  65.6 0.4 fusion.26
  66.1 0.0 collective-permute-done.11
  66.1 0.7 collective-permute-start.7
  66.8 1.5 fusion.19
  68.3 0.0 collective-permute-done.8
  68.3 3.7 %collective-permute-start.12 = (bf16[2,4,128,256]{3,2,0,1:T(8,128)(2,1)}, bf16[2,4,128,256]{3,2,0,1:T(8,128)(2,1)S(1)}, u32[]{:S(2)}, u32[]{:S(2)}) collective-permute-start(bf16[2,4,128,256]{3,2,0,1:T(8,128)(2,1)} %collective-permute-done.11), channel_id=1, source_target_pairs={{0,15},{1,0},{2,1},{3,2},{4,3},{5,4},{6,5},{7,6},{8,7},{9,8},{10,9... | collective-permute-start | bytes 1572872 | tf_op jit(solution)/shard_map/ppermute | solution.py:15
  72.0 0.4 fusion.25
  72.5 16.3 %collective-permute-done.4 = bf16[2,4,128,256]{3,2,0,1:T(8,128)(2,1)S(1)} collective-permute-done((bf16[2,4,128,256]{3,2,0,1:T(8,128)(2,1)S(1)}, bf16[2,4,128,256]{3,2,0,1:T(8,128)(2,1)S(1)}, u32[]{:S(2)}, u32[]{:S(2)}) %collective-permute-start.4) | collective-permute-done | bytes 524320 | tf_op jit(solution)/shard_map/ppermute | solution.py:15
  88.8 0.0 collective-permute-start.9
  88.8 0.4 fusion.28
  89.2 0.0 collective-permute-done
  89.2 0.4 fusion.34
  89.7 28.5 %collective-permute-done.7 = bf16[2,4,128,256]{3,2,0,1:T(8,128)(2,1)S(1)} collective-permute-done((bf16[2,4,128,256]{3,2,0,1:T(8,128)(2,1)S(1)}, bf16[2,4,128,256]{3,2,0,1:T(8,128)(2,1)S(1)}, u32[]{:S(2)}, u32[]{:S(2)}) %collective-permute-start.7) | collective-permute-done | bytes 524320 | tf_op jit(solution)/shard_map/ppermute | solution.py:15
  118.2 0.4 fusion.27
  118.7 0.1 collective-permute-start.5
  118.8 2.0 %collective-permute-start.1 = (bf16[2,4,128,256]{3,2,0,1:T(8,128)(2,1)S(1)}, bf16[2,4,128,256]{3,2,0,1:T(8,128)(2,1)S(1)}, u32[]{:S(2)}, u32[]{:S(2)}) collective-permute-start(bf16[2,4,128,256]{3,2,0,1:T(8,128)(2,1)S(1)} %collective-permute-done), channel_id=1, source_target_pairs={{0,1},{1,2},{2,3},{3,4},{4,5},{5,6},{6,7},{7,8},{8,9},{9,10},{10,1... | collective-permute-start | bytes 1572872 | tf_op jit(solution)/shard_map/ppermute | solution.py:15
  120.8 0.0 collective-permute-done.15
  120.8 1.5 fusion.18
  122.3 0.0 collective-permute-done.12
  122.3 3.8 %collective-permute-start.13 = (bf16[2,4,128,256]{3,2,0,1:T(8,128)(2,1)S(1)}, bf16[2,4,128,256]{3,2,0,1:T(8,128)(2,1)S(1)}, u32[]{:S(2)}, u32[]{:S(2)}) collective-permute-start(bf16[2,4,128,256]{3,2,0,1:T(8,128)(2,1)S(1)} %collective-permute-done.12), channel_id=1, source_target_pairs={{0,15},{1,0},{2,1},{3,2},{4,3},{5,4},{6,5},{7,6},{8,7},{9,8},{10,9... | collective-permute-start | bytes 1572872 | tf_op jit(solution)/shard_map/ppermute | solution.py:15
  126.1 0.4 fusion.20
  126.5 0.4 fusion.24
  127.0 0.1 collective-permute-start.10
  127.1 10.2 %collective-permute-done.1 = bf16[2,4,128,256]{3,2,0,1:T(8,128)(2,1)S(1)} collective-permute-done((bf16[2,4,128,256]{3,2,0,1:T(8,128)(2,1)S(1)}, bf16[2,4,128,256]{3,2,0,1:T(8,128)(2,1)S(1)}, u32[]{:S(2)}, u32[]{:S(2)}) %collective-permute-start.1) | collective-permute-done | bytes 524320 | tf_op jit(solution)/shard_map/ppermute | solution.py:15
  137.3 0.4 fusion.33
  137.7 0.3 collective-permute-start.2
  138.1 5.7 %collective-permute-start.6 = (bf16[2,4,128,256]{3,2,0,1:T(8,128)(2,1)S(1)}, bf16[2,4,128,256]{3,2,0,1:T(8,128)(2,1)S(1)}, u32[]{:S(2)}, u32[]{:S(2)}) collective-permute-start(bf16[2,4,128,256]{3,2,0,1:T(8,128)(2,1)S(1)} %collective-permute-done.5), channel_id=1, source_target_pairs={{0,15},{1,0},{2,1},{3,2},{4,3},{5,4},{6,5},{7,6},{8,7},{9,8},{10,9... | collective-permute-start | bytes 1572872 | tf_op jit(solution)/shard_map/ppermute | solution.py:15
  143.8 0.4 fusion.29
  144.3 0.5 collective-permute-done.13
  144.8 2.7 %collective-permute-start.14 = (bf16[2,4,128,256]{3,2,0,1:T(8,128)(2,1)S(1)}, bf16[2,4,128,256]{3,2,0,1:T(8,128)(2,1)S(1)}, u32[]{:S(2)}, u32[]{:S(2)}) collective-permute-start(bf16[2,4,128,256]{3,2,0,1:T(8,128)(2,1)S(1)} %collective-permute-done.13), channel_id=1, source_target_pairs={{0,15},{1,0},{2,1},{3,2},{4,3},{5,4},{6,5},{7,6},{8,7},{9,8},{10,9... | collective-permute-start | bytes 1572872 | tf_op jit(solution)/shard_map/ppermute | solution.py:15
  147.6 1.0 collective-permute-done.10
  148.5 0.4 fusion.23
  149.0 9.6 %collective-permute-done.2 = bf16[2,4,128,256]{3,2,0,1:T(8,128)(2,1)S(1)} collective-permute-done((bf16[2,4,128,256]{3,2,0,1:T(8,128)(2,1)S(1)}, bf16[2,4,128,256]{3,2,0,1:T(8,128)(2,1)S(1)}, u32[]{:S(2)}, u32[]{:S(2)}) %collective-permute-start.2) | collective-permute-done | bytes 524320 | tf_op jit(solution)/shard_map/ppermute | solution.py:15
  158.6 0.4 fusion.32
  159.1 0.1 collective-permute-start.3
  159.2 0.4 fusion.21
  159.7 0.4 fusion.30
  160.1 6.0 %collective-permute-done.14 = bf16[2,4,128,256]{3,2,0,1:T(8,128)(2,1)S(1)} collective-permute-done((bf16[2,4,128,256]{3,2,0,1:T(8,128)(2,1)S(1)}, bf16[2,4,128,256]{3,2,0,1:T(8,128)(2,1)S(1)}, u32[]{:S(2)}, u32[]{:S(2)}) %collective-permute-start.14) | collective-permute-done | bytes 524320 | tf_op jit(solution)/shard_map/ppermute | solution.py:15
  166.1 0.4 fusion.22
  166.8 8.8 %collective-permute-done.3 = bf16[2,4,128,256]{3,2,0,1:T(8,128)(2,1)S(1)} collective-permute-done((bf16[2,4,128,256]{3,2,0,1:T(8,128)(2,1)S(1)}, bf16[2,4,128,256]{3,2,0,1:T(8,128)(2,1)S(1)}, u32[]{:S(2)}, u32[]{:S(2)}) %collective-permute-start.3) | collective-permute-done | bytes 524320 | tf_op jit(solution)/shard_map/ppermute | solution.py:15
  175.6 0.4 fusion.31
  176.3 2.6 %maximum_bitcast_fusion = bf16[8,1,9,2,128,128]{5,4,3,2,1,0:T(8,128)(2,1)} fusion(bf16[4,9,2,128,128]{4,3,2,1,0:T(8,128)(2,1)S(1)} %constant_dynamic-update-slice_fusion.9, bf16[4,9,2,128,128]{4,3,2,1,0:T(8,128)(2,1)S(1)} %constant_dynamic-update-slice_fusion), kind=kLoop, calls=%fused_computation | loop fusion | flops 2359296 | bytes 9437184 | tf_op jit(solution)/shard_map/broadcast_in_dim | solution.py:97
  (34 shorter events, 1.0 us)
Async XLA Ops:
  0.0 3.7 %copy-start = (bf16[1,8,69376]{2,1,0:T(8,128)(2,1)S(1)}, bf16[1,8,69376]{2,1,0:T(8,128)(2,1)}, u32[]{:S(2)}) copy-start(bf16[1,8,69376]{2,1,0:T(8,128)(2,1)} %param.2) | copy-start | bytes 3330052
  9.6 13.8 %all-to-all-start.1 = ((bf16[16,2,4,8,256]{4,3,2,1,0:T(8,128)(2,1)}), bf16[16,2,4,8,256]{4,3,2,1,0:T(8,128)(2,1)S(1)}, u32[]{:S(2)}, u32[]{:S(2)}) async-start(bf16[16,2,4,8,256]{4,3,2,1,0:T(8,128)(2,1)} %bitcast.48), calls=%async_computation.1 | async-start | bytes 1048576 | tf_op jit(solution)/shard_map/all_to_all | solution.py:78
  23.4 36.8 %all-to-all-start = ((bf16[16,2,4,8,256]{4,3,2,1,0:T(8,128)(2,1)}), bf16[16,2,4,8,256]{4,3,2,1,0:T(8,128)(2,1)S(1)}, u32[]{:S(2)}, u32[]{:S(2)}) async-start(bf16[16,2,4,8,256]{4,3,2,1,0:T(8,128)(2,1)} %bitcast.2), calls=%async_computation | async-start | bytes 1048576 | tf_op jit(solution)/shard_map/all_to_all | solution.py:78
  29.8 36.3 %collective-permute-start.11 = (bf16[2,4,128,256]{3,2,0,1:T(8,128)(2,1)S(1)}, bf16[2,4,128,256]{3,2,0,1:T(8,128)(2,1)}, u32[]{:S(2)}, u32[]{:S(2)}) collective-permute-start(bf16[2,4,128,256]{3,2,0,1:T(8,128)(2,1)S(1)} %copy_bitcast_fusion), channel_id=1, source_target_pairs={{0,7},{1,8},{2,9},{3,10},{4,11},{5,12},{6,13},{7,14},{8,15},{9,0},... | collective-permute-start | bytes 1572872 | tf_op jit(solution)/shard_map/ppermute | solution.py:15
  35.9 32.4 %collective-permute-start.8 = (bf16[2,4,128,256]{3,2,0,1:T(8,128)(2,1)S(1)}, bf16[2,4,128,256]{3,2,0,1:T(8,128)(2,1)S(1)}, u32[]{:S(2)}, u32[]{:S(2)}) collective-permute-start(bf16[2,4,128,256]{3,2,0,1:T(8,128)(2,1)S(1)} %copy_bitcast_fusion), channel_id=1, source_target_pairs={{0,1},{1,2},{2,3},{3,4},{4,5},{5,6},{6,7},{7,8},{8,9},{9,10},{10,1... | collective-permute-start | bytes 1572872 | tf_op jit(solution)/shard_map/ppermute | solution.py:15
  35.9 84.9 %collective-permute-start.15 = (bf16[2,4,128,256]{3,2,0,1:T(8,128)(2,1)S(1)}, bf16[2,4,128,256]{3,2,0,1:T(8,128)(2,1)}, u32[]{:S(2)}, u32[]{:S(2)}) collective-permute-start(bf16[2,4,128,256]{3,2,0,1:T(8,128)(2,1)S(1)} %copy_bitcast_fusion), channel_id=1, source_target_pairs={{0,8},{1,9},{2,10},{3,11},{4,12},{5,13},{6,14},{7,15},{8,0},{9,1},... | collective-permute-start | bytes 1572872 | tf_op jit(solution)/shard_map/ppermute | solution.py:15
  60.3 28.5 %collective-permute-start.4 = (bf16[2,4,128,256]{3,2,0,1:T(8,128)(2,1)S(1)}, bf16[2,4,128,256]{3,2,0,1:T(8,128)(2,1)S(1)}, u32[]{:S(2)}, u32[]{:S(2)}) collective-permute-start(bf16[2,4,128,256]{3,2,0,1:T(8,128)(2,1)S(1)} %copy_bitcast_fusion.1), channel_id=1, source_target_pairs={{0,7},{1,8},{2,9},{3,10},{4,11},{5,12},{6,13},{7,14},{8,15},{9,0},... | collective-permute-start | bytes 1572872 | tf_op jit(solution)/shard_map/ppermute | solution.py:15
  60.4 28.8 %collective-permute-start = (bf16[2,4,128,256]{3,2,0,1:T(8,128)(2,1)S(1)}, bf16[2,4,128,256]{3,2,0,1:T(8,128)(2,1)S(1)}, u32[]{:S(2)}, u32[]{:S(2)}) collective-permute-start(bf16[2,4,128,256]{3,2,0,1:T(8,128)(2,1)S(1)} %copy_bitcast_fusion.1), channel_id=1, source_target_pairs={{0,1},{1,2},{2,3},{3,4},{4,5},{5,6},{6,7},{7,8},{8,9},{9,10},{10,1... | collective-permute-start | bytes 1572872 | tf_op jit(solution)/shard_map/ppermute | solution.py:15
  66.1 52.0 %collective-permute-start.7 = (bf16[2,4,128,256]{3,2,0,1:T(8,128)(2,1)S(1)}, bf16[2,4,128,256]{3,2,0,1:T(8,128)(2,1)S(1)}, u32[]{:S(2)}, u32[]{:S(2)}) collective-permute-start(bf16[2,4,128,256]{3,2,0,1:T(8,128)(2,1)S(1)} %copy_bitcast_fusion.1), channel_id=1, source_target_pairs={{0,8},{1,9},{2,10},{3,11},{4,12},{5,13},{6,14},{7,15},{8,0},{9,1},... | collective-permute-start | bytes 1572872 | tf_op jit(solution)/shard_map/ppermute | solution.py:15
  68.3 53.9 %collective-permute-start.12 = (bf16[2,4,128,256]{3,2,0,1:T(8,128)(2,1)}, bf16[2,4,128,256]{3,2,0,1:T(8,128)(2,1)S(1)}, u32[]{:S(2)}, u32[]{:S(2)}) collective-permute-start(bf16[2,4,128,256]{3,2,0,1:T(8,128)(2,1)} %collective-permute-done.11), channel_id=1, source_target_pairs={{0,15},{1,0},{2,1},{3,2},{4,3},{5,4},{6,5},{7,6},{8,7},{9,8},{10,9... | collective-permute-start | bytes 1572872 | tf_op jit(solution)/shard_map/ppermute | solution.py:15
  88.8 37.7 %collective-permute-start.9 = (bf16[2,4,128,256]{3,2,0,1:T(8,128)(2,1)S(1)}, bf16[2,4,128,256]{3,2,0,1:T(8,128)(2,1)S(1)}, u32[]{:S(2)}, u32[]{:S(2)}) collective-permute-start(bf16[2,4,128,256]{3,2,0,1:T(8,128)(2,1)S(1)} %collective-permute-done.8), channel_id=1, source_target_pairs={{0,1},{1,2},{2,3},{3,4},{4,5},{5,6},{6,7},{7,8},{8,9},{9,10},{10,1... | collective-permute-start | bytes 1572872 | tf_op jit(solution)/shard_map/ppermute | solution.py:15
  118.7 19.4 %collective-permute-start.5 = (bf16[2,4,128,256]{3,2,0,1:T(8,128)(2,1)S(1)}, bf16[2,4,128,256]{3,2,0,1:T(8,128)(2,1)S(1)}, u32[]{:S(2)}, u32[]{:S(2)}) collective-permute-start(bf16[2,4,128,256]{3,2,0,1:T(8,128)(2,1)S(1)} %collective-permute-done.4), channel_id=1, source_target_pairs={{0,15},{1,0},{2,1},{3,2},{4,3},{5,4},{6,5},{7,6},{8,7},{9,8},{10,9... | collective-permute-start | bytes 1572872 | tf_op jit(solution)/shard_map/ppermute | solution.py:15
  118.8 18.5 %collective-permute-start.1 = (bf16[2,4,128,256]{3,2,0,1:T(8,128)(2,1)S(1)}, bf16[2,4,128,256]{3,2,0,1:T(8,128)(2,1)S(1)}, u32[]{:S(2)}, u32[]{:S(2)}) collective-permute-start(bf16[2,4,128,256]{3,2,0,1:T(8,128)(2,1)S(1)} %collective-permute-done), channel_id=1, source_target_pairs={{0,1},{1,2},{2,3},{3,4},{4,5},{5,6},{6,7},{7,8},{8,9},{9,10},{10,1... | collective-permute-start | bytes 1572872 | tf_op jit(solution)/shard_map/ppermute | solution.py:15
  122.3 22.5 %collective-permute-start.13 = (bf16[2,4,128,256]{3,2,0,1:T(8,128)(2,1)S(1)}, bf16[2,4,128,256]{3,2,0,1:T(8,128)(2,1)S(1)}, u32[]{:S(2)}, u32[]{:S(2)}) collective-permute-start(bf16[2,4,128,256]{3,2,0,1:T(8,128)(2,1)S(1)} %collective-permute-done.12), channel_id=1, source_target_pairs={{0,15},{1,0},{2,1},{3,2},{4,3},{5,4},{6,5},{7,6},{8,7},{9,8},{10,9... | collective-permute-start | bytes 1572872 | tf_op jit(solution)/shard_map/ppermute | solution.py:15
  127.0 21.5 %collective-permute-start.10 = (bf16[2,4,128,256]{3,2,0,1:T(8,128)(2,1)S(1)}, bf16[2,4,128,256]{3,2,0,1:T(8,128)(2,1)S(1)}, u32[]{:S(2)}, u32[]{:S(2)}) collective-permute-start(bf16[2,4,128,256]{3,2,0,1:T(8,128)(2,1)S(1)} %collective-permute-done.9), channel_id=1, source_target_pairs={{0,1},{1,2},{2,3},{3,4},{4,5},{5,6},{6,7},{7,8},{8,9},{9,10},{10,1... | collective-permute-start | bytes 1572872 | tf_op jit(solution)/shard_map/ppermute | solution.py:15
  137.7 20.9 %collective-permute-start.2 = (bf16[2,4,128,256]{3,2,0,1:T(8,128)(2,1)S(1)}, bf16[2,4,128,256]{3,2,0,1:T(8,128)(2,1)S(1)}, u32[]{:S(2)}, u32[]{:S(2)}) collective-permute-start(bf16[2,4,128,256]{3,2,0,1:T(8,128)(2,1)S(1)} %collective-permute-done.1), channel_id=1, source_target_pairs={{0,1},{1,2},{2,3},{3,4},{4,5},{5,6},{6,7},{7,8},{8,9},{9,10},{10,1... | collective-permute-start | bytes 1572872 | tf_op jit(solution)/shard_map/ppermute | solution.py:15
  138.1 21.5 %collective-permute-start.6 = (bf16[2,4,128,256]{3,2,0,1:T(8,128)(2,1)S(1)}, bf16[2,4,128,256]{3,2,0,1:T(8,128)(2,1)S(1)}, u32[]{:S(2)}, u32[]{:S(2)}) collective-permute-start(bf16[2,4,128,256]{3,2,0,1:T(8,128)(2,1)S(1)} %collective-permute-done.5), channel_id=1, source_target_pairs={{0,15},{1,0},{2,1},{3,2},{4,3},{5,4},{6,5},{7,6},{8,7},{9,8},{10,9... | collective-permute-start | bytes 1572872 | tf_op jit(solution)/shard_map/ppermute | solution.py:15
  144.8 21.3 %collective-permute-start.14 = (bf16[2,4,128,256]{3,2,0,1:T(8,128)(2,1)S(1)}, bf16[2,4,128,256]{3,2,0,1:T(8,128)(2,1)S(1)}, u32[]{:S(2)}, u32[]{:S(2)}) collective-permute-start(bf16[2,4,128,256]{3,2,0,1:T(8,128)(2,1)S(1)} %collective-permute-done.13), channel_id=1, source_target_pairs={{0,15},{1,0},{2,1},{3,2},{4,3},{5,4},{6,5},{7,6},{8,7},{9,8},{10,9... | collective-permute-start | bytes 1572872 | tf_op jit(solution)/shard_map/ppermute | solution.py:15
  159.1 16.5 %collective-permute-start.3 = (bf16[2,4,128,256]{3,2,0,1:T(8,128)(2,1)S(1)}, bf16[2,4,128,256]{3,2,0,1:T(8,128)(2,1)S(1)}, u32[]{:S(2)}, u32[]{:S(2)}) collective-permute-start(bf16[2,4,128,256]{3,2,0,1:T(8,128)(2,1)S(1)} %collective-permute-done.2), channel_id=1, source_target_pairs={{0,1},{1,2},{2,3},{3,4},{4,5},{5,6},{6,7},{7,8},{8,9},{9,10},{10,1... | collective-permute-start | bytes 1572872 | tf_op jit(solution)/shard_map/ppermute | solution.py:15

commit v2 on v1

v2 whole, which is shorter than its diff:
```python
import jax
import jax.numpy as jnp
from jax import lax
from jax.sharding import PartitionSpec as P

POINTS = 256
TAPS = 16
CHANNELS = 128
SPECTRA = 256


def along_ring(value, steps, other=0):
    half = lax.axis_size("blk") // 2
    pairs = []
    for b in range(2 * half):
        column, plane = b // half, b % half
        pairs.append((b, (column + other) % 2 * half + (plane + steps) % half))
    return lax.ppermute(value, "blk", pairs)


def to_twin(value):
    return along_ring(value, 0, 1)


def filter_table(chan_list, freq_size):
    window_len = TAPS * POINTS
    position = jnp.arange(window_len, dtype=jnp.float32)
    offset_pos = (position - window_len / 2 + 0.5) / POINTS
    taper = 0.5 - 0.5 * jnp.cos(2.0 * jnp.pi * (position + 0.5) / window_len)
    window = jnp.sin(jnp.pi * offset_pos) / (jnp.pi * offset_pos) * taper
    window = window / jnp.sqrt(jnp.sum(window * window))
    window = window.reshape(TAPS, 1, POINTS)
    columns = jnp.arange(POINTS, dtype=jnp.int32)
    angles = (chan_list[:, None] * columns[None, :] % POINTS).astype(jnp.float32) * (
        2.0 * jnp.pi / POINTS
    )
    waves = jnp.stack([jnp.cos(angles), -jnp.sin(angles)], axis=0)
    waves = waves.reshape(2, freq_size, 2, -1, POINTS).transpose(2, 1, 0, 3, 4)
    return (window * waves.reshape(1, -1, POINTS)).astype(jnp.bfloat16)


def channelize(frames, filters):
    return lax.conv_general_dilated(
        frames,
        filters,
        window_strides=(1,),
        padding="VALID",
        dimension_numbers=("NWC", "WOI", "CNW"),
        preferred_element_type=jnp.float32,
    ).astype(jnp.bfloat16)


def cross_block(stacked, moving):
    product = lax.dot_general(
        stacked, moving, (((0, 3), (0, 3)), ((1,), (1,))), preferred_element_type=jnp.float32
    )
    chan_count, _, tile = product.shape
    return (product * (1.0 / SPECTRA)).astype(jnp.bfloat16).reshape(chan_count, 2, tile, tile)


def stack_parts(own):
    return jnp.stack(
        [
            jnp.concatenate([own[0], own[1]], axis=1),
            jnp.concatenate([own[1], -own[0]], axis=1),
        ]
    )


def body(samples, chan_list):
    freq_size = lax.axis_size("freq")
    half = lax.axis_size("blk") // 2
    column, plane = lax.axis_index("blk") // half, lax.axis_index("blk") % half
    inputs = samples.shape[1]
    tile = freq_size * inputs
    frames = samples.reshape(inputs, samples.shape[2] // POINTS, POINTS)
    chans = CHANNELS // freq_size // 2
    voltages = channelize(frames, filter_table(chan_list, freq_size))
    voltages = voltages.reshape(2, freq_size, 2, 1, chans, inputs, SPECTRA)

    kept = lax.dynamic_index_in_dim(voltages, column, 0, keepdims=False)
    given = lax.dynamic_index_in_dim(voltages, 1 - column, 0, keepdims=False)
    pair = jnp.concatenate([kept, to_twin(given)], axis=2)
    pair = lax.all_to_all(pair, "freq", split_axis=0, concat_axis=4, tiled=True)
    lower, upper = slice(0, chans // 2), slice(chans // 2, chans)

    blocks = {0: pair.reshape(2, 2, chans, tile, SPECTRA)}
    tiles = {}

    def cross(owner, partner, where):
        own, moving = blocks[owner][:, :, where], blocks[partner][:, :, where]
        swap = (plane + partner) % half > (plane + owner) % half
        return [
            cross_block(
                stack_parts(own[:, block]),
                jnp.where(swap, moving[:, 1 - block], moving[:, block]),
            )
            for block in range(2)
        ]

    def near_tiles(partners):
        made = [cross(0, partner, where) for partner, where in partners]
        moved = to_twin(jnp.stack([both[1] for both in made]))
        for index, (partner, where) in enumerate(partners):
            tiles[-partner % half, where.start] = (made[index][0], moved[index])

    def far_tiles(owner, partner, where):
        both = cross(owner, partner, where)
        tiles[(owner - partner) % half, where.start] = (
            along_ring(both[0], owner),
            along_ring(both[1], owner, 1),
        )

    def step(partner, where=slice(None)):
        way = 1 if partner < 0 else -1
        blocks[partner] = along_ring(blocks[partner + way][:, :, where], way)

    def settle():
        nonlocal tiles, blocks
        tiles, blocks = lax.optimization_barrier((tiles, blocks))

    every = slice(0, chans)
    step(-1), step(1)
    own = blocks[0]
    made = [
        cross_block(stack_parts(own[:, i]), own[:, i ^ other]) for other in range(2) for i in range(2)
    ]
    moved = to_twin(jnp.stack([made[1], made[3]]))
    tiles[0, 0], tiles[half, 0] = (made[0], moved[0]), (made[2], moved[1])
    settle()
    step(-2), step(2)
    near_tiles([(-1, every), (1, every)])
    settle()
    step(-3, lower), step(3, upper)
    far_tiles(-1, 2, lower), far_tiles(1, -2, upper)
    near_tiles([(-2, every), (2, every)])
    settle()
    blocks[-3] = jnp.concatenate([blocks[-3], blocks[-3]], axis=2)
    blocks[3] = jnp.concatenate([blocks[3], blocks[3]], axis=2)
    far_tiles(1, -3, lower), far_tiles(-1, 3, upper)
    near_tiles([(-3, lower), (3, upper)])

    def whole(place):
        found = []
        for offset in range(half + 1):
            parts = [tiles[key][place] for key in sorted(tiles) if key[0] == offset]
            found.append(parts[0] if len(parts) == 1 else jnp.concatenate(parts, axis=0))
        return jnp.stack(found, axis=1)

    mine, theirs = whole(0), whole(1)
    low = jnp.where(column == 0, mine, theirs)
    high = jnp.where(column == 0, theirs, mine)
    return jnp.concatenate([low, high], axis=0)[:, None]


def solution(mesh):
    in_specs = (P("blk", "freq", None), P())
    out_specs = P("freq", "blk", None, None, None, None)
    return jax.shard_map(body, mesh=mesh, in_specs=in_specs, out_specs=out_specs, check_vma=False)
```

time: 179 us -> 158 us (0.88)
  waiting for transfers between devices: 104 us -> 55.9 us
  blocking collectives: 0 us -> 19.2 us
  other arithmetic: 4.95 us -> 10.7 us
  local copies, waits for them, and re-layouts: 4.49 us -> 8.39 us
    ppermute x16 -> x19, waiting for transfers between devices: 81 us -> 55.9 us  [along_ring(): return lax.ppermute(value, 'blk', pairs)]
    all_to_all x2 -> x0, waiting for transfers between devices: 23.5 us -> none  [body(): lax.all_to_all(sectioned, 'freq', split_axis=0, concat_axis=3, tiled=True)]
    all_to_all x0 -> x1, blocking collectives: none -> 19.2 us  [body(): pair = lax.all_to_all(pair, 'freq', split_axis=0, concat_axis=4, tiled=True)]
    all_to_all x2 -> x0, starting transfers between devices: 12.2 us -> none  [body(): lax.all_to_all(sectioned, 'freq', split_axis=0, concat_axis=3, tiled=True)]
    ppermute x16 -> x19, starting transfers between devices: 32.7 us -> 44.8 us  [along_ring(): return lax.ppermute(value, 'blk', pairs)]
    conv_general_dilated x2 -> x1, matrix products: 9.03 us -> 4.6 us  [channelize(): lax.conv_general_dilated(frames, filters, window_strides=(1,), padding='V...]
    squeeze x0 -> x13, local copies, waits for them, and re-layouts: none -> 3.46 us  [the longest x8 2.19 us: stack_parts(): own[0]]
    dot_general x18 -> x24, matrix products: 9.9 us -> 12.8 us  [cross_block(): lax.dot_general(stacked, moving, (((0, 3), (0, 3)), ((1,), (1,))), prefer...]
  transfers between devices with their start and end apart: 18 -> 19, of which waited for: 10 -> 10; matrix products, arithmetic and copies ran while one was open for 9% -> 9% of each run, Pallas kernels for 0% -> 0%
where the time goes in v2:
time: 158 us
  waiting for transfers between devices  55.9 us (35%)
  starting transfers between devices  44.8 us (28%)
  blocking collectives  19.2 us (12%)
  matrix products  17.4 us (11%)
  other arithmetic  10.7 us (7%)
  local copies, waits for them, and re-layouts  8.39 us (5%)
    ppermute x19, waiting for transfers between devices, along_ring(): return lax.ppermute(value, 'blk', pairs)  55.9 us
    ppermute x19, starting transfers between devices, along_ring(): return lax.ppermute(value, 'blk', pairs)  44.8 us
    all_to_all x1, blocking collectives, body(): pair = lax.all_to_all(pair, 'freq', split_axis=0, concat_axis=4, tiled=True)  19.2 us
    dot_general x24, matrix products, cross_block(): lax.dot_general(stacked, moving, (((0, 3), (0, 3)), ((1,), (1,))), prefer...  12.8 us
    conv_general_dilated x1, matrix products, channelize(): lax.conv_general_dilated(frames, filters, window_strides=(1,), padding='V...  4.6 us
  transfers between devices with their start and end apart: 19, of which 10 were waited for; matrix products, arithmetic and copies ran while one was open for 9% of the time, Pallas kernels for 0%

profile of v2, /device:TPU:6, one launch (start us, length us, event | category | flops | bytes accessed | tf_op | source)
XLA Modules:
  0.0 158.0 jit_solution(9174128341011356209)
XLA Ops:
  0.0 0.7 fusion.207
  0.7 0.8 mul.182
  1.5 1.2 fusion.197
  3.8 4.6 %fusion.3 = bf16[256,8,256]{0,1,2:T(8,128)(2,1)S(1)} fusion(bf16[8,271,256]{2,0,1:T(8,128)(2,1)S(1)} %bitcast.510, f32[256,256]{1,0:T(8,128)S(1)} %mul.188, f32[16,256]{1,0:T(8,128)S(1)} %fusion.199), kind=kOutput, calls=%fused_computation.7 | convolution fusion | flops 4297588736 | bytes 2437120 | tf_op jit(solution)/shard_map/conv_general_dilated | solution.py:43
  8.4 1.3 copy.100
  9.8 3.3 %collective-permute-start = (bf16[16,2,1,4,8,256]{5,4,3,1,0,2:T(8,128)(2,1)S(1)}, bf16[16,2,1,4,8,256]{5,4,3,1,0,2:T(8,128)(2,1)S(1)}, u32[]{:S(2)}, u32[]{:S(2)}) collective-permute-start(bf16[16,2,1,4,8,256]{5,4,3,1,0,2:T(8,128)(2,1)S(1)} %get-tuple-element.144), channel_id=1, source_target_pairs={{0,8},{1,9},{2,10},{3,11},{4,12},{5,13},{6,14},{7,15},{8,0},{9,1},... | collective-permute-start | bytes 1572872 | tf_op jit(solution)/shard_map/ppermute | solution.py:18
  13.0 12.0 %collective-permute-done = bf16[16,2,1,4,8,256]{5,4,3,1,0,2:T(8,128)(2,1)S(1)} collective-permute-done((bf16[16,2,1,4,8,256]{5,4,3,1,0,2:T(8,128)(2,1)S(1)}, bf16[16,2,1,4,8,256]{5,4,3,1,0,2:T(8,128)(2,1)S(1)}, u32[]{:S(2)}, u32[]{:S(2)}) %collective-permute-start) | collective-permute-done | bytes 524320 | tf_op jit(solution)/shard_map/ppermute | solution.py:18
  25.2 19.2 %all_to_all.15 = bf16[16,2,2,4,8,256]{5,4,3,1,2,0:T(8,128)(2,1)S(1)} all-to-all(bf16[16,2,2,4,8,256]{5,4,3,1,2,0:T(8,128)(2,1)S(1)} %copy.101), channel_id=1, replica_groups=mesh['freq'=16,'blk'=16] {'freq'}, dimensions={0} | all-to-all | bytes 2097152 | tf_op jit(solution)/shard_map/all_to_all | solution.py:84
  44.7 2.0 %collective-permute-start.2 = (bf16[2,2,4,128,256]{4,3,2,0,1:T(8,128)(2,1)S(1)}, bf16[2,2,4,128,256]{4,3,2,0,1:T(8,128)(2,1)S(1)}, u32[]{:S(2)}, u32[]{:S(2)}) collective-permute-start(bf16[2,2,4,128,256]{4,3,2,0,1:T(8,128)(2,1)S(1)} %copy_bitcast_fusion), channel_id=1, source_target_pairs={{0,1},{1,2},{2,3},{3,4},{4,5},{5,6},{6,7},{7,0},{8,9},{9,10},{10,1... | collective-permute-start | bytes 3145736 | tf_op jit(solution)/shard_map/ppermute | solution.py:18
  46.7 4.0 %collective-permute-start.3 = (bf16[2,2,4,128,256]{4,3,2,0,1:T(8,128)(2,1)S(1)}, bf16[2,2,4,128,256]{4,3,2,0,1:T(8,128)(2,1)}, u32[]{:S(2)}, u32[]{:S(2)}) collective-permute-start(bf16[2,2,4,128,256]{4,3,2,0,1:T(8,128)(2,1)S(1)} %copy_bitcast_fusion), channel_id=1, source_target_pairs={{0,7},{1,0},{2,1},{3,2},{4,3},{5,4},{6,5},{7,6},{8,15},{9,8},{10,9... | collective-permute-start | bytes 3145736 | tf_op jit(solution)/shard_map/ppermute | solution.py:18
  50.7 1.1 maximum_bitcast_fusion.1
  51.8 0.4 fusion.26
  52.3 0.4 fusion.25
  52.7 0.8 pad_maximum_fusion.19
  53.6 2.9 %collective-permute-start.1 = (bf16[2,4,2,128,128]{4,3,2,1,0:T(8,128)(2,1)}, bf16[2,4,2,128,128]{4,3,2,1,0:T(8,128)(2,1)}, u32[]{:S(2)}, u32[]{:S(2)}) collective-permute-start(bf16[2,4,2,128,128]{4,3,2,1,0:T(8,128)(2,1)} %pad_maximum_fusion.19), channel_id=1, source_target_pairs={{0,8},{1,9},{2,10},{3,11},{4,12},{5,13},{6,14},{7,15},{8,0},{9,1},... | collective-permute-start | bytes 1572872 | tf_op jit(solution)/shard_map/ppermute | solution.py:18
  56.5 1.7 %fusion.24 = bf16[4,256,128]{2,1,0:T(8,128)(2,1)S(1)} fusion(bf16[1,4,256,256]{3,2,1,0:T(8,128)(2,1)} %get-tuple-element.164, bf16[1,4,256,256]{3,2,1,0:T(8,128)(2,1)} %get-tuple-element.163, bf16[2,2,4,128,256]{4,3,2,0,1:T(8,128)(2,1)S(1)} %copy_bitcast_fusion), kind=kOutput, calls=%fused_computation.40 | convolution fusion | flops 135004160 | bytes 1835008 | tf_op jit(solution)/shard_map/dot_general | solution.py:54
  58.2 0.4 fusion.27
  58.7 10.9 %collective-permute-done.1 = bf16[2,4,2,128,128]{4,3,2,1,0:T(8,128)(2,1)} collective-permute-done((bf16[2,4,2,128,128]{4,3,2,1,0:T(8,128)(2,1)}, bf16[2,4,2,128,128]{4,3,2,1,0:T(8,128)(2,1)}, u32[]{:S(2)}, u32[]{:S(2)}) %collective-permute-start.1) | collective-permute-done | bytes 524320 | tf_op jit(solution)/shard_map/ppermute | solution.py:18
  69.6 1.1 slice_bitcast_fusion.14
  70.7 3.9 %collective-permute-done.2 = bf16[2,2,4,128,256]{4,3,2,0,1:T(8,128)(2,1)S(1)} collective-permute-done((bf16[2,2,4,128,256]{4,3,2,0,1:T(8,128)(2,1)S(1)}, bf16[2,2,4,128,256]{4,3,2,0,1:T(8,128)(2,1)S(1)}, u32[]{:S(2)}, u32[]{:S(2)}) %collective-permute-start.2) | collective-permute-done | bytes 1048608 | tf_op jit(solution)/shard_map/ppermute | solution.py:18
  75.0 3.2 %collective-permute-start.6 = (bf16[2,2,4,128,256]{4,3,2,0,1:T(8,128)(2,1)}, bf16[2,2,4,128,256]{4,3,2,0,1:T(8,128)(2,1)S(1)}, u32[]{:S(2)}, u32[]{:S(2)}) collective-permute-start(bf16[2,2,4,128,256]{4,3,2,0,1:T(8,128)(2,1)} %collective-permute-done.3), channel_id=1, source_target_pairs={{0,7},{1,0},{2,1},{3,2},{4,3},{5,4},{6,5},{7,6},{8,15},{9,8},{10,9... | collective-permute-start | bytes 3145736 | tf_op jit(solution)/shard_map/ppermute | solution.py:18
  78.3 0.4 fusion.22
  78.8 1.7 %fusion.21 = bf16[4,256,128]{2,1,0:T(8,128)(2,1)S(1)} fusion(bf16[1,4,256,256]{3,2,1,0:T(8,128)(2,1)S(1)} %get-tuple-element.158, bf16[1,4,256,256]{3,2,1,0:T(8,128)(2,1)S(1)} %get-tuple-element.157, pred[]{:T(512)S(6)} %gt.31, bf16[2,2,4,128,256]{4,3,2,0,1:T(8,128)(2,1)} %collective-permute-done.3), kind=kOutput, calls=%fused_computation.37 | convolution fusion | flops 135266304 | bytes 2359297 | tf_op jit(solution)/shard_map/dot_general | solution.py:54
  80.5 3.0 %collective-permute-start.4 = (bf16[2,4,2,128,128]{4,3,2,1,0:T(8,128)(2,1)S(1)}, bf16[2,4,2,128,128]{4,3,2,1,0:T(8,128)(2,1)S(1)}, u32[]{:S(2)}, u32[]{:S(2)}) collective-permute-start(bf16[2,4,2,128,128]{4,3,2,1,0:T(8,128)(2,1)S(1)} %pad_maximum_fusion.20), channel_id=1, source_target_pairs={{0,8},{1,9},{2,10},{3,11},{4,12},{5,13},{6,14},{7,15},{8,0},{9,1},... | collective-permute-start | bytes 1572872 | tf_op jit(solution)/shard_map/ppermute | solution.py:18
  83.6 1.7 %fusion.20 = bf16[4,256,128]{2,1,0:T(8,128)(2,1)S(1)} fusion(bf16[1,4,256,256]{3,2,1,0:T(8,128)(2,1)S(1)} %get-tuple-element.160, bf16[1,4,256,256]{3,2,1,0:T(8,128)(2,1)S(1)} %get-tuple-element.159, pred[]{:T(512)S(6)} %gt.31, bf16[2,2,4,128,256]{4,3,2,0,1:T(8,128)(2,1)} %collective-permute-done.3), kind=kOutput, calls=%fused_computation.36 | convolution fusion | flops 135266304 | bytes 2359297 | tf_op jit(solution)/shard_map/dot_general | solution.py:54
  85.3 0.4 fusion.23
  85.8 9.7 %collective-permute-done.4 = bf16[2,4,2,128,128]{4,3,2,1,0:T(8,128)(2,1)S(1)} collective-permute-done((bf16[2,4,2,128,128]{4,3,2,1,0:T(8,128)(2,1)S(1)}, bf16[2,4,2,128,128]{4,3,2,1,0:T(8,128)(2,1)S(1)}, u32[]{:S(2)}, u32[]{:S(2)}) %collective-permute-start.4) | collective-permute-done | bytes 524320 | tf_op jit(solution)/shard_map/ppermute | solution.py:18
  95.5 5.8 %collective-permute-done.5 = bf16[2,2,4,128,256]{4,3,2,0,1:T(8,128)(2,1)S(1)} collective-permute-done((bf16[2,2,4,128,256]{4,3,2,0,1:T(8,128)(2,1)S(1)}, bf16[2,2,4,128,256]{4,3,2,0,1:T(8,128)(2,1)S(1)}, u32[]{:S(2)}, u32[]{:S(2)}) %collective-permute-start.5) | collective-permute-done | bytes 1048608 | tf_op jit(solution)/shard_map/ppermute | solution.py:18
  101.7 1.0 slice_bitcast_fusion.36
  102.7 1.0 slice_bitcast_fusion.48
  103.6 1.0 fusion.233
  104.9 0.5 fusion.16
  105.3 0.5 fusion.17
  105.8 0.5 fusion.18
  106.2 0.5 fusion.19
  106.8 0.3 fusion.43
  107.2 5.6 %collective-permute-start.11 = (bf16[2,2,128,128]{3,2,1,0:T(8,128)(2,1)S(1)}, bf16[2,2,128,128]{3,2,1,0:T(8,128)(2,1)S(1)}, u32[]{:S(2)}, u32[]{:S(2)}) collective-permute-start(bf16[2,2,128,128]{3,2,1,0:T(8,128)(2,1)S(1)} %bitcast.532), channel_id=1, source_target_pairs={{0,15},{1,8},{2,9},{3,10},{4,11},{5,12},{6,13},{7,14},{8,7},{9,0},... | collective-permute-start | bytes 393224 | tf_op jit(solution)/shard_map/ppermute | solution.py:18
  112.8 0.3 fusion.42
  113.1 0.5 collective-permute-start.10
  113.7 0.7 collective-permute-start.7
  114.4 1.6 %collective-permute-start.12 = (bf16[2,2,2,128,256]{4,3,2,0,1:T(8,128)(2,1)S(1)}, bf16[2,2,2,128,256]{4,3,2,0,1:T(8,128)(2,1)S(1)}, u32[]{:S(2)}, u32[]{:S(2)}) collective-permute-start(bf16[2,2,2,128,256]{4,3,2,0,1:T(8,128)(2,1)S(1)} %slice.438), channel_id=1, source_target_pairs={{0,1},{1,2},{2,3},{3,4},{4,5},{5,6},{6,7},{7,0},{8,9},{9,10},{10,1... | collective-permute-start | bytes 1572872 | tf_op jit(solution)/shard_map/ppermute | solution.py:18
  116.0 1.7 %collective-permute-start.13 = (bf16[2,2,2,128,256]{4,3,2,0,1:T(8,128)(2,1)S(1)}, bf16[2,2,2,128,256]{4,3,2,0,1:T(8,128)(2,1)S(1)}, u32[]{:S(2)}, u32[]{:S(2)}) collective-permute-start(bf16[2,2,2,128,256]{4,3,2,0,1:T(8,128)(2,1)S(1)} %slice.439), channel_id=1, source_target_pairs={{0,7},{1,0},{2,1},{3,2},{4,3},{5,4},{6,5},{7,6},{8,15},{9,8},{10,9... | collective-permute-start | bytes 1572872 | tf_op jit(solution)/shard_map/ppermute | solution.py:18
  118.0 0.3 fusion.40
  118.3 2.8 %collective-permute-start.9 = (bf16[2,2,128,128]{3,2,1,0:T(8,128)(2,1)S(1)}, bf16[2,2,128,128]{3,2,1,0:T(8,128)(2,1)S(1)}, u32[]{:S(2)}, u32[]{:S(2)}) collective-permute-start(bf16[2,2,128,128]{3,2,1,0:T(8,128)(2,1)S(1)} %bitcast.534), channel_id=1, source_target_pairs={{0,9},{1,10},{2,11},{3,12},{4,13},{5,14},{6,15},{7,8},{8,1},{9,2},... | collective-permute-start | bytes 393224 | tf_op jit(solution)/shard_map/ppermute | solution.py:18
  121.1 6.9 %collective-permute-done.7 = bf16[2,4,2,128,128]{4,3,2,1,0:T(8,128)(2,1)S(1)} collective-permute-done((bf16[2,4,2,128,128]{4,3,2,1,0:T(8,128)(2,1)S(1)}, bf16[2,4,2,128,128]{4,3,2,1,0:T(8,128)(2,1)S(1)}, u32[]{:S(2)}, u32[]{:S(2)}) %collective-permute-start.7) | collective-permute-done | bytes 524320 | tf_op jit(solution)/shard_map/ppermute | solution.py:18
  128.0 2.4 %collective-permute-start.8 = (bf16[2,2,128,128]{3,2,1,0:T(8,128)(2,1)S(1)}, bf16[2,2,128,128]{3,2,1,0:T(8,128)(2,1)S(1)}, u32[]{:S(2)}, u32[]{:S(2)}) collective-permute-start(bf16[2,2,128,128]{3,2,1,0:T(8,128)(2,1)S(1)} %bitcast.535), channel_id=1, source_target_pairs={{0,1},{1,2},{2,3},{3,4},{4,5},{5,6},{6,7},{7,0},{8,9},{9,10},{10,1... | collective-permute-start | bytes 393224 | tf_op jit(solution)/shard_map/ppermute | solution.py:18
  130.5 3.3 %collective-permute-done.9 = bf16[2,2,128,128]{3,2,1,0:T(8,128)(2,1)S(1)} collective-permute-done((bf16[2,2,128,128]{3,2,1,0:T(8,128)(2,1)S(1)}, bf16[2,2,128,128]{3,2,1,0:T(8,128)(2,1)S(1)}, u32[]{:S(2)}, u32[]{:S(2)}) %collective-permute-start.9) | collective-permute-done | bytes 131104 | tf_op jit(solution)/shard_map/ppermute | solution.py:18
  133.8 1.5 collective-permute-done.8
  135.3 1.0 slice_bitcast_fusion.32
  136.3 1.0 slice_bitcast_fusion.44
  137.3 1.0 fusion.237
  138.7 0.3 fusion.50
  139.0 2.6 %collective-permute-start.17 = (bf16[2,2,128,128]{3,2,1,0:T(8,128)(2,1)S(1)}, bf16[2,2,128,128]{3,2,1,0:T(8,128)(2,1)S(1)}, u32[]{:S(2)}, u32[]{:S(2)}) collective-permute-start(bf16[2,2,128,128]{3,2,1,0:T(8,128)(2,1)S(1)} %bitcast.528), channel_id=1, source_target_pairs={{0,9},{1,10},{2,11},{3,12},{4,13},{5,14},{6,15},{7,8},{8,1},{9,2},... | collective-permute-start | bytes 393224 | tf_op jit(solution)/shard_map/ppermute | solution.py:18
  141.6 0.3 fusion.51
  141.9 3.4 %collective-permute-start.18 = (bf16[2,2,128,128]{3,2,1,0:T(8,128)(2,1)S(1)}, bf16[2,2,128,128]{3,2,1,0:T(8,128)(2,1)S(1)}, u32[]{:S(2)}, u32[]{:S(2)}) collective-permute-start(bf16[2,2,128,128]{3,2,1,0:T(8,128)(2,1)S(1)} %bitcast.529), channel_id=1, source_target_pairs={{0,15},{1,8},{2,9},{3,10},{4,11},{5,12},{6,13},{7,14},{8,7},{9,0},... | collective-permute-start | bytes 393224 | tf_op jit(solution)/shard_map/ppermute | solution.py:18
  145.4 0.3 fusion.48
  145.8 0.3 fusion.49
  146.1 1.5 collective-permute-start.16
  148.0 0.3 collective-permute-start.14
  148.3 0.3 fusion.46
  148.7 3.1 %collective-permute-start.15 = (bf16[2,2,128,128]{3,2,1,0:T(8,128)(2,1)S(1)}, bf16[2,2,128,128]{3,2,1,0:T(8,128)(2,1)S(1)}, u32[]{:S(2)}, u32[]{:S(2)}) collective-permute-start(bf16[2,2,128,128]{3,2,1,0:T(8,128)(2,1)S(1)} %bitcast.533), channel_id=1, source_target_pairs={{0,7},{1,0},{2,1},{3,2},{4,3},{5,4},{6,5},{7,6},{8,15},{9,8},{10,9... | collective-permute-start | bytes 393224 | tf_op jit(solution)/shard_map/ppermute | solution.py:18
  152.3 0.3 fusion.44
  152.7 1.5 collective-permute-done.14
  155.4 2.6 %maximum_bitcast_fusion = bf16[8,1,9,2,128,128]{5,4,3,2,1,0:T(8,128)(2,1)} fusion(bf16[4,9,2,128,128]{4,3,2,1,0:T(8,128)(2,1)S(1)} %get-tuple-element.88, bf16[4,9,2,128,128]{4,3,2,1,0:T(8,128)(2,1)S(1)} %get-tuple-element.87), kind=kLoop, calls=%fused_computation | loop fusion | flops 2359296 | bytes 9437184 | tf_op jit(solution)/shard_map/broadcast_in_dim | solution.py:153
  (88 shorter events, 5.0 us)
Async XLA Ops:
  0.0 3.7 %copy-start = (bf16[1,8,69376]{2,1,0:T(8,128)(2,1)S(1)}, bf16[1,8,69376]{2,1,0:T(8,128)(2,1)}, u32[]{:S(2)}) copy-start(bf16[1,8,69376]{2,1,0:T(8,128)(2,1)} %param.2) | copy-start | bytes 3330052
  9.8 15.3 %collective-permute-start = (bf16[16,2,1,4,8,256]{5,4,3,1,0,2:T(8,128)(2,1)S(1)}, bf16[16,2,1,4,8,256]{5,4,3,1,0,2:T(8,128)(2,1)S(1)}, u32[]{:S(2)}, u32[]{:S(2)}) collective-permute-start(bf16[16,2,1,4,8,256]{5,4,3,1,0,2:T(8,128)(2,1)S(1)} %get-tuple-element.144), channel_id=1, source_target_pairs={{0,8},{1,9},{2,10},{3,11},{4,12},{5,13},{6,14},{7,15},{8,0},{9,1},... | collective-permute-start | bytes 1572872 | tf_op jit(solution)/shard_map/ppermute | solution.py:18
  44.7 29.9 %collective-permute-start.2 = (bf16[2,2,4,128,256]{4,3,2,0,1:T(8,128)(2,1)S(1)}, bf16[2,2,4,128,256]{4,3,2,0,1:T(8,128)(2,1)S(1)}, u32[]{:S(2)}, u32[]{:S(2)}) collective-permute-start(bf16[2,2,4,128,256]{4,3,2,0,1:T(8,128)(2,1)S(1)} %copy_bitcast_fusion), channel_id=1, source_target_pairs={{0,1},{1,2},{2,3},{3,4},{4,5},{5,6},{6,7},{7,0},{8,9},{9,10},{10,1... | collective-permute-start | bytes 3145736 | tf_op jit(solution)/shard_map/ppermute | solution.py:18
  46.7 27.9 %collective-permute-start.3 = (bf16[2,2,4,128,256]{4,3,2,0,1:T(8,128)(2,1)S(1)}, bf16[2,2,4,128,256]{4,3,2,0,1:T(8,128)(2,1)}, u32[]{:S(2)}, u32[]{:S(2)}) collective-permute-start(bf16[2,2,4,128,256]{4,3,2,0,1:T(8,128)(2,1)S(1)} %copy_bitcast_fusion), channel_id=1, source_target_pairs={{0,7},{1,0},{2,1},{3,2},{4,3},{5,4},{6,5},{7,6},{8,15},{9,8},{10,9... | collective-permute-start | bytes 3145736 | tf_op jit(solution)/shard_map/ppermute | solution.py:18
  53.6 16.0 %collective-permute-start.1 = (bf16[2,4,2,128,128]{4,3,2,1,0:T(8,128)(2,1)}, bf16[2,4,2,128,128]{4,3,2,1,0:T(8,128)(2,1)}, u32[]{:S(2)}, u32[]{:S(2)}) collective-permute-start(bf16[2,4,2,128,128]{4,3,2,1,0:T(8,128)(2,1)} %pad_maximum_fusion.19), channel_id=1, source_target_pairs={{0,8},{1,9},{2,10},{3,11},{4,12},{5,13},{6,14},{7,15},{8,0},{9,1},... | collective-permute-start | bytes 1572872 | tf_op jit(solution)/shard_map/ppermute | solution.py:18
  56.5 1.7 %copy-start.1 = (bf16[1,4,256,256]{3,2,1,0:T(8,128)(2,1)S(1)}, bf16[1,4,256,256]{3,2,1,0:T(8,128)(2,1)}, u32[]{:S(2)}) copy-start(bf16[1,4,256,256]{3,2,1,0:T(8,128)(2,1)} %get-tuple-element.163) | copy-start | bytes 1572868
  56.5 1.7 %copy-start.2 = (bf16[1,4,256,256]{3,2,1,0:T(8,128)(2,1)S(1)}, bf16[1,4,256,256]{3,2,1,0:T(8,128)(2,1)}, u32[]{:S(2)}) copy-start(bf16[1,4,256,256]{3,2,1,0:T(8,128)(2,1)} %get-tuple-element.164) | copy-start | bytes 1572868
  74.8 26.6 %collective-permute-start.5 = (bf16[2,2,4,128,256]{4,3,2,0,1:T(8,128)(2,1)S(1)}, bf16[2,2,4,128,256]{4,3,2,0,1:T(8,128)(2,1)S(1)}, u32[]{:S(2)}, u32[]{:S(2)}) collective-permute-start(bf16[2,2,4,128,256]{4,3,2,0,1:T(8,128)(2,1)S(1)} %collective-permute-done.2), channel_id=1, source_target_pairs={{0,1},{1,2},{2,3},{3,4},{4,5},{5,6},{6,7},{7,0},{8,9},{9,10},{10,1... | collective-permute-start | bytes 3145736 | tf_op jit(solution)/shard_map/ppermute | solution.py:18
  75.0 26.3 %collective-permute-start.6 = (bf16[2,2,4,128,256]{4,3,2,0,1:T(8,128)(2,1)}, bf16[2,2,4,128,256]{4,3,2,0,1:T(8,128)(2,1)S(1)}, u32[]{:S(2)}, u32[]{:S(2)}) collective-permute-start(bf16[2,2,4,128,256]{4,3,2,0,1:T(8,128)(2,1)} %collective-permute-done.3), channel_id=1, source_target_pairs={{0,7},{1,0},{2,1},{3,2},{4,3},{5,4},{6,5},{7,6},{8,15},{9,8},{10,9... | collective-permute-start | bytes 3145736 | tf_op jit(solution)/shard_map/ppermute | solution.py:18
  80.5 15.0 %collective-permute-start.4 = (bf16[2,4,2,128,128]{4,3,2,1,0:T(8,128)(2,1)S(1)}, bf16[2,4,2,128,128]{4,3,2,1,0:T(8,128)(2,1)S(1)}, u32[]{:S(2)}, u32[]{:S(2)}) collective-permute-start(bf16[2,4,2,128,128]{4,3,2,1,0:T(8,128)(2,1)S(1)} %pad_maximum_fusion.20), channel_id=1, source_target_pairs={{0,8},{1,9},{2,10},{3,11},{4,12},{5,13},{6,14},{7,15},{8,0},{9,1},... | collective-permute-start | bytes 1572872 | tf_op jit(solution)/shard_map/ppermute | solution.py:18
  107.2 11.2 %collective-permute-start.11 = (bf16[2,2,128,128]{3,2,1,0:T(8,128)(2,1)S(1)}, bf16[2,2,128,128]{3,2,1,0:T(8,128)(2,1)S(1)}, u32[]{:S(2)}, u32[]{:S(2)}) collective-permute-start(bf16[2,2,128,128]{3,2,1,0:T(8,128)(2,1)S(1)} %bitcast.532), channel_id=1, source_target_pairs={{0,15},{1,8},{2,9},{3,10},{4,11},{5,12},{6,13},{7,14},{8,7},{9,0},... | collective-permute-start | bytes 393224 | tf_op jit(solution)/shard_map/ppermute | solution.py:18
  113.1 17.4 %collective-permute-start.10 = (bf16[2,2,128,128]{3,2,1,0:T(8,128)(2,1)S(1)}, bf16[2,2,128,128]{3,2,1,0:T(8,128)(2,1)S(1)}, u32[]{:S(2)}, u32[]{:S(2)}) collective-permute-start(bf16[2,2,128,128]{3,2,1,0:T(8,128)(2,1)S(1)} %bitcast.531), channel_id=1, source_target_pairs={{0,7},{1,0},{2,1},{3,2},{4,3},{5,4},{6,5},{7,6},{8,15},{9,8},{10,9... | collective-permute-start | bytes 393224 | tf_op jit(solution)/shard_map/ppermute | solution.py:18
  113.7 14.3 %collective-permute-start.7 = (bf16[2,4,2,128,128]{4,3,2,1,0:T(8,128)(2,1)S(1)}, bf16[2,4,2,128,128]{4,3,2,1,0:T(8,128)(2,1)S(1)}, u32[]{:S(2)}, u32[]{:S(2)}) collective-permute-start(bf16[2,4,2,128,128]{4,3,2,1,0:T(8,128)(2,1)S(1)} %pad_maximum_fusion.21), channel_id=1, source_target_pairs={{0,8},{1,9},{2,10},{3,11},{4,12},{5,13},{6,14},{7,15},{8,0},{9,1},... | collective-permute-start | bytes 1572872 | tf_op jit(solution)/shard_map/ppermute | solution.py:18
  114.4 20.9 %collective-permute-start.12 = (bf16[2,2,2,128,256]{4,3,2,0,1:T(8,128)(2,1)S(1)}, bf16[2,2,2,128,256]{4,3,2,0,1:T(8,128)(2,1)S(1)}, u32[]{:S(2)}, u32[]{:S(2)}) collective-permute-start(bf16[2,2,2,128,256]{4,3,2,0,1:T(8,128)(2,1)S(1)} %slice.438), channel_id=1, source_target_pairs={{0,1},{1,2},{2,3},{3,4},{4,5},{5,6},{6,7},{7,0},{8,9},{9,10},{10,1... | collective-permute-start | bytes 1572872 | tf_op jit(solution)/shard_map/ppermute | solution.py:18
  116.0 19.4 %collective-permute-start.13 = (bf16[2,2,2,128,256]{4,3,2,0,1:T(8,128)(2,1)S(1)}, bf16[2,2,2,128,256]{4,3,2,0,1:T(8,128)(2,1)S(1)}, u32[]{:S(2)}, u32[]{:S(2)}) collective-permute-start(bf16[2,2,2,128,256]{4,3,2,0,1:T(8,128)(2,1)S(1)} %slice.439), channel_id=1, source_target_pairs={{0,7},{1,0},{2,1},{3,2},{4,3},{5,4},{6,5},{7,6},{8,15},{9,8},{10,9... | collective-permute-start | bytes 1572872 | tf_op jit(solution)/shard_map/ppermute | solution.py:18
  118.3 15.5 %collective-permute-start.9 = (bf16[2,2,128,128]{3,2,1,0:T(8,128)(2,1)S(1)}, bf16[2,2,128,128]{3,2,1,0:T(8,128)(2,1)S(1)}, u32[]{:S(2)}, u32[]{:S(2)}) collective-permute-start(bf16[2,2,128,128]{3,2,1,0:T(8,128)(2,1)S(1)} %bitcast.534), channel_id=1, source_target_pairs={{0,9},{1,10},{2,11},{3,12},{4,13},{5,14},{6,15},{7,8},{8,1},{9,2},... | collective-permute-start | bytes 393224 | tf_op jit(solution)/shard_map/ppermute | solution.py:18
  128.0 7.3 %collective-permute-start.8 = (bf16[2,2,128,128]{3,2,1,0:T(8,128)(2,1)S(1)}, bf16[2,2,128,128]{3,2,1,0:T(8,128)(2,1)S(1)}, u32[]{:S(2)}, u32[]{:S(2)}) collective-permute-start(bf16[2,2,128,128]{3,2,1,0:T(8,128)(2,1)S(1)} %bitcast.535), channel_id=1, source_target_pairs={{0,1},{1,2},{2,3},{3,4},{4,5},{5,6},{6,7},{7,0},{8,9},{9,10},{10,1... | collective-permute-start | bytes 393224 | tf_op jit(solution)/shard_map/ppermute | solution.py:18
  139.0 15.8 %collective-permute-start.17 = (bf16[2,2,128,128]{3,2,1,0:T(8,128)(2,1)S(1)}, bf16[2,2,128,128]{3,2,1,0:T(8,128)(2,1)S(1)}, u32[]{:S(2)}, u32[]{:S(2)}) collective-permute-start(bf16[2,2,128,128]{3,2,1,0:T(8,128)(2,1)S(1)} %bitcast.528), channel_id=1, source_target_pairs={{0,9},{1,10},{2,11},{3,12},{4,13},{5,14},{6,15},{7,8},{8,1},{9,2},... | collective-permute-start | bytes 393224 | tf_op jit(solution)/shard_map/ppermute | solution.py:18
  141.9 12.9 %collective-permute-start.18 = (bf16[2,2,128,128]{3,2,1,0:T(8,128)(2,1)S(1)}, bf16[2,2,128,128]{3,2,1,0:T(8,128)(2,1)S(1)}, u32[]{:S(2)}, u32[]{:S(2)}) collective-permute-start(bf16[2,2,128,128]{3,2,1,0:T(8,128)(2,1)S(1)} %bitcast.529), channel_id=1, source_target_pairs={{0,15},{1,8},{2,9},{3,10},{4,11},{5,12},{6,13},{7,14},{8,7},{9,0},... | collective-permute-start | bytes 393224 | tf_op jit(solution)/shard_map/ppermute | solution.py:18
  146.1 8.6 %collective-permute-start.16 = (bf16[2,2,2,128,128]{4,3,2,1,0:T(8,128)(2,1)S(1)}, bf16[2,2,2,128,128]{4,3,2,1,0:T(8,128)(2,1)S(1)}, u32[]{:S(2)}, u32[]{:S(2)}) collective-permute-start(bf16[2,2,2,128,128]{4,3,2,1,0:T(8,128)(2,1)S(1)} %pad_maximum_fusion.22), channel_id=1, source_target_pairs={{0,8},{1,9},{2,10},{3,11},{4,12},{5,13},{6,14},{7,15},{8,0},{9,1},... | collective-permute-start | bytes 786440 | tf_op jit(solution)/shard_map/ppermute | solution.py:18
  148.0 6.3 %collective-permute-start.14 = (bf16[2,2,128,128]{3,2,1,0:T(8,128)(2,1)S(1)}, bf16[2,2,128,128]{3,2,1,0:T(8,128)(2,1)S(1)}, u32[]{:S(2)}, u32[]{:S(2)}) collective-permute-start(bf16[2,2,128,128]{3,2,1,0:T(8,128)(2,1)S(1)} %bitcast.530), channel_id=1, source_target_pairs={{0,1},{1,2},{2,3},{3,4},{4,5},{5,6},{6,7},{7,0},{8,9},{9,10},{10,1... | collective-permute-start | bytes 393224 | tf_op jit(solution)/shard_map/ppermute | solution.py:18
  148.7 5.6 %collective-permute-start.15 = (bf16[2,2,128,128]{3,2,1,0:T(8,128)(2,1)S(1)}, bf16[2,2,128,128]{3,2,1,0:T(8,128)(2,1)S(1)}, u32[]{:S(2)}, u32[]{:S(2)}) collective-permute-start(bf16[2,2,128,128]{3,2,1,0:T(8,128)(2,1)S(1)} %bitcast.533), channel_id=1, source_target_pairs={{0,7},{1,0},{2,1},{3,2},{4,3},{5,4},{6,5},{7,6},{8,15},{9,8},{10,9... | collective-permute-start | bytes 393224 | tf_op jit(solution)/shard_map/ppermute | solution.py:18

commit v3 on v2

v3 whole, which is shorter than its diff:
```python
import jax
import jax.numpy as jnp
from jax import lax
from jax.experimental import pallas as pl
from jax.experimental.pallas import tpu as pltpu
from jax.sharding import PartitionSpec as P

POINTS = 256
TAPS = 16
CHANNELS = 128
SPECTRA = 256


def along_ring(value, steps, other=0):
    half = lax.axis_size("blk") // 2
    pairs = []
    for b in range(2 * half):
        column, plane = b // half, b % half
        pairs.append((b, (column + other) % 2 * half + (plane + steps) % half))
    return lax.ppermute(value, "blk", pairs)


def to_twin(value):
    return along_ring(value, 0, 1)


def filter_table(chan_list, freq_size):
    window_len = TAPS * POINTS
    position = jnp.arange(window_len, dtype=jnp.float32)
    offset_pos = (position - window_len / 2 + 0.5) / POINTS
    taper = 0.5 - 0.5 * jnp.cos(2.0 * jnp.pi * (position + 0.5) / window_len)
    window = jnp.sin(jnp.pi * offset_pos) / (jnp.pi * offset_pos) * taper
    window = window / jnp.sqrt(jnp.sum(window * window))
    window = window.reshape(TAPS, 1, POINTS)
    columns = jnp.arange(POINTS, dtype=jnp.int32)
    angles = (chan_list[:, None] * columns[None, :] % POINTS).astype(jnp.float32) * (
        2.0 * jnp.pi / POINTS
    )
    waves = jnp.stack([jnp.cos(angles), -jnp.sin(angles)], axis=0)
    waves = waves.reshape(2, freq_size, 2, -1, POINTS).transpose(2, 1, 0, 3, 4)
    return (window * waves.reshape(1, -1, POINTS)).astype(jnp.bfloat16)


def channelize(frames, filters):
    return lax.conv_general_dilated(
        frames,
        filters,
        window_strides=(1,),
        padding="VALID",
        dimension_numbers=("NWC", "WOI", "CNW"),
        preferred_element_type=jnp.float32,
    ).astype(jnp.bfloat16)


def visibility_kernel(swaps, own, *refs):
    partners, (kept, given) = refs[:-2], refs[-2:]
    for block in range(2):
        real, imag = own[0, block, 0], own[1, block, 0]
        stacked = jnp.concatenate(
            [
                jnp.concatenate([real, imag], axis=1),
                jnp.concatenate([imag, -real], axis=1),
            ],
            axis=0,
        )
        tile = real.shape[0]
        found = kept if block == 0 else given
        for index, partner in enumerate(partners):
            other = swaps[index] if block == 0 else 1 - swaps[index]
            moving = jnp.concatenate([partner[0, other, 0], partner[1, other, 0]], axis=1)
            product = lax.dot_general(
                stacked, moving, (((1,), (1,)), ((), ())), preferred_element_type=jnp.float32
            )
            product = (product * (1.0 / SPECTRA)).astype(jnp.bfloat16)
            found[index, 0, 0] = product[:tile]
            found[index, 0, 1] = product[tile:]


def visibilities(own, partners, swaps):
    _, _, chans, tile, spectra = own.shape
    count = len(partners)
    data = pl.BlockSpec((2, 2, 1, tile, spectra), lambda chan, _: (0, 0, chan, 0, 0))
    made = pl.BlockSpec((count, 1, 2, tile, tile), lambda chan, _: (0, chan, 0, 0, 0))
    shape = jax.ShapeDtypeStruct((count, chans, 2, tile, tile), jnp.bfloat16)
    return pl.pallas_call(
        visibility_kernel,
        grid_spec=pltpu.PrefetchScalarGridSpec(
            num_scalar_prefetch=1,
            grid=(chans,),
            in_specs=[data] * (1 + count),
            out_specs=[made, made],
        ),
        out_shape=[shape, shape],
        compiler_params=pltpu.CompilerParams(vmem_limit_bytes=24 * 1024 * 1024),
    )(jnp.stack(swaps).astype(jnp.int32), own, *partners)


def body(samples, chan_list):
    freq_size = lax.axis_size("freq")
    half = lax.axis_size("blk") // 2
    column, plane = lax.axis_index("blk") // half, lax.axis_index("blk") % half
    inputs = samples.shape[1]
    tile = freq_size * inputs
    frames = samples.reshape(inputs, samples.shape[2] // POINTS, POINTS)
    chans = CHANNELS // freq_size // 2
    voltages = channelize(frames, filter_table(chan_list, freq_size))
    voltages = voltages.reshape(2, freq_size, 2, 1, chans, inputs, SPECTRA)

    kept = lax.dynamic_index_in_dim(voltages, column, 0, keepdims=False)
    given = lax.dynamic_index_in_dim(voltages, 1 - column, 0, keepdims=False)
    pair = jnp.concatenate([kept, to_twin(given)], axis=2)
    pair = lax.all_to_all(pair, "freq", split_axis=0, concat_axis=4, tiled=True)

    blocks, tiles = {0: pair.reshape(2, 2, chans, tile, SPECTRA)}, {}

    def near(*partners):
        sources = [blocks[0 if at == half else at] for at in partners]
        swaps = [
            jnp.bool_(True) if at == half else (plane + at) % half > plane for at in partners
        ]
        mine, theirs = visibilities(blocks[0], sources, swaps)
        moved = to_twin(theirs)
        for index, at in enumerate(partners):
            tiles[half if at == half else -at % half] = (mine[index], moved[index])

    def far(owner, partner):
        swap = (plane + partner) % half > (plane + owner) % half
        mine, theirs = visibilities(blocks[owner], [blocks[partner]], [swap])
        tiles[(owner - partner) % half] = (
            along_ring(mine, owner)[0],
            along_ring(theirs, owner, 1)[0],
        )

    def step(partner):
        way = 1 if partner < 0 else -1
        blocks[partner] = along_ring(blocks[partner + way], way)

    def settle():
        nonlocal tiles, blocks
        tiles, blocks = lax.optimization_barrier((tiles, blocks))

    step(-1), step(1)
    near(0, half)
    settle()
    step(-2), step(2)
    near(-1, 1)
    settle()
    step(-3)
    near(-2, 2)
    far(-1, 2)
    settle()
    far(1, -3)
    near(-3)

    def whole(place):
        return jnp.stack([tiles[offset][place] for offset in range(half + 1)], axis=1)

    mine, theirs = whole(0), whole(1)
    low = jnp.where(column == 0, mine, theirs)
    high = jnp.where(column == 0, theirs, mine)
    return jnp.concatenate([low, high], axis=0)[:, None]


def solution(mesh):
    in_specs = (P("blk", "freq", None), P())
    out_specs = P("freq", "blk", None, None, None, None)
    return jax.shard_map(body, mesh=mesh, in_specs=in_specs, out_specs=out_specs, check_vma=False)
```

time: 158 us -> 152 us (0.962)
  Pallas kernels: 0 us -> 17.4 us
  matrix products: 17.4 us -> 4.59 us
  starting transfers between devices: 44.8 us -> 32.3 us
  other arithmetic: 10.7 us -> 3.19 us
  waiting for transfers between devices: 55.9 us -> 62.3 us
  local copies, waits for them, and re-layouts: 8.39 us -> 11.4 us
    pallas_call x0 -> x6, Pallas kernels: none -> 17.4 us  [visibilities(): pl.pallas_call(visibility_kernel, grid_spec=pltpu.PrefetchScalarGridSpec(...]
    dot_general x24 -> x0, matrix products: 12.8 us -> none  [cross_block(): lax.dot_general(stacked, moving, (((0, 3), (0, 3)), ((1,), (1,))), prefer...]
    ppermute x19 -> x14, starting transfers between devices: 44.8 us -> 32.3 us  [along_ring(): return lax.ppermute(value, 'blk', pairs)]
    ppermute x19 -> x14, waiting for transfers between devices: 55.9 us -> 62.3 us  [along_ring(): return lax.ppermute(value, 'blk', pairs)]
    broadcast_in_dim x0 -> x1, local copies, waits for them, and re-layouts: none -> 3.15 us  [body(): return jnp.concatenate([low, high], axis=0)[:, None]]
    another operation x21 -> x0, other arithmetic: 2.89 us -> none  [the longest x17 1.92 us: stack_parts(): jnp.stack([jnp.concatenate([own[0], own[1]], axis=1), jnp.concatenate([ow...]
    neg x8 -> x0, other arithmetic: 2.46 us -> none  [stack_parts(): -own[0]]
    broadcast_in_dim x1, other arithmetic: 2.59 us -> 0.41 us  [body(): return jnp.concatenate([low, high], axis=0)[:, None]]
  transfers between devices with their start and end apart: 19 -> 14, of which waited for: 10 -> 9; matrix products, arithmetic and copies ran while one was open for 9% -> 3% of each run, Pallas kernels for 0% -> 11%
where the time goes in v3:
time: 152 us
  waiting for transfers between devices  62.3 us (41%)
  starting transfers between devices  32.3 us (21%)
  blocking collectives  19.2 us (13%)
  Pallas kernels  17.4 us (11%)
  local copies, waits for them, and re-layouts  11.4 us (8%)
  matrix products  4.59 us (3%)
  other arithmetic  3.19 us (2%)
    ppermute x14, waiting for transfers between devices, along_ring(): return lax.ppermute(value, 'blk', pairs)  62.3 us
    ppermute x14, starting transfers between devices, along_ring(): return lax.ppermute(value, 'blk', pairs)  32.3 us
    all_to_all x1, blocking collectives, body(): pair = lax.all_to_all(pair, 'freq', split_axis=0, concat_axis=4, tiled=True)  19.2 us
    pallas_call x6, Pallas kernels, visibilities(): pl.pallas_call(visibility_kernel, grid_spec=pltpu.PrefetchScalarGridSpec(...  17.4 us
    conv_general_dilated x1, matrix products, channelize(): lax.conv_general_dilated(frames, filters, window_strides=(1,), padding='V...  4.59 us
    squeeze x6, local copies, waits for them, and re-layouts, near(): tiles[half if at == half else -at % half] = (mine[index], moved[index])  4.38 us
    broadcast_in_dim x1, local copies, waits for them, and re-layouts, body(): return jnp.concatenate([low, high], axis=0)[:, None]  3.15 us
  transfers between devices with their start and end apart: 14, of which 9 were waited for; matrix products, arithmetic and copies ran while one was open for 3% of the time, Pallas kernels for 11%

profile of v3, /device:TPU:6, one launch (start us, length us, event | category | flops | bytes accessed | tf_op | source)
XLA Modules:
  0.0 151.6 jit_solution(3793005286021305163)
XLA Ops:
  0.0 0.0 copy-start
  0.0 0.7 fusion.17
  1.4 0.1 fusion.9
  1.6 0.8 mul.110
  2.4 1.2 fusion.7
  3.6 0.1 maximum_bitcast_fusion.1
  3.7 0.1 mul.116
  3.8 4.6 %fusion.3 = bf16[256,8,256]{0,1,2:T(8,128)(2,1)S(1)} fusion(bf16[8,271,256]{2,0,1:T(8,128)(2,1)S(1)} %bitcast.88, f32[256,256]{1,0:T(8,128)S(1)} %mul.116, f32[16,256]{1,0:T(8,128)S(1)} %fusion.9), kind=kOutput, calls=%fused_computation.7 | convolution fusion | flops 4297588736 | bytes 2437120 | tf_op jit(solution)/shard_map/conv_general_dilated | solution.py:45
  8.4 1.3 copy.15
  9.6 0.1 dynamic-slice_bitcast_fusion.1
  9.8 3.3 %collective-permute-start = (bf16[16,2,1,4,8,256]{5,4,3,1,0,2:T(8,128)(2,1)S(1)}, bf16[16,2,1,4,8,256]{5,4,3,1,0,2:T(8,128)(2,1)S(1)}, u32[]{:S(2)}, u32[]{:S(2)}) collective-permute-start(bf16[16,2,1,4,8,256]{5,4,3,1,0,2:T(8,128)(2,1)S(1)} %get-tuple-element.106), channel_id=1, source_target_pairs={{0,8},{1,9},{2,10},{3,11},{4,12},{5,13},{6,14},{7,15},{8,0},{9,1},... | collective-permute-start | bytes 1572872 | tf_op jit(solution)/shard_map/ppermute | solution.py:20
  13.0 12.0 %collective-permute-done = bf16[16,2,1,4,8,256]{5,4,3,1,0,2:T(8,128)(2,1)S(1)} collective-permute-done((bf16[16,2,1,4,8,256]{5,4,3,1,0,2:T(8,128)(2,1)S(1)}, bf16[16,2,1,4,8,256]{5,4,3,1,0,2:T(8,128)(2,1)S(1)}, u32[]{:S(2)}, u32[]{:S(2)}) %collective-permute-start) | collective-permute-done | bytes 524320 | tf_op jit(solution)/shard_map/ppermute | solution.py:20
  25.0 0.1 pad_maximum_fusion
  25.1 0.1 copy.16
  25.2 19.2 %all_to_all.15 = bf16[16,2,2,4,8,256]{5,4,3,1,2,0:T(8,128)(2,1)S(1)} all-to-all(bf16[16,2,2,4,8,256]{5,4,3,1,2,0:T(8,128)(2,1)S(1)} %copy.16), channel_id=1, replica_groups=mesh['freq'=16,'blk'=16] {'freq'}, dimensions={0} | all-to-all | bytes 2097152 | tf_op jit(solution)/shard_map/all_to_all | solution.py:112
  44.4 0.1 copy_bitcast_fusion.own.refs_0_.refs_1_
  44.6 5.9 %collective-permute-start.3 = (bf16[2,2,4,128,256]{4,3,2,1,0:T(8,128)(2,1)S(1)}, bf16[2,2,4,128,256]{4,3,2,1,0:T(8,128)(2,1)S(1)}, u32[]{:S(2)}, u32[]{:S(2)}) collective-permute-start(bf16[2,2,4,128,256]{4,3,2,1,0:T(8,128)(2,1)S(1)} %copy_bitcast_fusion.own.refs_0_.refs_1_), channel_id=1, source_target_pairs={{0,7},{1,0},{2,1},{3,2},{4,3},{5,4},{6,5},{7,6},{8,15},{9,8},{10,9... | collective-permute-start | bytes 3145736 | tf_op jit(solution)/shard_map/ppermute | solution.py:20
  50.5 0.0 collective-permute-start.2
  50.5 0.1 add_convert_fusion.swaps
  50.6 2.6 %shard_map.28 = (bf16[2,4,2,128,128]{4,3,2,1,0:T(8,128)(2,1)S(1)}, bf16[2,4,2,128,128]{4,3,2,1,0:T(8,128)(2,1)S(1)}) custom-call(s32[2]{0:T(128)S(1)} %add_convert_fusion.swaps, bf16[2,2,4,128,256]{4,3,2,1,0:T(8,128)(2,1)S(1)} %copy_bitcast_fusion.own.refs_0_.refs_1_, bf16[2,2,4,128,256]{4,3,2,1,0:T(8,128)(2,1)S(1)} %copy_bitcast_fusion.own.refs_0_.refs_1_, ...), custom_call_target="tpu_custom_call" | custom-call | tf_op jit(solution)/shard_map/pallas_call | solution.py:85
  53.2 3.0 %collective-permute-start.1 = (bf16[2,4,2,128,128]{4,3,2,1,0:T(8,128)(2,1)S(1)}, bf16[2,4,2,128,128]{4,3,2,1,0:T(8,128)(2,1)S(1)}, u32[]{:S(2)}, u32[]{:S(2)}) collective-permute-start(bf16[2,4,2,128,128]{4,3,2,1,0:T(8,128)(2,1)S(1)} %get-tuple-element.55), channel_id=1, source_target_pairs={{0,8},{1,9},{2,10},{3,11},{4,12},{5,13},{6,14},{7,15},{8,0},{9,1},... | collective-permute-start | bytes 1572872 | tf_op jit(solution)/shard_map/ppermute | solution.py:20
  56.2 0.7 slice_bitcast_fusion.10
  56.9 12.1 %collective-permute-done.1 = bf16[2,4,2,128,128]{4,3,2,1,0:T(8,128)(2,1)S(1)} collective-permute-done((bf16[2,4,2,128,128]{4,3,2,1,0:T(8,128)(2,1)S(1)}, bf16[2,4,2,128,128]{4,3,2,1,0:T(8,128)(2,1)S(1)}, u32[]{:S(2)}, u32[]{:S(2)}) %collective-permute-start.1) | collective-permute-done | bytes 524320 | tf_op jit(solution)/shard_map/ppermute | solution.py:20
  69.0 0.9 slice_bitcast_fusion.4
  69.8 3.9 %collective-permute-done.3.refs_1_.own = bf16[2,2,4,128,256]{4,3,2,1,0:T(8,128)(2,1)S(1)} collective-permute-done((bf16[2,2,4,128,256]{4,3,2,1,0:T(8,128)(2,1)S(1)}, bf16[2,2,4,128,256]{4,3,2,1,0:T(8,128)(2,1)S(1)}, u32[]{:S(2)}, u32[]{:S(2)}) %collective-permute-start.3) | collective-permute-done | bytes 1048608 | tf_op jit(solution)/shard_map/ppermute | solution.py:20
  73.7 3.5 %collective-permute-done.2.refs_0_.own = bf16[2,2,4,128,256]{4,3,2,1,0:T(8,128)(2,1)} collective-permute-done((bf16[2,2,4,128,256]{4,3,2,1,0:T(8,128)(2,1)S(1)}, bf16[2,2,4,128,256]{4,3,2,1,0:T(8,128)(2,1)}, u32[]{:S(2)}, u32[]{:S(2)}) %collective-permute-start.2) | collective-permute-done | bytes 1048608 | tf_op jit(solution)/shard_map/ppermute | solution.py:20
  77.2 0.0 collective-permute-start.5
  77.2 3.2 %collective-permute-start.6 = (bf16[2,2,4,128,256]{4,3,2,1,0:T(8,128)(2,1)S(1)}, bf16[2,2,4,128,256]{4,3,2,1,0:T(8,128)(2,1)}, u32[]{:S(2)}, u32[]{:S(2)}) collective-permute-start(bf16[2,2,4,128,256]{4,3,2,1,0:T(8,128)(2,1)S(1)} %collective-permute-done.3.refs_1_.own), channel_id=1, source_target_pairs={{0,7},{1,0},{2,1},{3,2},{4,3},{5,4},{6,5},{7,6},{8,15},{9,8},{10,9... | collective-permute-start | bytes 3145736 | tf_op jit(solution)/shard_map/ppermute | solution.py:20
  80.5 0.1 add_convert_fusion.1.swaps
  80.5 3.9 %shard_map.29 = (bf16[2,4,2,128,128]{4,3,2,1,0:T(8,128)(2,1)S(1)}, bf16[2,4,2,128,128]{4,3,2,1,0:T(8,128)(2,1)S(1)}) custom-call(s32[2]{0:T(128)S(1)} %add_convert_fusion.1.swaps, bf16[2,2,4,128,256]{4,3,2,1,0:T(8,128)(2,1)S(1)} %copy_bitcast_fusion.own.refs_0_.refs_1_, bf16[2,2,4,128,256]{4,3,2,1,0:T(8,128)(2,1)} %collective-permute-done.2.refs_0_.own, ...), custom_call_target="tpu_custom_call" | custom-call | tf_op jit(solution)/shard_map/pallas_call | solution.py:85
  84.5 3.2 %collective-permute-start.4 = (bf16[2,4,2,128,128]{4,3,2,1,0:T(8,128)(2,1)S(1)}, bf16[2,4,2,128,128]{4,3,2,1,0:T(8,128)(2,1)S(1)}, u32[]{:S(2)}, u32[]{:S(2)}) collective-permute-start(bf16[2,4,2,128,128]{4,3,2,1,0:T(8,128)(2,1)S(1)} %get-tuple-element.62), channel_id=1, source_target_pairs={{0,8},{1,9},{2,10},{3,11},{4,12},{5,13},{6,14},{7,15},{8,0},{9,1},... | collective-permute-start | bytes 1572872 | tf_op jit(solution)/shard_map/ppermute | solution.py:20
  87.7 0.9 slice_bitcast_fusion.8
  88.5 10.6 %collective-permute-done.4 = bf16[2,4,2,128,128]{4,3,2,1,0:T(8,128)(2,1)S(1)} collective-permute-done((bf16[2,4,2,128,128]{4,3,2,1,0:T(8,128)(2,1)S(1)}, bf16[2,4,2,128,128]{4,3,2,1,0:T(8,128)(2,1)S(1)}, u32[]{:S(2)}, u32[]{:S(2)}) %collective-permute-start.4) | collective-permute-done | bytes 524320 | tf_op jit(solution)/shard_map/ppermute | solution.py:20
  99.1 0.8 slice_bitcast_fusion.2
  99.9 3.5 %collective-permute-done.5.refs_0_ = bf16[2,2,4,128,256]{4,3,2,1,0:T(8,128)(2,1)} collective-permute-done((bf16[2,2,4,128,256]{4,3,2,1,0:T(8,128)(2,1)}, bf16[2,2,4,128,256]{4,3,2,1,0:T(8,128)(2,1)}, u32[]{:S(2)}, u32[]{:S(2)}) %collective-permute-start.5) | collective-permute-done | bytes 1048608 | tf_op jit(solution)/shard_map/ppermute | solution.py:20
  103.4 0.0 collective-permute-done.6.refs_1_.refs_0_
  103.4 0.0 collective-permute-start.10
  103.4 0.1 add_convert_fusion.2.swaps
  103.5 4.9 %shard_map.30 = (bf16[2,4,2,128,128]{4,3,2,1,0:T(8,128)(2,1)S(1)}, bf16[2,4,2,128,128]{4,3,2,1,0:T(8,128)(2,1)}) custom-call(s32[2]{0:T(128)S(1)} %add_convert_fusion.2.swaps, bf16[2,2,4,128,256]{4,3,2,1,0:T(8,128)(2,1)S(1)} %copy_bitcast_fusion.own.refs_0_.refs_1_, bf16[2,2,4,128,256]{4,3,2,1,0:T(8,128)(2,1)} %collective-permute-done.5.refs_0_, ...), custom_call_target="tpu_custom_call" | custom-call | tf_op jit(solution)/shard_map/pallas_call | solution.py:85
  108.3 0.8 copy-done.3
  109.1 2.9 %collective-permute-start.7 = (bf16[2,4,2,128,128]{4,3,2,1,0:T(8,128)(2,1)}, bf16[2,4,2,128,128]{4,3,2,1,0:T(8,128)(2,1)}, u32[]{:S(2)}, u32[]{:S(2)}) collective-permute-start(bf16[2,4,2,128,128]{4,3,2,1,0:T(8,128)(2,1)} %get-tuple-element.73), channel_id=1, source_target_pairs={{0,8},{1,9},{2,10},{3,11},{4,12},{5,13},{6,14},{7,15},{8,0},{9,1},... | collective-permute-start | bytes 1572872 | tf_op jit(solution)/shard_map/ppermute | solution.py:20
  112.0 3.1 %shard_map.31 = (bf16[1,4,2,128,128]{4,3,2,1,0:T(8,128)(2,1)S(1)}, bf16[1,4,2,128,128]{4,3,2,1,0:T(8,128)(2,1)S(1)}) custom-call(s32[1]{0:T(128)} %bitcast.23.swaps, bf16[2,2,4,128,256]{4,3,2,1,0:T(8,128)(2,1)} %collective-permute-done.2.refs_0_.own, bf16[2,2,4,128,256]{4,3,2,1,0:T(8,128)(2,1)} %collective-permute-done.6.refs_1_.refs_0_), custom_call_target="tpu_custom_call" | custom-call | tf_op jit(solution)/shard_map/pallas_call | solution.py:85
  115.2 0.0 copy-start.2
  115.2 3.3 %collective-permute-start.8 = (bf16[1,4,2,128,128]{4,3,2,1,0:T(8,128)(2,1)S(1)}, bf16[1,4,2,128,128]{4,3,2,1,0:T(8,128)(2,1)S(1)}, u32[]{:S(2)}, u32[]{:S(2)}) collective-permute-start(bf16[1,4,2,128,128]{4,3,2,1,0:T(8,128)(2,1)S(1)} %get-tuple-element.75), channel_id=1, source_target_pairs={{0,7},{1,0},{2,1},{3,2},{4,3},{5,4},{6,5},{7,6},{8,15},{9,8},{10,9... | collective-permute-start | bytes 786440 | tf_op jit(solution)/shard_map/ppermute | solution.py:20
  118.5 1.6 %collective-permute-start.9 = (bf16[1,4,2,128,128]{4,3,2,1,0:T(8,128)(2,1)S(1)}, bf16[1,4,2,128,128]{4,3,2,1,0:T(8,128)(2,1)S(1)}, u32[]{:S(2)}, u32[]{:S(2)}) collective-permute-start(bf16[1,4,2,128,128]{4,3,2,1,0:T(8,128)(2,1)S(1)} %get-tuple-element.76), channel_id=1, source_target_pairs={{0,15},{1,8},{2,9},{3,10},{4,11},{5,12},{6,13},{7,14},{8,7},{9,0},... | collective-permute-start | bytes 786440 | tf_op jit(solution)/shard_map/ppermute | solution.py:20
  120.1 8.9 %collective-permute-done.7 = bf16[2,4,2,128,128]{4,3,2,1,0:T(8,128)(2,1)} collective-permute-done((bf16[2,4,2,128,128]{4,3,2,1,0:T(8,128)(2,1)}, bf16[2,4,2,128,128]{4,3,2,1,0:T(8,128)(2,1)}, u32[]{:S(2)}, u32[]{:S(2)}) %collective-permute-start.7) | collective-permute-done | bytes 524320 | tf_op jit(solution)/shard_map/ppermute | solution.py:20
  129.0 1.1 slice_bitcast_fusion
  130.1 0.0 collective-permute-done.8
  130.1 0.0 collective-permute-done.9
  130.1 0.0 collective-permute-done.10.refs_0_
  130.2 1.4 shard_map.32
  131.6 0.0 copy-start.11
  131.6 3.0 %collective-permute-start.12 = (bf16[1,4,2,128,128]{4,3,2,1,0:T(8,128)(2,1)S(1)}, bf16[1,4,2,128,128]{4,3,2,1,0:T(8,128)(2,1)S(1)}, u32[]{:S(2)}, u32[]{:S(2)}) collective-permute-start(bf16[1,4,2,128,128]{4,3,2,1,0:T(8,128)(2,1)S(1)} %get-tuple-element.97), channel_id=1, source_target_pairs={{0,8},{1,9},{2,10},{3,11},{4,12},{5,13},{6,14},{7,15},{8,0},{9,1},... | collective-permute-start | bytes 786440 | tf_op jit(solution)/shard_map/ppermute | solution.py:20
  134.6 1.4 shard_map.33
  136.0 0.2 collective-permute-start.11
  136.2 2.7 %collective-permute-start.13 = (bf16[1,4,2,128,128]{4,3,2,1,0:T(8,128)(2,1)S(1)}, bf16[1,4,2,128,128]{4,3,2,1,0:T(8,128)(2,1)S(1)}, u32[]{:S(2)}, u32[]{:S(2)}) collective-permute-start(bf16[1,4,2,128,128]{4,3,2,1,0:T(8,128)(2,1)S(1)} %get-tuple-element.98), channel_id=1, source_target_pairs={{0,9},{1,10},{2,11},{3,12},{4,13},{5,14},{6,15},{7,8},{8,1},{9,2},... | collective-permute-start | bytes 786440 | tf_op jit(solution)/shard_map/ppermute | solution.py:20
  139.0 0.0 copy-done.7
  139.1 0.1 bitcast_dynamic-update-slice_fusion.6
  139.3 3.1 %collective-permute-done.12 = bf16[1,4,2,128,128]{4,3,2,1,0:T(8,128)(2,1)S(1)} collective-permute-done((bf16[1,4,2,128,128]{4,3,2,1,0:T(8,128)(2,1)S(1)}, bf16[1,4,2,128,128]{4,3,2,1,0:T(8,128)(2,1)S(1)}, u32[]{:S(2)}, u32[]{:S(2)}) %collective-permute-start.12) | collective-permute-done | bytes 262176 | tf_op jit(solution)/shard_map/ppermute | solution.py:20
  142.4 4.8 %collective-permute-done.13 = bf16[1,4,2,128,128]{4,3,2,1,0:T(8,128)(2,1)S(1)} collective-permute-done((bf16[1,4,2,128,128]{4,3,2,1,0:T(8,128)(2,1)S(1)}, bf16[1,4,2,128,128]{4,3,2,1,0:T(8,128)(2,1)S(1)}, u32[]{:S(2)}, u32[]{:S(2)}) %collective-permute-start.13) | collective-permute-done | bytes 262176 | tf_op jit(solution)/shard_map/ppermute | solution.py:20
  147.4 0.0 collective-permute-done.11
  147.7 0.3 broadcast_select_fusion.1
  148.0 0.4 maximum_bitcast_fusion
  148.4 3.1 %copy.18 = bf16[8,1,9,2,128,128]{5,4,3,2,1,0:T(8,128)(2,1)} copy(bf16[8,1,9,2,128,128]{5,4,3,0,2,1:T(8,128)(2,1)S(1)} %maximum_bitcast_fusion) | data formatting | bytes 9437184 | tf_op jit(solution)/shard_map/broadcast_in_dim | solution.py:161
  (37 shorter events, 0.6 us)
Async XLA Ops:
  0.0 3.8 %copy-start = (bf16[1,8,69376]{2,1,0:T(8,128)(2,1)S(1)}, bf16[1,8,69376]{2,1,0:T(8,128)(2,1)}, u32[]{:S(2)}) copy-start(bf16[1,8,69376]{2,1,0:T(8,128)(2,1)} %param.2) | copy-start | bytes 3330052
  9.8 15.3 %collective-permute-start = (bf16[16,2,1,4,8,256]{5,4,3,1,0,2:T(8,128)(2,1)S(1)}, bf16[16,2,1,4,8,256]{5,4,3,1,0,2:T(8,128)(2,1)S(1)}, u32[]{:S(2)}, u32[]{:S(2)}) collective-permute-start(bf16[16,2,1,4,8,256]{5,4,3,1,0,2:T(8,128)(2,1)S(1)} %get-tuple-element.106), channel_id=1, source_target_pairs={{0,8},{1,9},{2,10},{3,11},{4,12},{5,13},{6,14},{7,15},{8,0},{9,1},... | collective-permute-start | bytes 1572872 | tf_op jit(solution)/shard_map/ppermute | solution.py:20
  44.6 29.2 %collective-permute-start.3 = (bf16[2,2,4,128,256]{4,3,2,1,0:T(8,128)(2,1)S(1)}, bf16[2,2,4,128,256]{4,3,2,1,0:T(8,128)(2,1)S(1)}, u32[]{:S(2)}, u32[]{:S(2)}) collective-permute-start(bf16[2,2,4,128,256]{4,3,2,1,0:T(8,128)(2,1)S(1)} %copy_bitcast_fusion.own.refs_0_.refs_1_), channel_id=1, source_target_pairs={{0,7},{1,0},{2,1},{3,2},{4,3},{5,4},{6,5},{7,6},{8,15},{9,8},{10,9... | collective-permute-start | bytes 3145736 | tf_op jit(solution)/shard_map/ppermute | solution.py:20
  50.5 26.7 %collective-permute-start.2 = (bf16[2,2,4,128,256]{4,3,2,1,0:T(8,128)(2,1)S(1)}, bf16[2,2,4,128,256]{4,3,2,1,0:T(8,128)(2,1)}, u32[]{:S(2)}, u32[]{:S(2)}) collective-permute-start(bf16[2,2,4,128,256]{4,3,2,1,0:T(8,128)(2,1)S(1)} %copy_bitcast_fusion.own.refs_0_.refs_1_), channel_id=1, source_target_pairs={{0,1},{1,2},{2,3},{3,4},{4,5},{5,6},{6,7},{7,0},{8,9},{9,10},{10,1... | collective-permute-start | bytes 3145736 | tf_op jit(solution)/shard_map/ppermute | solution.py:20
  53.2 15.8 %collective-permute-start.1 = (bf16[2,4,2,128,128]{4,3,2,1,0:T(8,128)(2,1)S(1)}, bf16[2,4,2,128,128]{4,3,2,1,0:T(8,128)(2,1)S(1)}, u32[]{:S(2)}, u32[]{:S(2)}) collective-permute-start(bf16[2,4,2,128,128]{4,3,2,1,0:T(8,128)(2,1)S(1)} %get-tuple-element.55), channel_id=1, source_target_pairs={{0,8},{1,9},{2,10},{3,11},{4,12},{5,13},{6,14},{7,15},{8,0},{9,1},... | collective-permute-start | bytes 1572872 | tf_op jit(solution)/shard_map/ppermute | solution.py:20
  73.7 26.2 %copy-start.1 = (bf16[2,2,4,128,256]{4,3,2,1,0:T(8,128)(2,1)}, bf16[2,2,4,128,256]{4,3,2,1,0:T(8,128)(2,1)S(1)}, u32[]{:S(2)}) copy-start(bf16[2,2,4,128,256]{4,3,2,1,0:T(8,128)(2,1)S(1)} %collective-permute-done.3.refs_1_.own) | copy-start | bytes 3145732
  77.2 26.1 %collective-permute-start.5 = (bf16[2,2,4,128,256]{4,3,2,1,0:T(8,128)(2,1)}, bf16[2,2,4,128,256]{4,3,2,1,0:T(8,128)(2,1)}, u32[]{:S(2)}, u32[]{:S(2)}) collective-permute-start(bf16[2,2,4,128,256]{4,3,2,1,0:T(8,128)(2,1)} %collective-permute-done.2.refs_0_.own), channel_id=1, source_target_pairs={{0,1},{1,2},{2,3},{3,4},{4,5},{5,6},{6,7},{7,0},{8,9},{9,10},{10,1... | collective-permute-start | bytes 3145736 | tf_op jit(solution)/shard_map/ppermute | solution.py:20
  77.2 26.1 %collective-permute-start.6 = (bf16[2,2,4,128,256]{4,3,2,1,0:T(8,128)(2,1)S(1)}, bf16[2,2,4,128,256]{4,3,2,1,0:T(8,128)(2,1)}, u32[]{:S(2)}, u32[]{:S(2)}) collective-permute-start(bf16[2,2,4,128,256]{4,3,2,1,0:T(8,128)(2,1)S(1)} %collective-permute-done.3.refs_1_.own), channel_id=1, source_target_pairs={{0,7},{1,0},{2,1},{3,2},{4,3},{5,4},{6,5},{7,6},{8,15},{9,8},{10,9... | collective-permute-start | bytes 3145736 | tf_op jit(solution)/shard_map/ppermute | solution.py:20
  84.5 14.6 %collective-permute-start.4 = (bf16[2,4,2,128,128]{4,3,2,1,0:T(8,128)(2,1)S(1)}, bf16[2,4,2,128,128]{4,3,2,1,0:T(8,128)(2,1)S(1)}, u32[]{:S(2)}, u32[]{:S(2)}) collective-permute-start(bf16[2,4,2,128,128]{4,3,2,1,0:T(8,128)(2,1)S(1)} %get-tuple-element.62), channel_id=1, source_target_pairs={{0,8},{1,9},{2,10},{3,11},{4,12},{5,13},{6,14},{7,15},{8,0},{9,1},... | collective-permute-start | bytes 1572872 | tf_op jit(solution)/shard_map/ppermute | solution.py:20
  103.4 26.8 %collective-permute-start.10 = (bf16[2,2,4,128,256]{4,3,2,1,0:T(8,128)(2,1)}, bf16[2,2,4,128,256]{4,3,2,1,0:T(8,128)(2,1)S(1)}, u32[]{:S(2)}, u32[]{:S(2)}) collective-permute-start(bf16[2,2,4,128,256]{4,3,2,1,0:T(8,128)(2,1)} %collective-permute-done.5.refs_0_), channel_id=1, source_target_pairs={{0,1},{1,2},{2,3},{3,4},{4,5},{5,6},{6,7},{7,0},{8,9},{9,10},{10,1... | collective-permute-start | bytes 3145736 | tf_op jit(solution)/shard_map/ppermute | solution.py:20
  108.3 0.8 copy-start.3
  109.1 19.9 %collective-permute-start.7 = (bf16[2,4,2,128,128]{4,3,2,1,0:T(8,128)(2,1)}, bf16[2,4,2,128,128]{4,3,2,1,0:T(8,128)(2,1)}, u32[]{:S(2)}, u32[]{:S(2)}) collective-permute-start(bf16[2,4,2,128,128]{4,3,2,1,0:T(8,128)(2,1)} %get-tuple-element.73), channel_id=1, source_target_pairs={{0,8},{1,9},{2,10},{3,11},{4,12},{5,13},{6,14},{7,15},{8,0},{9,1},... | collective-permute-start | bytes 1572872 | tf_op jit(solution)/shard_map/ppermute | solution.py:20
  112.0 8.0 %copy-start.4 = (bf16[2,4,2,128,128]{4,3,2,1,0:T(8,128)(2,1)S(1)}, bf16[2,4,2,128,128]{4,3,2,1,0:T(8,128)(2,1)}, u32[]{:S(2)}) copy-start(bf16[2,4,2,128,128]{4,3,2,1,0:T(8,128)(2,1)} %copy-done.3) | copy-start | bytes 1572868
  115.2 19.4 %copy-start.2 = (bf16[2,2,4,128,256]{4,3,2,1,0:T(8,128)(2,1)S(1)}, bf16[2,2,4,128,256]{4,3,2,1,0:T(8,128)(2,1)}, u32[]{:S(2)}) copy-start(bf16[2,2,4,128,256]{4,3,2,1,0:T(8,128)(2,1)} %copy-done.1) | copy-start | bytes 3145732
  115.2 15.0 %collective-permute-start.8 = (bf16[1,4,2,128,128]{4,3,2,1,0:T(8,128)(2,1)S(1)}, bf16[1,4,2,128,128]{4,3,2,1,0:T(8,128)(2,1)S(1)}, u32[]{:S(2)}, u32[]{:S(2)}) collective-permute-start(bf16[1,4,2,128,128]{4,3,2,1,0:T(8,128)(2,1)S(1)} %get-tuple-element.75), channel_id=1, source_target_pairs={{0,7},{1,0},{2,1},{3,2},{4,3},{5,4},{6,5},{7,6},{8,15},{9,8},{10,9... | collective-permute-start | bytes 786440 | tf_op jit(solution)/shard_map/ppermute | solution.py:20
  118.5 11.7 %collective-permute-start.9 = (bf16[1,4,2,128,128]{4,3,2,1,0:T(8,128)(2,1)S(1)}, bf16[1,4,2,128,128]{4,3,2,1,0:T(8,128)(2,1)S(1)}, u32[]{:S(2)}, u32[]{:S(2)}) collective-permute-start(bf16[1,4,2,128,128]{4,3,2,1,0:T(8,128)(2,1)S(1)} %get-tuple-element.76), channel_id=1, source_target_pairs={{0,15},{1,8},{2,9},{3,10},{4,11},{5,12},{6,13},{7,14},{8,7},{9,0},... | collective-permute-start | bytes 786440 | tf_op jit(solution)/shard_map/ppermute | solution.py:20
  130.1 8.8 %copy-start.6 = (bf16[4,2,128,128]{3,2,1,0:T(8,128)(2,1)S(1)}, bf16[4,2,128,128]{3,2,1,0:T(8,128)(2,1)}, u32[]{:S(2)}) copy-start(bf16[4,2,128,128]{3,2,1,0:T(8,128)(2,1)} %get-tuple-element.82) | copy-start | bytes 786436
  130.1 8.8 %copy-start.7 = (bf16[4,2,128,128]{3,2,1,0:T(8,128)(2,1)S(1)}, bf16[4,2,128,128]{3,2,1,0:T(8,128)(2,1)}, u32[]{:S(2)}) copy-start(bf16[4,2,128,128]{3,2,1,0:T(8,128)(2,1)} %get-tuple-element.94) | copy-start | bytes 786436
  130.2 8.8 %copy-start.10 = (bf16[4,2,128,128]{3,2,1,0:T(8,128)(2,1)S(1)}, bf16[4,2,128,128]{3,2,1,0:T(8,128)(2,1)}, u32[]{:S(2)}) copy-start(bf16[4,2,128,128]{3,2,1,0:T(8,128)(2,1)} %get-tuple-element.83) | copy-start | bytes 786436
  131.6 7.5 %copy-start.11 = (bf16[4,2,128,128]{3,2,1,0:T(8,128)(2,1)S(1)}, bf16[4,2,128,128]{3,2,1,0:T(8,128)(2,1)}, u32[]{:S(2)}) copy-start(bf16[4,2,128,128]{3,2,1,0:T(8,128)(2,1)} %get-tuple-element.95) | copy-start | bytes 786436
  131.6 10.8 %collective-permute-start.12 = (bf16[1,4,2,128,128]{4,3,2,1,0:T(8,128)(2,1)S(1)}, bf16[1,4,2,128,128]{4,3,2,1,0:T(8,128)(2,1)S(1)}, u32[]{:S(2)}, u32[]{:S(2)}) collective-permute-start(bf16[1,4,2,128,128]{4,3,2,1,0:T(8,128)(2,1)S(1)} %get-tuple-element.97), channel_id=1, source_target_pairs={{0,8},{1,9},{2,10},{3,11},{4,12},{5,13},{6,14},{7,15},{8,0},{9,1},... | collective-permute-start | bytes 786440 | tf_op jit(solution)/shard_map/ppermute | solution.py:20
  136.0 11.4 %collective-permute-start.11 = (bf16[1,4,2,128,128]{4,3,2,1,0:T(8,128)(2,1)S(1)}, bf16[1,4,2,128,128]{4,3,2,1,0:T(8,128)(2,1)S(1)}, u32[]{:S(2)}, u32[]{:S(2)}) collective-permute-start(bf16[1,4,2,128,128]{4,3,2,1,0:T(8,128)(2,1)S(1)} %get-tuple-element.89), channel_id=1, source_target_pairs={{0,1},{1,2},{2,3},{3,4},{4,5},{5,6},{6,7},{7,0},{8,9},{9,10},{10,1... | collective-permute-start | bytes 786440 | tf_op jit(solution)/shard_map/ppermute | solution.py:20
  136.2 11.0 %collective-permute-start.13 = (bf16[1,4,2,128,128]{4,3,2,1,0:T(8,128)(2,1)S(1)}, bf16[1,4,2,128,128]{4,3,2,1,0:T(8,128)(2,1)S(1)}, u32[]{:S(2)}, u32[]{:S(2)}) collective-permute-start(bf16[1,4,2,128,128]{4,3,2,1,0:T(8,128)(2,1)S(1)} %get-tuple-element.98), channel_id=1, source_target_pairs={{0,9},{1,10},{2,11},{3,12},{4,13},{5,14},{6,15},{7,8},{8,1},{9,2},... | collective-permute-start | bytes 786440 | tf_op jit(solution)/shard_map/ppermute | solution.py:20
  139.0 8.3 %copy-start.9 = (bf16[4,2,128,128]{3,2,1,0:T(8,128)(2,1)S(1)}, bf16[4,2,128,128]{3,2,1,0:T(8,128)(2,1)}, u32[]{:S(2)}) copy-start(bf16[4,2,128,128]{3,2,1,0:T(8,128)(2,1)} %get-tuple-element.101) | copy-start | bytes 786436
  139.1 8.3 %copy-start.5 = (bf16[4,2,128,128]{3,2,1,0:T(8,128)(2,1)S(1)}, bf16[4,2,128,128]{3,2,1,0:T(8,128)(2,1)}, u32[]{:S(2)}) copy-start(bf16[4,2,128,128]{3,2,1,0:T(8,128)(2,1)} %get-tuple-element.102) | copy-start | bytes 786436
  142.4 5.2 %copy-start.8 = (bf16[4,2,128,128]{3,2,1,0:T(8,128)(2,1)S(1)}, bf16[4,2,128,128]{3,2,1,0:T(8,128)(2,1)}, u32[]{:S(2)}) copy-start(bf16[4,2,128,128]{3,2,1,0:T(8,128)(2,1)} %get-tuple-element.92) | copy-start | bytes 786436

commit v4 on v3

--- a/solution.py
+++ b/solution.py
@@ -3,6 +3,7 @@
 from jax import lax
 from jax.experimental import pallas as pl
 from jax.experimental.pallas import tpu as pltpu
+from jax.sharding import Mesh
 from jax.sharding import PartitionSpec as P
 
 POINTS = 256
@@ -12,12 +13,12 @@
 
 
 def along_ring(value, steps, other=0):
-    half = lax.axis_size("blk") // 2
+    half = lax.axis_size("plane")
     pairs = []
     for b in range(2 * half):
         column, plane = b // half, b % half
         pairs.append((b, (column + other) % 2 * half + (plane + steps) % half))
-    return lax.ppermute(value, "blk", pairs)
+    return lax.ppermute(value, ("column", "plane"), pairs)
 
 
 def to_twin(value):
@@ -37,7 +38,7 @@
         2.0 * jnp.pi / POINTS
     )
     waves = jnp.stack([jnp.cos(angles), -jnp.sin(angles)], axis=0)
-    waves = waves.reshape(2, freq_size, 2, -1, POINTS).transpose(2, 1, 0, 3, 4)
+    waves = waves.reshape(2, freq_size, 2, -1, POINTS).transpose(1, 2, 0, 3, 4)
     return (window * waves.reshape(1, -1, POINTS)).astype(jnp.bfloat16)
 
 
@@ -97,19 +98,24 @@
 
 def body(samples, chan_list):
     freq_size = lax.axis_size("freq")
-    half = lax.axis_size("blk") // 2
-    column, plane = lax.axis_index("blk") // half, lax.axis_index("blk") % half
+    half = lax.axis_size("plane")
+    column, plane = lax.axis_index("column"), lax.axis_index("plane")
     inputs = samples.shape[1]
     tile = freq_size * inputs
     frames = samples.reshape(inputs, samples.shape[2] // POINTS, POINTS)
     chans = CHANNELS // freq_size // 2
     voltages = channelize(frames, filter_table(chan_list, freq_size))
-    voltages = voltages.reshape(2, freq_size, 2, 1, chans, inputs, SPECTRA)
+    voltages = voltages.reshape(2 * freq_size, 2, chans, inputs, SPECTRA)
 
-    kept = lax.dynamic_index_in_dim(voltages, column, 0, keepdims=False)
-    given = lax.dynamic_index_in_dim(voltages, 1 - column, 0, keepdims=False)
-    pair = jnp.concatenate([kept, to_twin(given)], axis=2)
-    pair = lax.all_to_all(pair, "freq", split_axis=0, concat_axis=4, tiled=True)
+    pair = lax.all_to_all(voltages, ("freq", "column"), split_axis=0, concat_axis=0, tiled=True)
+    pair = pair.reshape(freq_size, 2, 2, chans, inputs, SPECTRA)
+    pair = jnp.stack(
+        [
+            lax.dynamic_index_in_dim(pair, side, 1, keepdims=False).transpose(1, 2, 0, 3, 4)
+            for side in (column, 1 - column)
+        ],
+        axis=1,
+    )
 
     blocks, tiles = {0: pair.reshape(2, 2, chans, tile, SPECTRA)}, {}
 
@@ -162,6 +168,11 @@
 
 
 def solution(mesh):
-    in_specs = (P("blk", "freq", None), P())
-    out_specs = P("freq", "blk", None, None, None, None)
-    return jax.shard_map(body, mesh=mesh, in_specs=in_specs, out_specs=out_specs, check_vma=False)
+    freq_size, blk_size = mesh.devices.shape
+    planes = Mesh(
+        mesh.devices.reshape(freq_size, 2, blk_size // 2), ("freq", "column", "plane")
+    )
+    blk = ("column", "plane")
+    in_specs = (P(blk, "freq", None), P())
+    out_specs = P("freq", blk, None, None, None, None)
+    return jax.shard_map(body, mesh=planes, in_specs=in_specs, out_specs=out_specs, check_vma=False)

time: 152 us -> 139 us (0.914); the launches traced: 152 us -> 137 us
  blocking collectives: 19.2 us -> 0 us
  waiting for transfers between devices: 62.3 us -> 65.1 us
    all_to_all x1 -> x0, blocking collectives: 19.2 us -> none  [body(): pair = lax.all_to_all(pair, 'freq', split_axis=0, concat_axis=4, tiled=True)]
    all_to_all x0 -> x1, waiting for transfers between devices: none -> 15.8 us  [body(): lax.all_to_all(voltages, ('freq', 'column'), split_axis=0, concat_axis=0,...]
    ppermute x14 -> x13, waiting for transfers between devices: 62.3 us -> 49.3 us  [along_ring(): return lax.ppermute(value, ('column', 'plane'), pairs)]
    all_to_all x0 -> x1, starting transfers between devices: none -> 7.56 us  [body(): lax.all_to_all(voltages, ('freq', 'column'), split_axis=0, concat_axis=0,...]
    ppermute x14 -> x13, starting transfers between devices: 32.3 us -> 25.9 us  [along_ring(): return lax.ppermute(value, ('column', 'plane'), pairs)]
  transfers between devices with their start and end apart: 14 -> 14, of which waited for: 9 -> 9; matrix products, arithmetic and copies ran while one was open for 3% -> 4% of each run, Pallas kernels for 11% -> 12%
where the time goes in v4:
time: 139 us; the launch traced here: 137 us
  waiting for transfers between devices  65.1 us (47%)
  starting transfers between devices  33.5 us (24%)
  Pallas kernels  17.4 us (13%)
  local copies, waits for them, and re-layouts  12.1 us (9%)
  matrix products  4.59 us (3%)
  other arithmetic  3.19 us (2%)
    ppermute x13, waiting for transfers between devices, along_ring(): return lax.ppermute(value, ('column', 'plane'), pairs)  49.3 us
    ppermute x13, starting transfers between devices, along_ring(): return lax.ppermute(value, ('column', 'plane'), pairs)  25.9 us
    pallas_call x6, Pallas kernels, visibilities(): pl.pallas_call(visibility_kernel, grid_spec=pltpu.PrefetchScalarGridSpec(...  17.4 us
    all_to_all x1, waiting for transfers between devices, body(): lax.all_to_all(voltages, ('freq', 'column'), split_axis=0, concat_axis=0,...  15.8 us
    all_to_all x1, starting transfers between devices, body(): lax.all_to_all(voltages, ('freq', 'column'), split_axis=0, concat_axis=0,...  7.56 us
    conv_general_dilated x1, matrix products, channelize(): lax.conv_general_dilated(frames, filters, window_strides=(1,), padding='V...  4.59 us
    squeeze x6, local copies, waits for them, and re-layouts, near(): tiles[half if at == half else -at % half] = (mine[index], moved[index])  4.39 us
    broadcast_in_dim x1, local copies, waits for them, and re-layouts, body(): return jnp.concatenate([low, high], axis=0)[:, None]  3.15 us
  transfers between devices with their start and end apart: 14, of which 9 were waited for; matrix products, arithmetic and copies ran while one was open for 4% of the time, Pallas kernels for 12%

profile of v4, /device:TPU:6, one launch (start us, length us, event | category | flops | bytes accessed | tf_op | source)
XLA Modules:
  0.0 137.0 jit_solution(15024792671499001219)
XLA Ops:
  0.0 0.0 copy-start
  0.0 0.7 fusion.17
  1.4 0.1 fusion.9
  1.6 0.8 mul.110
  2.3 1.2 fusion.7
  3.6 0.1 maximum_bitcast_fusion.1
  3.6 0.1 mul.116
  3.7 0.0 copy-done
  3.7 4.6 %fusion.3 = bf16[256,8,256]{0,1,2:T(8,128)(2,1)S(1)} fusion(bf16[8,271,256]{2,0,1:T(8,128)(2,1)S(1)} %bitcast.90, f32[256,256]{1,0:T(8,128)S(1)} %mul.116, f32[16,256]{1,0:T(8,128)S(1)} %fusion.9), kind=kOutput, calls=%fused_computation.7 | convolution fusion | flops 4297588736 | bytes 2437120 | tf_op jit(solution)/shard_map/conv_general_dilated | solution.py:46
  8.3 2.0 %copy.6 = bf16[256,8,256]{2,1,0:T(8,128)(2,1)} copy(bf16[256,8,256]{0,1,2:T(8,128)(2,1)S(1)} %fusion.3) | data formatting | bytes 2097152 | tf_op jit(solution)/shard_map/convert_element_type | solution.py:53
  10.4 7.6 %all-to-all-start = ((bf16[32,2,4,8,256]{4,3,2,1,0:T(8,128)(2,1)}), bf16[32,2,4,8,256]{4,3,2,1,0:T(8,128)(2,1)S(1)}, u32[]{:S(2)}, u32[]{:S(2)}) async-start(bf16[32,2,4,8,256]{4,3,2,1,0:T(8,128)(2,1)} %bitcast.3), calls=%async_computation | async-start | bytes 2097152 | tf_op jit(solution)/shard_map/all_to_all | solution.py:110
  18.0 15.8 %all-to-all-done = bf16[32,2,4,8,256]{4,3,2,1,0:T(8,128)(2,1)S(1)} async-done(((bf16[32,2,4,8,256]{4,3,2,1,0:T(8,128)(2,1)}), bf16[32,2,4,8,256]{4,3,2,1,0:T(8,128)(2,1)S(1)}, u32[]{:S(2)}, u32[]{:S(2)}) %all-to-all-start) | async-done | bytes 1048608 | tf_op jit(solution)/shard_map/all_to_all | solution.py:110
  33.8 0.1 constant_dynamic-slice_fusion.1
  33.9 0.1 copy_bitcast_fusion
  34.0 0.1 pad_maximum_fusion.own.refs_0_.refs_1_
  34.1 5.9 %collective-permute-start.2 = (bf16[2,2,4,128,256]{4,3,2,1,0:T(8,128)(2,1)S(1)}, bf16[2,2,4,128,256]{4,3,2,1,0:T(8,128)(2,1)S(1)}, u32[]{:S(2)}, u32[]{:S(2)}) collective-permute-start(bf16[2,2,4,128,256]{4,3,2,1,0:T(8,128)(2,1)S(1)} %pad_maximum_fusion.own.refs_0_.refs_1_), channel_id=1, source_target_pairs={{0,7},{1,0},{2,1},{3,2},{4,3},{5,4},{6,5},{7,6},{8,15},{9,8},{10,9... | collective-permute-start | bytes 3145736 | tf_op jit(solution)/shard_map/ppermute | solution.py:21
  40.1 0.0 collective-permute-start.1
  40.1 0.1 add_convert_fusion.swaps
  40.1 2.6 %shard_map.28 = (bf16[2,4,2,128,128]{4,3,2,1,0:T(8,128)(2,1)S(1)}, bf16[2,4,2,128,128]{4,3,2,1,0:T(8,128)(2,1)S(1)}) custom-call(s32[2]{0:T(128)S(1)} %add_convert_fusion.swaps, bf16[2,2,4,128,256]{4,3,2,1,0:T(8,128)(2,1)S(1)} %pad_maximum_fusion.own.refs_0_.refs_1_, bf16[2,2,4,128,256]{4,3,2,1,0:T(8,128)(2,1)S(1)} %pad_maximum_fusion.own.refs_0_.refs_1_, ...), custom_call_target="tpu_custom_call" | custom-call | tf_op jit(solution)/shard_map/pallas_call | solution.py:86
  42.8 1.0 collective-permute-start
  43.8 0.9 slice_bitcast_fusion.10
  44.7 12.7 %collective-permute-done = bf16[2,4,2,128,128]{4,3,2,1,0:T(8,128)(2,1)S(1)} collective-permute-done((bf16[2,4,2,128,128]{4,3,2,1,0:T(8,128)(2,1)S(1)}, bf16[2,4,2,128,128]{4,3,2,1,0:T(8,128)(2,1)S(1)}, u32[]{:S(2)}, u32[]{:S(2)}) %collective-permute-start) | collective-permute-done | bytes 524320 | tf_op jit(solution)/shard_map/ppermute | solution.py:21
  57.3 0.7 slice_bitcast_fusion.4
  58.1 4.0 %collective-permute-done.2.refs_1_.own = bf16[2,2,4,128,256]{4,3,2,1,0:T(8,128)(2,1)S(1)} collective-permute-done((bf16[2,2,4,128,256]{4,3,2,1,0:T(8,128)(2,1)S(1)}, bf16[2,2,4,128,256]{4,3,2,1,0:T(8,128)(2,1)S(1)}, u32[]{:S(2)}, u32[]{:S(2)}) %collective-permute-start.2) | collective-permute-done | bytes 1048608 | tf_op jit(solution)/shard_map/ppermute | solution.py:21
  62.0 3.5 %collective-permute-done.1.refs_0_.own = bf16[2,2,4,128,256]{4,3,2,1,0:T(8,128)(2,1)} collective-permute-done((bf16[2,2,4,128,256]{4,3,2,1,0:T(8,128)(2,1)S(1)}, bf16[2,2,4,128,256]{4,3,2,1,0:T(8,128)(2,1)}, u32[]{:S(2)}, u32[]{:S(2)}) %collective-permute-start.1) | collective-permute-done | bytes 1048608 | tf_op jit(solution)/shard_map/ppermute | solution.py:21
  65.6 0.0 collective-permute-start.4
  65.6 3.2 %collective-permute-start.5 = (bf16[2,2,4,128,256]{4,3,2,1,0:T(8,128)(2,1)S(1)}, bf16[2,2,4,128,256]{4,3,2,1,0:T(8,128)(2,1)}, u32[]{:S(2)}, u32[]{:S(2)}) collective-permute-start(bf16[2,2,4,128,256]{4,3,2,1,0:T(8,128)(2,1)S(1)} %collective-permute-done.2.refs_1_.own), channel_id=1, source_target_pairs={{0,7},{1,0},{2,1},{3,2},{4,3},{5,4},{6,5},{7,6},{8,15},{9,8},{10,9... | collective-permute-start | bytes 3145736 | tf_op jit(solution)/shard_map/ppermute | solution.py:21
  68.8 0.1 add_convert_fusion.1.swaps
  68.9 3.9 %shard_map.29 = (bf16[2,4,2,128,128]{4,3,2,1,0:T(8,128)(2,1)S(1)}, bf16[2,4,2,128,128]{4,3,2,1,0:T(8,128)(2,1)S(1)}) custom-call(s32[2]{0:T(128)S(1)} %add_convert_fusion.1.swaps, bf16[2,2,4,128,256]{4,3,2,1,0:T(8,128)(2,1)S(1)} %pad_maximum_fusion.own.refs_0_.refs_1_, bf16[2,2,4,128,256]{4,3,2,1,0:T(8,128)(2,1)} %collective-permute-done.1.refs_0_.own, ...), custom_call_target="tpu_custom_call" | custom-call | tf_op jit(solution)/shard_map/pallas_call | solution.py:86
  72.8 1.8 %collective-permute-start.3 = (bf16[2,4,2,128,128]{4,3,2,1,0:T(8,128)(2,1)S(1)}, bf16[2,4,2,128,128]{4,3,2,1,0:T(8,128)(2,1)S(1)}, u32[]{:S(2)}, u32[]{:S(2)}) collective-permute-start(bf16[2,4,2,128,128]{4,3,2,1,0:T(8,128)(2,1)S(1)} %get-tuple-element.62), channel_id=1, source_target_pairs={{0,8},{1,9},{2,10},{3,11},{4,12},{5,13},{6,14},{7,15},{8,0},{9,1},... | collective-permute-start | bytes 1572872 | tf_op jit(solution)/shard_map/ppermute | solution.py:21
  74.7 0.8 slice_bitcast_fusion.8
  75.5 10.4 %collective-permute-done.3 = bf16[2,4,2,128,128]{4,3,2,1,0:T(8,128)(2,1)S(1)} collective-permute-done((bf16[2,4,2,128,128]{4,3,2,1,0:T(8,128)(2,1)S(1)}, bf16[2,4,2,128,128]{4,3,2,1,0:T(8,128)(2,1)S(1)}, u32[]{:S(2)}, u32[]{:S(2)}) %collective-permute-start.3) | collective-permute-done | bytes 524320 | tf_op jit(solution)/shard_map/ppermute | solution.py:21
  85.9 0.8 slice_bitcast_fusion.2
  86.7 0.0 copy-done.1
  86.7 3.6 %collective-permute-done.4.refs_0_ = bf16[2,2,4,128,256]{4,3,2,1,0:T(8,128)(2,1)} collective-permute-done((bf16[2,2,4,128,256]{4,3,2,1,0:T(8,128)(2,1)}, bf16[2,2,4,128,256]{4,3,2,1,0:T(8,128)(2,1)}, u32[]{:S(2)}, u32[]{:S(2)}) %collective-permute-start.4) | collective-permute-done | bytes 1048608 | tf_op jit(solution)/shard_map/ppermute | solution.py:21
  90.4 0.0 collective-permute-done.5.refs_1_.refs_0_
  90.4 0.0 collective-permute-start.9
  90.4 0.1 add_convert_fusion.2.swaps
  90.4 4.9 %shard_map.30 = (bf16[2,4,2,128,128]{4,3,2,1,0:T(8,128)(2,1)S(1)}, bf16[2,4,2,128,128]{4,3,2,1,0:T(8,128)(2,1)}) custom-call(s32[2]{0:T(128)S(1)} %add_convert_fusion.2.swaps, bf16[2,2,4,128,256]{4,3,2,1,0:T(8,128)(2,1)S(1)} %pad_maximum_fusion.own.refs_0_.refs_1_, bf16[2,2,4,128,256]{4,3,2,1,0:T(8,128)(2,1)} %collective-permute-done.4.refs_0_, ...), custom_call_target="tpu_custom_call" | custom-call | tf_op jit(solution)/shard_map/pallas_call | solution.py:86
  95.3 0.8 copy-done.3
  96.1 2.6 %collective-permute-start.6 = (bf16[2,4,2,128,128]{4,3,2,1,0:T(8,128)(2,1)}, bf16[2,4,2,128,128]{4,3,2,1,0:T(8,128)(2,1)}, u32[]{:S(2)}, u32[]{:S(2)}) collective-permute-start(bf16[2,4,2,128,128]{4,3,2,1,0:T(8,128)(2,1)} %get-tuple-element.73), channel_id=1, source_target_pairs={{0,8},{1,9},{2,10},{3,11},{4,12},{5,13},{6,14},{7,15},{8,0},{9,1},... | collective-permute-start | bytes 1572872 | tf_op jit(solution)/shard_map/ppermute | solution.py:21
  98.8 3.1 %shard_map.31 = (bf16[1,4,2,128,128]{4,3,2,1,0:T(8,128)(2,1)S(1)}, bf16[1,4,2,128,128]{4,3,2,1,0:T(8,128)(2,1)S(1)}) custom-call(s32[1]{0:T(128)} %bitcast.25.swaps, bf16[2,2,4,128,256]{4,3,2,1,0:T(8,128)(2,1)} %collective-permute-done.1.refs_0_.own, bf16[2,2,4,128,256]{4,3,2,1,0:T(8,128)(2,1)} %collective-permute-done.5.refs_1_.refs_0_), custom_call_target="tpu_custom_call" | custom-call | tf_op jit(solution)/shard_map/pallas_call | solution.py:86
  101.9 0.0 copy-start.2
  101.9 3.3 %collective-permute-start.7 = (bf16[1,4,2,128,128]{4,3,2,1,0:T(8,128)(2,1)S(1)}, bf16[1,4,2,128,128]{4,3,2,1,0:T(8,128)(2,1)S(1)}, u32[]{:S(2)}, u32[]{:S(2)}) collective-permute-start(bf16[1,4,2,128,128]{4,3,2,1,0:T(8,128)(2,1)S(1)} %get-tuple-element.75), channel_id=1, source_target_pairs={{0,7},{1,0},{2,1},{3,2},{4,3},{5,4},{6,5},{7,6},{8,15},{9,8},{10,9... | collective-permute-start | bytes 786440 | tf_op jit(solution)/shard_map/ppermute | solution.py:21
  105.2 1.9 %collective-permute-start.8 = (bf16[1,4,2,128,128]{4,3,2,1,0:T(8,128)(2,1)S(1)}, bf16[1,4,2,128,128]{4,3,2,1,0:T(8,128)(2,1)S(1)}, u32[]{:S(2)}, u32[]{:S(2)}) collective-permute-start(bf16[1,4,2,128,128]{4,3,2,1,0:T(8,128)(2,1)S(1)} %get-tuple-element.76), channel_id=1, source_target_pairs={{0,15},{1,8},{2,9},{3,10},{4,11},{5,12},{6,13},{7,14},{8,7},{9,0},... | collective-permute-start | bytes 786440 | tf_op jit(solution)/shard_map/ppermute | solution.py:21
  107.1 7.8 %collective-permute-done.6 = bf16[2,4,2,128,128]{4,3,2,1,0:T(8,128)(2,1)} collective-permute-done((bf16[2,4,2,128,128]{4,3,2,1,0:T(8,128)(2,1)}, bf16[2,4,2,128,128]{4,3,2,1,0:T(8,128)(2,1)}, u32[]{:S(2)}, u32[]{:S(2)}) %collective-permute-start.6) | collective-permute-done | bytes 524320 | tf_op jit(solution)/shard_map/ppermute | solution.py:21
  114.9 1.1 slice_bitcast_fusion
  116.0 0.0 collective-permute-done.7
  116.0 0.0 collective-permute-done.8
  116.0 0.0 collective-permute-done.9.refs_0_
  116.1 1.4 %shard_map.32 = (bf16[1,4,2,128,128]{4,3,2,1,0:T(8,128)(2,1)S(1)}, bf16[1,4,2,128,128]{4,3,2,1,0:T(8,128)(2,1)S(1)}) custom-call(s32[1]{0:T(128)} %bitcast.33.swaps, bf16[2,2,4,128,256]{4,3,2,1,0:T(8,128)(2,1)S(1)} %pad_maximum_fusion.own.refs_0_.refs_1_, bf16[2,2,4,128,256]{4,3,2,1,0:T(8,128)(2,1)S(1)} %collective-permute-done.9.refs_0_), custom_call_target="tpu_custom_call" | custom-call | tf_op jit(solution)/shard_map/pallas_call | solution.py:86
  117.5 3.3 %collective-permute-start.11 = (bf16[1,4,2,128,128]{4,3,2,1,0:T(8,128)(2,1)S(1)}, bf16[1,4,2,128,128]{4,3,2,1,0:T(8,128)(2,1)S(1)}, u32[]{:S(2)}, u32[]{:S(2)}) collective-permute-start(bf16[1,4,2,128,128]{4,3,2,1,0:T(8,128)(2,1)S(1)} %get-tuple-element.97), channel_id=1, source_target_pairs={{0,8},{1,9},{2,10},{3,11},{4,12},{5,13},{6,14},{7,15},{8,0},{9,1},... | collective-permute-start | bytes 786440 | tf_op jit(solution)/shard_map/ppermute | solution.py:21
  120.8 1.4 %shard_map.33 = (bf16[1,4,2,128,128]{4,3,2,1,0:T(8,128)(2,1)S(1)}, bf16[1,4,2,128,128]{4,3,2,1,0:T(8,128)(2,1)S(1)}) custom-call(s32[1]{0:T(128)} %bitcast.35.swaps, bf16[2,2,4,128,256]{4,3,2,1,0:T(8,128)(2,1)S(1)} %copy-done.2, bf16[2,2,4,128,256]{4,3,2,1,0:T(8,128)(2,1)S(1)} %collective-permute-done.9.refs_0_), custom_call_target="tpu_custom_call" | custom-call | tf_op jit(solution)/shard_map/pallas_call | solution.py:86
  122.3 0.4 collective-permute-start.10
  122.6 2.4 %collective-permute-start.12 = (bf16[1,4,2,128,128]{4,3,2,1,0:T(8,128)(2,1)S(1)}, bf16[1,4,2,128,128]{4,3,2,1,0:T(8,128)(2,1)S(1)}, u32[]{:S(2)}, u32[]{:S(2)}) collective-permute-start(bf16[1,4,2,128,128]{4,3,2,1,0:T(8,128)(2,1)S(1)} %get-tuple-element.98), channel_id=1, source_target_pairs={{0,9},{1,10},{2,11},{3,12},{4,13},{5,14},{6,15},{7,8},{8,1},{9,2},... | collective-permute-start | bytes 786440 | tf_op jit(solution)/shard_map/ppermute | solution.py:21
  125.1 0.0 copy-done.11
  125.1 0.0 copy-start.5
  125.3 4.6 %collective-permute-done.10 = bf16[1,4,2,128,128]{4,3,2,1,0:T(8,128)(2,1)S(1)} collective-permute-done((bf16[1,4,2,128,128]{4,3,2,1,0:T(8,128)(2,1)S(1)}, bf16[1,4,2,128,128]{4,3,2,1,0:T(8,128)(2,1)S(1)}, u32[]{:S(2)}, u32[]{:S(2)}) %collective-permute-start.10) | collective-permute-done | bytes 262176 | tf_op jit(solution)/shard_map/ppermute | solution.py:21
  130.0 0.0 copy-done.9
  130.2 0.0 collective-permute-done.11
  130.2 2.7 %collective-permute-done.12 = bf16[1,4,2,128,128]{4,3,2,1,0:T(8,128)(2,1)S(1)} collective-permute-done((bf16[1,4,2,128,128]{4,3,2,1,0:T(8,128)(2,1)S(1)}, bf16[1,4,2,128,128]{4,3,2,1,0:T(8,128)(2,1)S(1)}, u32[]{:S(2)}, u32[]{:S(2)}) %collective-permute-start.12) | collective-permute-done | bytes 262176 | tf_op jit(solution)/shard_map/ppermute | solution.py:21
  133.2 0.3 broadcast_select_fusion.1
  133.5 0.4 maximum_bitcast_fusion
  133.9 3.1 %copy.9 = bf16[8,1,9,2,128,128]{5,4,3,2,1,0:T(8,128)(2,1)} copy(bf16[8,1,9,2,128,128]{5,4,3,0,2,1:T(8,128)(2,1)S(1)} %maximum_bitcast_fusion) | data formatting | bytes 9437184 | tf_op jit(solution)/shard_map/broadcast_in_dim | solution.py:167
  (35 shorter events, 0.7 us)
Async XLA Ops:
  0.0 3.7 %copy-start = (bf16[1,8,69376]{2,1,0:T(8,128)(2,1)S(1)}, bf16[1,8,69376]{2,1,0:T(8,128)(2,1)}, u32[]{:S(2)}) copy-start(bf16[1,8,69376]{2,1,0:T(8,128)(2,1)} %param.2) | copy-start | bytes 3330052
  10.4 23.4 %all-to-all-start = ((bf16[32,2,4,8,256]{4,3,2,1,0:T(8,128)(2,1)}), bf16[32,2,4,8,256]{4,3,2,1,0:T(8,128)(2,1)S(1)}, u32[]{:S(2)}, u32[]{:S(2)}) async-start(bf16[32,2,4,8,256]{4,3,2,1,0:T(8,128)(2,1)} %bitcast.3), calls=%async_computation | async-start | bytes 2097152 | tf_op jit(solution)/shard_map/all_to_all | solution.py:110
  34.1 27.9 %collective-permute-start.2 = (bf16[2,2,4,128,256]{4,3,2,1,0:T(8,128)(2,1)S(1)}, bf16[2,2,4,128,256]{4,3,2,1,0:T(8,128)(2,1)S(1)}, u32[]{:S(2)}, u32[]{:S(2)}) collective-permute-start(bf16[2,2,4,128,256]{4,3,2,1,0:T(8,128)(2,1)S(1)} %pad_maximum_fusion.own.refs_0_.refs_1_), channel_id=1, source_target_pairs={{0,7},{1,0},{2,1},{3,2},{4,3},{5,4},{6,5},{7,6},{8,15},{9,8},{10,9... | collective-permute-start | bytes 3145736 | tf_op jit(solution)/shard_map/ppermute | solution.py:21
  40.1 25.5 %collective-permute-start.1 = (bf16[2,2,4,128,256]{4,3,2,1,0:T(8,128)(2,1)S(1)}, bf16[2,2,4,128,256]{4,3,2,1,0:T(8,128)(2,1)}, u32[]{:S(2)}, u32[]{:S(2)}) collective-permute-start(bf16[2,2,4,128,256]{4,3,2,1,0:T(8,128)(2,1)S(1)} %pad_maximum_fusion.own.refs_0_.refs_1_), channel_id=1, source_target_pairs={{0,1},{1,2},{2,3},{3,4},{4,5},{5,6},{6,7},{7,0},{8,9},{9,10},{10,1... | collective-permute-start | bytes 3145736 | tf_op jit(solution)/shard_map/ppermute | solution.py:21
  42.8 14.5 %collective-permute-start = (bf16[2,4,2,128,128]{4,3,2,1,0:T(8,128)(2,1)S(1)}, bf16[2,4,2,128,128]{4,3,2,1,0:T(8,128)(2,1)S(1)}, u32[]{:S(2)}, u32[]{:S(2)}) collective-permute-start(bf16[2,4,2,128,128]{4,3,2,1,0:T(8,128)(2,1)S(1)} %get-tuple-element.55), channel_id=1, source_target_pairs={{0,8},{1,9},{2,10},{3,11},{4,12},{5,13},{6,14},{7,15},{8,0},{9,1},... | collective-permute-start | bytes 1572872 | tf_op jit(solution)/shard_map/ppermute | solution.py:21
  62.0 24.7 %copy-start.1 = (bf16[2,2,4,128,256]{4,3,2,1,0:T(8,128)(2,1)}, bf16[2,2,4,128,256]{4,3,2,1,0:T(8,128)(2,1)S(1)}, u32[]{:S(2)}) copy-start(bf16[2,2,4,128,256]{4,3,2,1,0:T(8,128)(2,1)S(1)} %collective-permute-done.2.refs_1_.own) | copy-start | bytes 3145732
  65.6 24.8 %collective-permute-start.4 = (bf16[2,2,4,128,256]{4,3,2,1,0:T(8,128)(2,1)}, bf16[2,2,4,128,256]{4,3,2,1,0:T(8,128)(2,1)}, u32[]{:S(2)}, u32[]{:S(2)}) collective-permute-start(bf16[2,2,4,128,256]{4,3,2,1,0:T(8,128)(2,1)} %collective-permute-done.1.refs_0_.own), channel_id=1, source_target_pairs={{0,1},{1,2},{2,3},{3,4},{4,5},{5,6},{6,7},{7,0},{8,9},{9,10},{10,1... | collective-permute-start | bytes 3145736 | tf_op jit(solution)/shard_map/ppermute | solution.py:21
  65.6 24.8 %collective-permute-start.5 = (bf16[2,2,4,128,256]{4,3,2,1,0:T(8,128)(2,1)S(1)}, bf16[2,2,4,128,256]{4,3,2,1,0:T(8,128)(2,1)}, u32[]{:S(2)}, u32[]{:S(2)}) collective-permute-start(bf16[2,2,4,128,256]{4,3,2,1,0:T(8,128)(2,1)S(1)} %collective-permute-done.2.refs_1_.own), channel_id=1, source_target_pairs={{0,7},{1,0},{2,1},{3,2},{4,3},{5,4},{6,5},{7,6},{8,15},{9,8},{10,9... | collective-permute-start | bytes 3145736 | tf_op jit(solution)/shard_map/ppermute | solution.py:21
  72.8 13.1 %collective-permute-start.3 = (bf16[2,4,2,128,128]{4,3,2,1,0:T(8,128)(2,1)S(1)}, bf16[2,4,2,128,128]{4,3,2,1,0:T(8,128)(2,1)S(1)}, u32[]{:S(2)}, u32[]{:S(2)}) collective-permute-start(bf16[2,4,2,128,128]{4,3,2,1,0:T(8,128)(2,1)S(1)} %get-tuple-element.62), channel_id=1, source_target_pairs={{0,8},{1,9},{2,10},{3,11},{4,12},{5,13},{6,14},{7,15},{8,0},{9,1},... | collective-permute-start | bytes 1572872 | tf_op jit(solution)/shard_map/ppermute | solution.py:21
  90.4 25.7 %collective-permute-start.9 = (bf16[2,2,4,128,256]{4,3,2,1,0:T(8,128)(2,1)}, bf16[2,2,4,128,256]{4,3,2,1,0:T(8,128)(2,1)S(1)}, u32[]{:S(2)}, u32[]{:S(2)}) collective-permute-start(bf16[2,2,4,128,256]{4,3,2,1,0:T(8,128)(2,1)} %collective-permute-done.4.refs_0_), channel_id=1, source_target_pairs={{0,1},{1,2},{2,3},{3,4},{4,5},{5,6},{6,7},{7,0},{8,9},{9,10},{10,1... | collective-permute-start | bytes 3145736 | tf_op jit(solution)/shard_map/ppermute | solution.py:21
  95.3 0.8 copy-start.3
  96.1 18.8 %collective-permute-start.6 = (bf16[2,4,2,128,128]{4,3,2,1,0:T(8,128)(2,1)}, bf16[2,4,2,128,128]{4,3,2,1,0:T(8,128)(2,1)}, u32[]{:S(2)}, u32[]{:S(2)}) collective-permute-start(bf16[2,4,2,128,128]{4,3,2,1,0:T(8,128)(2,1)} %get-tuple-element.73), channel_id=1, source_target_pairs={{0,8},{1,9},{2,10},{3,11},{4,12},{5,13},{6,14},{7,15},{8,0},{9,1},... | collective-permute-start | bytes 1572872 | tf_op jit(solution)/shard_map/ppermute | solution.py:21
  98.8 8.3 %copy-start.4 = (bf16[2,4,2,128,128]{4,3,2,1,0:T(8,128)(2,1)S(1)}, bf16[2,4,2,128,128]{4,3,2,1,0:T(8,128)(2,1)}, u32[]{:S(2)}) copy-start(bf16[2,4,2,128,128]{4,3,2,1,0:T(8,128)(2,1)} %copy-done.3) | copy-start | bytes 1572868
  101.9 19.0 %copy-start.2 = (bf16[2,2,4,128,256]{4,3,2,1,0:T(8,128)(2,1)S(1)}, bf16[2,2,4,128,256]{4,3,2,1,0:T(8,128)(2,1)}, u32[]{:S(2)}) copy-start(bf16[2,2,4,128,256]{4,3,2,1,0:T(8,128)(2,1)} %copy-done.1) | copy-start | bytes 3145732
  101.9 14.1 %collective-permute-start.7 = (bf16[1,4,2,128,128]{4,3,2,1,0:T(8,128)(2,1)S(1)}, bf16[1,4,2,128,128]{4,3,2,1,0:T(8,128)(2,1)S(1)}, u32[]{:S(2)}, u32[]{:S(2)}) collective-permute-start(bf16[1,4,2,128,128]{4,3,2,1,0:T(8,128)(2,1)S(1)} %get-tuple-element.75), channel_id=1, source_target_pairs={{0,7},{1,0},{2,1},{3,2},{4,3},{5,4},{6,5},{7,6},{8,15},{9,8},{10,9... | collective-permute-start | bytes 786440 | tf_op jit(solution)/shard_map/ppermute | solution.py:21
  105.2 10.8 %collective-permute-start.8 = (bf16[1,4,2,128,128]{4,3,2,1,0:T(8,128)(2,1)S(1)}, bf16[1,4,2,128,128]{4,3,2,1,0:T(8,128)(2,1)S(1)}, u32[]{:S(2)}, u32[]{:S(2)}) collective-permute-start(bf16[1,4,2,128,128]{4,3,2,1,0:T(8,128)(2,1)S(1)} %get-tuple-element.76), channel_id=1, source_target_pairs={{0,15},{1,8},{2,9},{3,10},{4,11},{5,12},{6,13},{7,14},{8,7},{9,0},... | collective-permute-start | bytes 786440 | tf_op jit(solution)/shard_map/ppermute | solution.py:21
  116.0 9.0 %copy-start.6 = (bf16[4,2,128,128]{3,2,1,0:T(8,128)(2,1)S(1)}, bf16[4,2,128,128]{3,2,1,0:T(8,128)(2,1)}, u32[]{:S(2)}) copy-start(bf16[4,2,128,128]{3,2,1,0:T(8,128)(2,1)} %get-tuple-element.82) | copy-start | bytes 786436
  116.1 9.0 %copy-start.7 = (bf16[4,2,128,128]{3,2,1,0:T(8,128)(2,1)S(1)}, bf16[4,2,128,128]{3,2,1,0:T(8,128)(2,1)}, u32[]{:S(2)}) copy-start(bf16[4,2,128,128]{3,2,1,0:T(8,128)(2,1)} %get-tuple-element.94) | copy-start | bytes 786436
  116.1 9.0 %copy-start.11 = (bf16[4,2,128,128]{3,2,1,0:T(8,128)(2,1)S(1)}, bf16[4,2,128,128]{3,2,1,0:T(8,128)(2,1)}, u32[]{:S(2)}) copy-start(bf16[4,2,128,128]{3,2,1,0:T(8,128)(2,1)} %get-tuple-element.83) | copy-start | bytes 786436
  117.5 12.7 %collective-permute-start.11 = (bf16[1,4,2,128,128]{4,3,2,1,0:T(8,128)(2,1)S(1)}, bf16[1,4,2,128,128]{4,3,2,1,0:T(8,128)(2,1)S(1)}, u32[]{:S(2)}, u32[]{:S(2)}) collective-permute-start(bf16[1,4,2,128,128]{4,3,2,1,0:T(8,128)(2,1)S(1)} %get-tuple-element.97), channel_id=1, source_target_pairs={{0,8},{1,9},{2,10},{3,11},{4,12},{5,13},{6,14},{7,15},{8,0},{9,1},... | collective-permute-start | bytes 786440 | tf_op jit(solution)/shard_map/ppermute | solution.py:21
  120.8 4.4 %copy-start.10 = (bf16[4,2,128,128]{3,2,1,0:T(8,128)(2,1)S(1)}, bf16[4,2,128,128]{3,2,1,0:T(8,128)(2,1)}, u32[]{:S(2)}) copy-start(bf16[4,2,128,128]{3,2,1,0:T(8,128)(2,1)} %get-tuple-element.95) | copy-start | bytes 786436
  122.3 7.7 %collective-permute-start.10 = (bf16[1,4,2,128,128]{4,3,2,1,0:T(8,128)(2,1)S(1)}, bf16[1,4,2,128,128]{4,3,2,1,0:T(8,128)(2,1)S(1)}, u32[]{:S(2)}, u32[]{:S(2)}) collective-permute-start(bf16[1,4,2,128,128]{4,3,2,1,0:T(8,128)(2,1)S(1)} %get-tuple-element.89), channel_id=1, source_target_pairs={{0,1},{1,2},{2,3},{3,4},{4,5},{5,6},{6,7},{7,0},{8,9},{9,10},{10,1... | collective-permute-start | bytes 786440 | tf_op jit(solution)/shard_map/ppermute | solution.py:21
  122.6 10.3 %collective-permute-start.12 = (bf16[1,4,2,128,128]{4,3,2,1,0:T(8,128)(2,1)S(1)}, bf16[1,4,2,128,128]{4,3,2,1,0:T(8,128)(2,1)S(1)}, u32[]{:S(2)}, u32[]{:S(2)}) collective-permute-start(bf16[1,4,2,128,128]{4,3,2,1,0:T(8,128)(2,1)S(1)} %get-tuple-element.98), channel_id=1, source_target_pairs={{0,9},{1,10},{2,11},{3,12},{4,13},{5,14},{6,15},{7,8},{8,1},{9,2},... | collective-permute-start | bytes 786440 | tf_op jit(solution)/shard_map/ppermute | solution.py:21
  125.1 5.0 %copy-start.9 = (bf16[4,2,128,128]{3,2,1,0:T(8,128)(2,1)S(1)}, bf16[4,2,128,128]{3,2,1,0:T(8,128)(2,1)}, u32[]{:S(2)}) copy-start(bf16[4,2,128,128]{3,2,1,0:T(8,128)(2,1)} %get-tuple-element.92) | copy-start | bytes 786436
  125.1 5.0 %copy-start.5 = (bf16[4,2,128,128]{3,2,1,0:T(8,128)(2,1)S(1)}, bf16[4,2,128,128]{3,2,1,0:T(8,128)(2,1)}, u32[]{:S(2)}) copy-start(bf16[4,2,128,128]{3,2,1,0:T(8,128)(2,1)} %get-tuple-element.93) | copy-start | bytes 786436
  125.3 7.7 %copy-start.8 = (bf16[4,2,128,128]{3,2,1,0:T(8,128)(2,1)S(1)}, bf16[4,2,128,128]{3,2,1,0:T(8,128)(2,1)}, u32[]{:S(2)}) copy-start(bf16[4,2,128,128]{3,2,1,0:T(8,128)(2,1)} %get-tuple-element.101) | copy-start | bytes 786436

commit v5 on v4

--- a/solution.py
+++ b/solution.py
@@ -55,45 +55,86 @@
 
 def visibility_kernel(swaps, own, *refs):
     partners, (kept, given) = refs[:-2], refs[-2:]
-    for block in range(2):
-        real, imag = own[0, block, 0], own[1, block, 0]
-        stacked = jnp.concatenate(
-            [
-                jnp.concatenate([real, imag], axis=1),
-                jnp.concatenate([imag, -real], axis=1),
-            ],
-            axis=0,
-        )
-        tile = real.shape[0]
-        found = kept if block == 0 else given
-        for index, partner in enumerate(partners):
-            other = swaps[index] if block == 0 else 1 - swaps[index]
-            moving = jnp.concatenate([partner[0, other, 0], partner[1, other, 0]], axis=1)
-            product = lax.dot_general(
-                stacked, moving, (((1,), (1,)), ((), ())), preferred_element_type=jnp.float32
+    for chan in range(own.shape[2]):
+        for block in range(2):
+            real, imag = own[0, block, chan], own[1, block, chan]
+            stacked = jnp.concatenate(
+                [
+                    jnp.concatenate([real, imag], axis=1),
+                    jnp.concatenate([imag, -real], axis=1),
+                ],
+                axis=0,
             )
-            product = (product * (1.0 / SPECTRA)).astype(jnp.bfloat16)
-            found[index, 0, 0] = product[:tile]
-            found[index, 0, 1] = product[tile:]
+            tile = real.shape[0]
+            found = kept if block == 0 else given
+            for index, partner in enumerate(partners):
+                other = swaps[index] if block == 0 else 1 - swaps[index]
+                moving = jnp.concatenate([partner[0, other, chan], partner[1, other, chan]], axis=1)
+                product = lax.dot_general(
+                    stacked, moving, (((1,), (1,)), ((), ())), preferred_element_type=jnp.float32
+                )
+                product = (product * (1.0 / SPECTRA)).astype(jnp.bfloat16)
+                found[index, chan, 0] = product[:tile]
+                found[index, chan, 1] = product[tile:]
 
 
 def visibilities(own, partners, swaps):
     _, _, chans, tile, spectra = own.shape
     count = len(partners)
-    data = pl.BlockSpec((2, 2, 1, tile, spectra), lambda chan, _: (0, 0, chan, 0, 0))
-    made = pl.BlockSpec((count, 1, 2, tile, tile), lambda chan, _: (0, chan, 0, 0, 0))
+    data = pl.BlockSpec((2, 2, 2, tile, spectra), lambda chan, _: (0, 0, chan, 0, 0))
+    made = pl.BlockSpec((count, 2, 2, tile, tile), lambda chan, _: (0, chan, 0, 0, 0))
     shape = jax.ShapeDtypeStruct((count, chans, 2, tile, tile), jnp.bfloat16)
     return pl.pallas_call(
         visibility_kernel,
         grid_spec=pltpu.PrefetchScalarGridSpec(
             num_scalar_prefetch=1,
-            grid=(chans,),
+            grid=(chans // 2,),
             in_specs=[data] * (1 + count),
             out_specs=[made, made],
         ),
         out_shape=[shape, shape],
         compiler_params=pltpu.CompilerParams(vmem_limit_bytes=24 * 1024 * 1024),
     )(jnp.stack(swaps).astype(jnp.int32), own, *partners)
+
+
+def placement_kernel(column, *refs):
+    out, sources = refs[-1], refs[:6]
+    side, part = pl.program_id(0), pl.program_id(1)
+    local = side == column[0]
+    for index in range(3):
+        at = jnp.where(part == 0, index, 2 - index)
+
+        @pl.when(local)
+        def _(index=index, at=at):
+            out[:, 0, at] = sources[2 * index][0]
+
+        @pl.when(jnp.logical_not(local))
+        def _(index=index, at=at):
+            out[:, 0, at] = sources[2 * index + 1][0]
+
+
+def placed(column, groups, parts, first, into=None):
+    _, chans, two, tile, _ = groups[0][0].shape
+    sources = [array for group in groups for array in group]
+    source = pl.BlockSpec(
+        (1, chans, two, tile, tile), lambda side, part, _: (part, 0, 0, 0, 0)
+    )
+    made = pl.BlockSpec(
+        (chans, 1, 3, two, tile, tile), lambda side, part, _: (side, 0, first + 2 * part, 0, 0, 0)
+    )
+    kept = [] if into is None else [into]
+    return pl.pallas_call(
+        placement_kernel,
+        grid_spec=pltpu.PrefetchScalarGridSpec(
+            num_scalar_prefetch=1,
+            grid=(2, parts),
+            in_specs=[source] * 6 + [pl.BlockSpec(memory_space=pl.ANY)] * len(kept),
+            out_specs=made,
+        ),
+        out_shape=jax.ShapeDtypeStruct((2 * chans, 1, 9, two, tile, tile), jnp.bfloat16),
+        input_output_aliases={7: 0} if kept else {},
+        compiler_params=pltpu.CompilerParams(vmem_limit_bytes=24 * 1024 * 1024),
+    )(column.astype(jnp.int32)[None], *sources, *kept)
 
 
 def body(samples, chan_list):
@@ -125,16 +166,17 @@
             jnp.bool_(True) if at == half else (plane + at) % half > plane for at in partners
         ]
         mine, theirs = visibilities(blocks[0], sources, swaps)
-        moved = to_twin(theirs)
-        for index, at in enumerate(partners):
-            tiles[half if at == half else -at % half] = (mine[index], moved[index])
+        tiles[tuple(half if at == half else -at % half for at in partners)] = (
+            mine,
+            to_twin(theirs),
+        )
 
     def far(owner, partner):
         swap = (plane + partner) % half > (plane + owner) % half
         mine, theirs = visibilities(blocks[owner], [blocks[partner]], [swap])
-        tiles[(owner - partner) % half] = (
-            along_ring(mine, owner)[0],
-            along_ring(theirs, owner, 1)[0],
+        tiles[((owner - partner) % half,)] = (
+            along_ring(mine, owner),
+            along_ring(theirs, owner, 1),
         )
 
     def step(partner):
@@ -157,14 +199,8 @@
     settle()
     far(1, -3)
     near(-3)
-
-    def whole(place):
-        return jnp.stack([tiles[offset][place] for offset in range(half + 1)], axis=1)
-
-    mine, theirs = whole(0), whole(1)
-    low = jnp.where(column == 0, mine, theirs)
-    high = jnp.where(column == 0, theirs, mine)
-    return jnp.concatenate([low, high], axis=0)[:, None]
+    most = placed(column, [tiles[0, 8], tiles[1, 7], tiles[2, 6]], 2, 0)
+    return placed(column, [tiles[(3,)], tiles[(4,)], tiles[(5,)]], 1, 1, most)
 
 
 def solution(mesh):

time: 139 us -> 136 us (0.978)
  local copies, waits for them, and re-layouts: 12.1 us -> 7.16 us
  Pallas kernels: 17.4 us -> 20.3 us
    pallas_call x0 -> x2, Pallas kernels: none -> 5.99 us  [placed(): pl.pallas_call(placement_kernel, grid_spec=pltpu.PrefetchScalarGridSpec(n...]
    squeeze x6 -> x0, local copies, waits for them, and re-layouts: 4.39 us -> none  [near(): tiles[half if at == half else -at % half] = (mine[index], moved[index])]
    broadcast_in_dim x1 -> x0, local copies, waits for them, and re-layouts: 3.15 us -> none  [body(): return jnp.concatenate([low, high], axis=0)[:, None]]
    pallas_call x6, Pallas kernels: 17.4 us -> 14.3 us  [visibilities(): pl.pallas_call(visibility_kernel, grid_spec=pltpu.PrefetchScalarGridSpec(...]
    unnamed x40 -> x26, local copies, waits for them, and re-layouts: 1.38 us -> 4.05 us
  transfers between devices with their start and end apart: 14 -> 14, of which waited for: 9 -> 12; matrix products, arithmetic and copies ran while one was open for 4% -> 0% of each run, Pallas kernels for 12% -> 13%
where the time goes in v5:
time: 136 us; the launch traced here: 134 us
  waiting for transfers between devices  65.5 us (48%)
  starting transfers between devices  33.1 us (24%)
  Pallas kernels  20.3 us (15%)
  local copies, waits for them, and re-layouts  7.16 us (5%)
  matrix products  4.59 us (3%)
  other arithmetic  2.48 us (2%)
    ppermute x13, waiting for transfers between devices, along_ring(): return lax.ppermute(value, ('column', 'plane'), pairs)  49.7 us
    ppermute x13, starting transfers between devices, along_ring(): return lax.ppermute(value, ('column', 'plane'), pairs)  25.5 us
    all_to_all x1, waiting for transfers between devices, body(): lax.all_to_all(voltages, ('freq', 'column'), split_axis=0, concat_axis=0,...  15.8 us
    pallas_call x6, Pallas kernels, visibilities(): pl.pallas_call(visibility_kernel, grid_spec=pltpu.PrefetchScalarGridSpec(...  14.3 us
    all_to_all x1, starting transfers between devices, body(): lax.all_to_all(voltages, ('freq', 'column'), split_axis=0, concat_axis=0,...  7.56 us
    pallas_call x2, Pallas kernels, placed(): pl.pallas_call(placement_kernel, grid_spec=pltpu.PrefetchScalarGridSpec(n...  5.99 us
    conv_general_dilated x1, matrix products, channelize(): lax.conv_general_dilated(frames, filters, window_strides=(1,), padding='V...  4.59 us
    unnamed x26, local copies, waits for them, and re-layouts  4.05 us
  transfers between devices with their start and end apart: 14, of which 12 were waited for; matrix products, arithmetic and copies ran while one was open for 0% of the time, Pallas kernels for 13%

profile of v5, /device:TPU:6, one launch (start us, length us, event | category | flops | bytes accessed | tf_op | source)
XLA Modules:
  0.0 134.0 jit_solution(10667121275421872205)
XLA Ops:
  0.0 0.0 copy-start
  0.0 0.7 fusion.17
  1.4 0.1 fusion.9
  1.6 0.8 mul.110
  2.3 1.2 fusion.7
  3.6 0.1 maximum_bitcast_fusion
  3.6 0.1 mul.116
  3.7 0.0 copy-done
  3.7 4.6 %fusion.3 = bf16[256,8,256]{0,1,2:T(8,128)(2,1)S(1)} fusion(bf16[8,271,256]{2,0,1:T(8,128)(2,1)S(1)} %bitcast.27, f32[256,256]{1,0:T(8,128)S(1)} %mul.116, f32[16,256]{1,0:T(8,128)S(1)} %fusion.9), kind=kOutput, calls=%fused_computation.4 | convolution fusion | flops 4297588736 | bytes 2437120 | tf_op jit(solution)/shard_map/conv_general_dilated | solution.py:46
  8.3 2.0 %copy.6 = bf16[256,8,256]{2,1,0:T(8,128)(2,1)} copy(bf16[256,8,256]{0,1,2:T(8,128)(2,1)S(1)} %fusion.3) | data formatting | bytes 2097152 | tf_op jit(solution)/shard_map/convert_element_type | solution.py:53
  10.4 7.6 %all-to-all-start = ((bf16[32,2,4,8,256]{4,3,2,1,0:T(8,128)(2,1)}), bf16[32,2,4,8,256]{4,3,2,1,0:T(8,128)(2,1)S(1)}, u32[]{:S(2)}, u32[]{:S(2)}) async-start(bf16[32,2,4,8,256]{4,3,2,1,0:T(8,128)(2,1)} %bitcast.5), calls=%async_computation | async-start | bytes 2097152 | tf_op jit(solution)/shard_map/all_to_all | solution.py:151
  18.0 15.8 %all-to-all-done = bf16[32,2,4,8,256]{4,3,2,1,0:T(8,128)(2,1)S(1)} async-done(((bf16[32,2,4,8,256]{4,3,2,1,0:T(8,128)(2,1)}), bf16[32,2,4,8,256]{4,3,2,1,0:T(8,128)(2,1)S(1)}, u32[]{:S(2)}, u32[]{:S(2)}) %all-to-all-start) | async-done | bytes 1048608 | tf_op jit(solution)/shard_map/all_to_all | solution.py:151
  33.8 0.1 constant_dynamic-slice_fusion.1
  33.9 0.1 copy_bitcast_fusion
  34.0 0.1 pad_maximum_fusion.own.refs_0_.refs_1_
  34.1 5.9 %collective-permute-start.2 = (bf16[2,2,4,128,256]{4,3,2,1,0:T(8,128)(2,1)S(1)}, bf16[2,2,4,128,256]{4,3,2,1,0:T(8,128)(2,1)S(1)}, u32[]{:S(2)}, u32[]{:S(2)}) collective-permute-start(bf16[2,2,4,128,256]{4,3,2,1,0:T(8,128)(2,1)S(1)} %pad_maximum_fusion.own.refs_0_.refs_1_), channel_id=1, source_target_pairs={{0,7},{1,0},{2,1},{3,2},{4,3},{5,4},{6,5},{7,6},{8,15},{9,8},{10,9... | collective-permute-start | bytes 3145736 | tf_op jit(solution)/shard_map/ppermute | solution.py:21
  40.1 0.0 collective-permute-start.1
  40.1 0.1 add_convert_fusion.swaps
  40.1 2.3 %shard_map.28 = (bf16[2,4,2,128,128]{4,3,2,1,0:T(8,128)(2,1)S(1)}, bf16[2,4,2,128,128]{4,3,2,1,0:T(8,128)(2,1)S(1)}) custom-call(s32[2]{0:T(128)S(1)} %add_convert_fusion.swaps, bf16[2,2,4,128,256]{4,3,2,1,0:T(8,128)(2,1)S(1)} %pad_maximum_fusion.own.refs_0_.refs_1_, bf16[2,2,4,128,256]{4,3,2,1,0:T(8,128)(2,1)S(1)} %pad_maximum_fusion.own.refs_0_.refs_1_, ...), custom_call_target="tpu_custom_call" | custom-call | tf_op jit(solution)/shard_map/pallas_call | solution.py:87
  42.4 0.0 copy-start.3
  42.4 0.8 copy-done.3
  43.2 0.9 collective-permute-start
  44.1 13.5 %collective-permute-done.refs_1_ = bf16[2,4,2,128,128]{4,3,2,1,0:T(8,128)(2,1)S(1)} collective-permute-done((bf16[2,4,2,128,128]{4,3,2,1,0:T(8,128)(2,1)S(1)}, bf16[2,4,2,128,128]{4,3,2,1,0:T(8,128)(2,1)S(1)}, u32[]{:S(2)}, u32[]{:S(2)}) %collective-permute-start) | collective-permute-done | bytes 524320 | tf_op jit(solution)/shard_map/ppermute | solution.py:21
  57.7 0.8 copy-done.5
  58.5 3.6 %collective-permute-done.2.refs_1_.own = bf16[2,2,4,128,256]{4,3,2,1,0:T(8,128)(2,1)S(1)} collective-permute-done((bf16[2,2,4,128,256]{4,3,2,1,0:T(8,128)(2,1)S(1)}, bf16[2,2,4,128,256]{4,3,2,1,0:T(8,128)(2,1)S(1)}, u32[]{:S(2)}, u32[]{:S(2)}) %collective-permute-start.2) | collective-permute-done | bytes 1048608 | tf_op jit(solution)/shard_map/ppermute | solution.py:21
  62.0 3.5 %collective-permute-done.1.refs_0_.own = bf16[2,2,4,128,256]{4,3,2,1,0:T(8,128)(2,1)} collective-permute-done((bf16[2,2,4,128,256]{4,3,2,1,0:T(8,128)(2,1)S(1)}, bf16[2,2,4,128,256]{4,3,2,1,0:T(8,128)(2,1)}, u32[]{:S(2)}, u32[]{:S(2)}) %collective-permute-start.1) | collective-permute-done | bytes 1048608 | tf_op jit(solution)/shard_map/ppermute | solution.py:21
  65.6 0.0 collective-permute-start.4
  65.6 3.2 %collective-permute-start.5 = (bf16[2,2,4,128,256]{4,3,2,1,0:T(8,128)(2,1)S(1)}, bf16[2,2,4,128,256]{4,3,2,1,0:T(8,128)(2,1)}, u32[]{:S(2)}, u32[]{:S(2)}) collective-permute-start(bf16[2,2,4,128,256]{4,3,2,1,0:T(8,128)(2,1)S(1)} %collective-permute-done.2.refs_1_.own), channel_id=1, source_target_pairs={{0,7},{1,0},{2,1},{3,2},{4,3},{5,4},{6,5},{7,6},{8,15},{9,8},{10,9... | collective-permute-start | bytes 3145736 | tf_op jit(solution)/shard_map/ppermute | solution.py:21
  68.8 0.1 add_convert_fusion.1.swaps
  68.9 3.1 %shard_map.29 = (bf16[2,4,2,128,128]{4,3,2,1,0:T(8,128)(2,1)S(1)}, bf16[2,4,2,128,128]{4,3,2,1,0:T(8,128)(2,1)S(1)}) custom-call(s32[2]{0:T(128)S(1)} %add_convert_fusion.1.swaps, bf16[2,2,4,128,256]{4,3,2,1,0:T(8,128)(2,1)S(1)} %pad_maximum_fusion.own.refs_0_.refs_1_, bf16[2,2,4,128,256]{4,3,2,1,0:T(8,128)(2,1)} %collective-permute-done.1.refs_0_.own, ...), custom_call_target="tpu_custom_call" | custom-call | tf_op jit(solution)/shard_map/pallas_call | solution.py:87
  72.0 0.0 copy-start.7
  72.0 0.8 copy-done.7
  72.8 1.7 %collective-permute-start.3 = (bf16[2,4,2,128,128]{4,3,2,1,0:T(8,128)(2,1)S(1)}, bf16[2,4,2,128,128]{4,3,2,1,0:T(8,128)(2,1)S(1)}, u32[]{:S(2)}, u32[]{:S(2)}) collective-permute-start(bf16[2,4,2,128,128]{4,3,2,1,0:T(8,128)(2,1)S(1)} %get-tuple-element.50), channel_id=1, source_target_pairs={{0,8},{1,9},{2,10},{3,11},{4,12},{5,13},{6,14},{7,15},{8,0},{9,1},... | collective-permute-start | bytes 1572872 | tf_op jit(solution)/shard_map/ppermute | solution.py:21
  74.6 11.2 %collective-permute-done.3.refs_3_ = bf16[2,4,2,128,128]{4,3,2,1,0:T(8,128)(2,1)S(1)} collective-permute-done((bf16[2,4,2,128,128]{4,3,2,1,0:T(8,128)(2,1)S(1)}, bf16[2,4,2,128,128]{4,3,2,1,0:T(8,128)(2,1)S(1)}, u32[]{:S(2)}, u32[]{:S(2)}) %collective-permute-start.3) | collective-permute-done | bytes 524320 | tf_op jit(solution)/shard_map/ppermute | solution.py:21
  85.8 0.8 copy-done.9
  86.6 3.7 %collective-permute-done.4.refs_0_ = bf16[2,2,4,128,256]{4,3,2,1,0:T(8,128)(2,1)} collective-permute-done((bf16[2,2,4,128,256]{4,3,2,1,0:T(8,128)(2,1)}, bf16[2,2,4,128,256]{4,3,2,1,0:T(8,128)(2,1)}, u32[]{:S(2)}, u32[]{:S(2)}) %collective-permute-start.4) | collective-permute-done | bytes 1048608 | tf_op jit(solution)/shard_map/ppermute | solution.py:21
  90.4 0.0 collective-permute-done.5.refs_1_.refs_0_
  90.4 0.0 copy-done.1
  90.4 0.0 collective-permute-start.9
  90.4 0.1 add_convert_fusion.2.swaps
  90.5 4.0 %shard_map.30 = (bf16[2,4,2,128,128]{4,3,2,1,0:T(8,128)(2,1)S(1)}, bf16[2,4,2,128,128]{4,3,2,1,0:T(8,128)(2,1)}) custom-call(s32[2]{0:T(128)S(1)} %add_convert_fusion.2.swaps, bf16[2,2,4,128,256]{4,3,2,1,0:T(8,128)(2,1)S(1)} %pad_maximum_fusion.own.refs_0_.refs_1_, bf16[2,2,4,128,256]{4,3,2,1,0:T(8,128)(2,1)} %collective-permute-done.4.refs_0_, ...), custom_call_target="tpu_custom_call" | custom-call | tf_op jit(solution)/shard_map/pallas_call | solution.py:87
  94.4 0.8 copy-done.11
  95.2 2.6 %collective-permute-start.6 = (bf16[2,4,2,128,128]{4,3,2,1,0:T(8,128)(2,1)}, bf16[2,4,2,128,128]{4,3,2,1,0:T(8,128)(2,1)}, u32[]{:S(2)}, u32[]{:S(2)}) collective-permute-start(bf16[2,4,2,128,128]{4,3,2,1,0:T(8,128)(2,1)} %get-tuple-element.59), channel_id=1, source_target_pairs={{0,8},{1,9},{2,10},{3,11},{4,12},{5,13},{6,14},{7,15},{8,0},{9,1},... | collective-permute-start | bytes 1572872 | tf_op jit(solution)/shard_map/ppermute | solution.py:21
  97.9 2.8 %shard_map.31 = (bf16[1,4,2,128,128]{4,3,2,1,0:T(8,128)(2,1)}, bf16[1,4,2,128,128]{4,3,2,1,0:T(8,128)(2,1)}) custom-call(s32[1]{0:T(128)} %bitcast.17.swaps, bf16[2,2,4,128,256]{4,3,2,1,0:T(8,128)(2,1)} %collective-permute-done.1.refs_0_.own, bf16[2,2,4,128,256]{4,3,2,1,0:T(8,128)(2,1)} %collective-permute-done.5.refs_1_.refs_0_), custom_call_target="tpu_custom_call" | custom-call | tf_op jit(solution)/shard_map/pallas_call | solution.py:87
  100.7 3.2 %collective-permute-start.7 = (bf16[1,4,2,128,128]{4,3,2,1,0:T(8,128)(2,1)}, bf16[1,4,2,128,128]{4,3,2,1,0:T(8,128)(2,1)S(1)}, u32[]{:S(2)}, u32[]{:S(2)}) collective-permute-start(bf16[1,4,2,128,128]{4,3,2,1,0:T(8,128)(2,1)} %get-tuple-element.61), channel_id=1, source_target_pairs={{0,7},{1,0},{2,1},{3,2},{4,3},{5,4},{6,5},{7,6},{8,15},{9,8},{10,9... | collective-permute-start | bytes 786440 | tf_op jit(solution)/shard_map/ppermute | solution.py:21
  103.9 1.9 %collective-permute-start.8 = (bf16[1,4,2,128,128]{4,3,2,1,0:T(8,128)(2,1)}, bf16[1,4,2,128,128]{4,3,2,1,0:T(8,128)(2,1)}, u32[]{:S(2)}, u32[]{:S(2)}) collective-permute-start(bf16[1,4,2,128,128]{4,3,2,1,0:T(8,128)(2,1)} %get-tuple-element.62), channel_id=1, source_target_pairs={{0,15},{1,8},{2,9},{3,10},{4,11},{5,12},{6,13},{7,14},{8,7},{9,0},... | collective-permute-start | bytes 786440 | tf_op jit(solution)/shard_map/ppermute | solution.py:21
  105.7 4.6 %collective-permute-done.7.refs_4_ = bf16[1,4,2,128,128]{4,3,2,1,0:T(8,128)(2,1)S(1)} collective-permute-done((bf16[1,4,2,128,128]{4,3,2,1,0:T(8,128)(2,1)}, bf16[1,4,2,128,128]{4,3,2,1,0:T(8,128)(2,1)S(1)}, u32[]{:S(2)}, u32[]{:S(2)}) %collective-permute-start.7) | collective-permute-done | bytes 262176 | tf_op jit(solution)/shard_map/ppermute | solution.py:21
  110.3 3.1 %collective-permute-done.8.refs_5_ = bf16[1,4,2,128,128]{4,3,2,1,0:T(8,128)(2,1)} collective-permute-done((bf16[1,4,2,128,128]{4,3,2,1,0:T(8,128)(2,1)}, bf16[1,4,2,128,128]{4,3,2,1,0:T(8,128)(2,1)}, u32[]{:S(2)}, u32[]{:S(2)}) %collective-permute-start.8) | collective-permute-done | bytes 262176 | tf_op jit(solution)/shard_map/ppermute | solution.py:21
  113.4 0.6 collective-permute-done.6.refs_5_
  114.1 0.1 collective-permute-done.9.refs_0_
  114.1 0.0 copy-start.12
  114.1 1.1 shard_map.32
  115.2 3.6 %collective-permute-start.10 = (bf16[1,4,2,128,128]{4,3,2,1,0:T(8,128)(2,1)S(1)}, bf16[1,4,2,128,128]{4,3,2,1,0:T(8,128)(2,1)S(1)}, u32[]{:S(2)}, u32[]{:S(2)}) collective-permute-start(bf16[1,4,2,128,128]{4,3,2,1,0:T(8,128)(2,1)S(1)} %get-tuple-element.67), channel_id=1, source_target_pairs={{0,8},{1,9},{2,10},{3,11},{4,12},{5,13},{6,14},{7,15},{8,0},{9,1},... | collective-permute-start | bytes 786440 | tf_op jit(solution)/shard_map/ppermute | solution.py:21
  118.8 0.0 copy-done.2
  118.8 1.1 shard_map.33
  119.9 0.1 collective-permute-start.11
  120.0 2.3 %collective-permute-start.12 = (bf16[1,4,2,128,128]{4,3,2,1,0:T(8,128)(2,1)S(1)}, bf16[1,4,2,128,128]{4,3,2,1,0:T(8,128)(2,1)S(1)}, u32[]{:S(2)}, u32[]{:S(2)}) collective-permute-start(bf16[1,4,2,128,128]{4,3,2,1,0:T(8,128)(2,1)S(1)} %get-tuple-element.70), channel_id=1, source_target_pairs={{0,9},{1,10},{2,11},{3,12},{4,13},{5,14},{6,15},{7,8},{8,1},{9,2},... | collective-permute-start | bytes 786440 | tf_op jit(solution)/shard_map/ppermute | solution.py:21
  122.3 0.0 copy-done.4
  122.3 0.0 copy-done.12
  122.3 3.8 %shard_map.34.refs_6_ = bf16[8,1,9,2,128,128]{5,4,3,2,1,0:T(8,128)(2,1)} custom-call(s32[1]{0:T(128)} %bitcast.column, bf16[2,4,2,128,128]{4,3,2,1,0:T(8,128)(2,1)S(1)} %copy-done.4, bf16[2,4,2,128,128]{4,3,2,1,0:T(8,128)(2,1)S(1)} %copy-done.6, bf16[2,4,2,128,128]{4,3,2,1,0:T(8,128)(2,1)S(1)} %copy-done.8, bf16[2,4,2,128,128]{4,3,2,1,0:T(8,128)(2,1)S(1)} %copy-done.10, ...), custom_call_target="tpu_custom_call" | custom-call | tf_op jit(solution)/shard_map/pallas_call | solution.py:126
  126.1 0.0 collective-permute-done.10.refs_1_
  126.2 3.1 %collective-permute-done.11.refs_2_ = bf16[1,4,2,128,128]{4,3,2,1,0:T(8,128)(2,1)S(1)} collective-permute-done((bf16[1,4,2,128,128]{4,3,2,1,0:T(8,128)(2,1)S(1)}, bf16[1,4,2,128,128]{4,3,2,1,0:T(8,128)(2,1)S(1)}, u32[]{:S(2)}, u32[]{:S(2)}) %collective-permute-start.11) | collective-permute-done | bytes 262176 | tf_op jit(solution)/shard_map/ppermute | solution.py:21
  129.3 2.6 %collective-permute-done.12.refs_3_ = bf16[1,4,2,128,128]{4,3,2,1,0:T(8,128)(2,1)S(1)} collective-permute-done((bf16[1,4,2,128,128]{4,3,2,1,0:T(8,128)(2,1)S(1)}, bf16[1,4,2,128,128]{4,3,2,1,0:T(8,128)(2,1)S(1)}, u32[]{:S(2)}, u32[]{:S(2)}) %collective-permute-start.12) | collective-permute-done | bytes 262176 | tf_op jit(solution)/shard_map/ppermute | solution.py:21
  131.8 2.2 %shard_map.35 = bf16[8,1,9,2,128,128]{5,4,3,2,1,0:T(8,128)(2,1)} custom-call(s32[1]{0:T(128)} %bitcast.column, bf16[1,4,2,128,128]{4,3,2,1,0:T(8,128)(2,1)S(1)} %get-tuple-element.66.refs_0_, bf16[1,4,2,128,128]{4,3,2,1,0:T(8,128)(2,1)S(1)} %collective-permute-done.10.refs_1_, ...), custom_call_target="tpu_custom_call", output_to_operand_aliasing={{}: (7, {})} | custom-call | tf_op jit(solution)/shard_map/pallas_call | solution.py:126
  (12 shorter events, 0.0 us)
Async XLA Ops:
  0.0 3.7 %copy-start = (bf16[1,8,69376]{2,1,0:T(8,128)(2,1)S(1)}, bf16[1,8,69376]{2,1,0:T(8,128)(2,1)}, u32[]{:S(2)}) copy-start(bf16[1,8,69376]{2,1,0:T(8,128)(2,1)} %param.2) | copy-start | bytes 3330052
  10.4 23.4 %all-to-all-start = ((bf16[32,2,4,8,256]{4,3,2,1,0:T(8,128)(2,1)}), bf16[32,2,4,8,256]{4,3,2,1,0:T(8,128)(2,1)S(1)}, u32[]{:S(2)}, u32[]{:S(2)}) async-start(bf16[32,2,4,8,256]{4,3,2,1,0:T(8,128)(2,1)} %bitcast.5), calls=%async_computation | async-start | bytes 2097152 | tf_op jit(solution)/shard_map/all_to_all | solution.py:151
  34.1 27.9 %collective-permute-start.2 = (bf16[2,2,4,128,256]{4,3,2,1,0:T(8,128)(2,1)S(1)}, bf16[2,2,4,128,256]{4,3,2,1,0:T(8,128)(2,1)S(1)}, u32[]{:S(2)}, u32[]{:S(2)}) collective-permute-start(bf16[2,2,4,128,256]{4,3,2,1,0:T(8,128)(2,1)S(1)} %pad_maximum_fusion.own.refs_0_.refs_1_), channel_id=1, source_target_pairs={{0,7},{1,0},{2,1},{3,2},{4,3},{5,4},{6,5},{7,6},{8,15},{9,8},{10,9... | collective-permute-start | bytes 3145736 | tf_op jit(solution)/shard_map/ppermute | solution.py:21
  40.1 25.5 %collective-permute-start.1 = (bf16[2,2,4,128,256]{4,3,2,1,0:T(8,128)(2,1)S(1)}, bf16[2,2,4,128,256]{4,3,2,1,0:T(8,128)(2,1)}, u32[]{:S(2)}, u32[]{:S(2)}) collective-permute-start(bf16[2,2,4,128,256]{4,3,2,1,0:T(8,128)(2,1)S(1)} %pad_maximum_fusion.own.refs_0_.refs_1_), channel_id=1, source_target_pairs={{0,1},{1,2},{2,3},{3,4},{4,5},{5,6},{6,7},{7,0},{8,9},{9,10},{10,1... | collective-permute-start | bytes 3145736 | tf_op jit(solution)/shard_map/ppermute | solution.py:21
  42.4 0.8 copy-start.3
  43.2 14.5 %collective-permute-start = (bf16[2,4,2,128,128]{4,3,2,1,0:T(8,128)(2,1)S(1)}, bf16[2,4,2,128,128]{4,3,2,1,0:T(8,128)(2,1)S(1)}, u32[]{:S(2)}, u32[]{:S(2)}) collective-permute-start(bf16[2,4,2,128,128]{4,3,2,1,0:T(8,128)(2,1)S(1)} %get-tuple-element.43), channel_id=1, source_target_pairs={{0,8},{1,9},{2,10},{3,11},{4,12},{5,13},{6,14},{7,15},{8,0},{9,1},... | collective-permute-start | bytes 1572872 | tf_op jit(solution)/shard_map/ppermute | solution.py:21
  57.7 0.8 copy-start.5
  62.0 28.3 %copy-start.1 = (bf16[2,2,4,128,256]{4,3,2,1,0:T(8,128)(2,1)}, bf16[2,2,4,128,256]{4,3,2,1,0:T(8,128)(2,1)S(1)}, u32[]{:S(2)}) copy-start(bf16[2,2,4,128,256]{4,3,2,1,0:T(8,128)(2,1)S(1)} %collective-permute-done.2.refs_1_.own) | copy-start | bytes 3145732
  65.6 24.8 %collective-permute-start.4 = (bf16[2,2,4,128,256]{4,3,2,1,0:T(8,128)(2,1)}, bf16[2,2,4,128,256]{4,3,2,1,0:T(8,128)(2,1)}, u32[]{:S(2)}, u32[]{:S(2)}) collective-permute-start(bf16[2,2,4,128,256]{4,3,2,1,0:T(8,128)(2,1)} %collective-permute-done.1.refs_0_.own), channel_id=1, source_target_pairs={{0,1},{1,2},{2,3},{3,4},{4,5},{5,6},{6,7},{7,0},{8,9},{9,10},{10,1... | collective-permute-start | bytes 3145736 | tf_op jit(solution)/shard_map/ppermute | solution.py:21
  65.6 24.8 %collective-permute-start.5 = (bf16[2,2,4,128,256]{4,3,2,1,0:T(8,128)(2,1)S(1)}, bf16[2,2,4,128,256]{4,3,2,1,0:T(8,128)(2,1)}, u32[]{:S(2)}, u32[]{:S(2)}) collective-permute-start(bf16[2,2,4,128,256]{4,3,2,1,0:T(8,128)(2,1)S(1)} %collective-permute-done.2.refs_1_.own), channel_id=1, source_target_pairs={{0,7},{1,0},{2,1},{3,2},{4,3},{5,4},{6,5},{7,6},{8,15},{9,8},{10,9... | collective-permute-start | bytes 3145736 | tf_op jit(solution)/shard_map/ppermute | solution.py:21
  72.0 0.8 copy-start.7
  72.8 13.0 %collective-permute-start.3 = (bf16[2,4,2,128,128]{4,3,2,1,0:T(8,128)(2,1)S(1)}, bf16[2,4,2,128,128]{4,3,2,1,0:T(8,128)(2,1)S(1)}, u32[]{:S(2)}, u32[]{:S(2)}) collective-permute-start(bf16[2,4,2,128,128]{4,3,2,1,0:T(8,128)(2,1)S(1)} %get-tuple-element.50), channel_id=1, source_target_pairs={{0,8},{1,9},{2,10},{3,11},{4,12},{5,13},{6,14},{7,15},{8,0},{9,1},... | collective-permute-start | bytes 1572872 | tf_op jit(solution)/shard_map/ppermute | solution.py:21
  85.8 0.8 copy-start.9
  90.4 23.8 %collective-permute-start.9 = (bf16[2,2,4,128,256]{4,3,2,1,0:T(8,128)(2,1)}, bf16[2,2,4,128,256]{4,3,2,1,0:T(8,128)(2,1)S(1)}, u32[]{:S(2)}, u32[]{:S(2)}) collective-permute-start(bf16[2,2,4,128,256]{4,3,2,1,0:T(8,128)(2,1)} %collective-permute-done.4.refs_0_), channel_id=1, source_target_pairs={{0,1},{1,2},{2,3},{3,4},{4,5},{5,6},{6,7},{7,0},{8,9},{9,10},{10,1... | collective-permute-start | bytes 3145736 | tf_op jit(solution)/shard_map/ppermute | solution.py:21
  94.4 0.8 copy-start.11
  95.2 18.8 %collective-permute-start.6 = (bf16[2,4,2,128,128]{4,3,2,1,0:T(8,128)(2,1)}, bf16[2,4,2,128,128]{4,3,2,1,0:T(8,128)(2,1)}, u32[]{:S(2)}, u32[]{:S(2)}) collective-permute-start(bf16[2,4,2,128,128]{4,3,2,1,0:T(8,128)(2,1)} %get-tuple-element.59), channel_id=1, source_target_pairs={{0,8},{1,9},{2,10},{3,11},{4,12},{5,13},{6,14},{7,15},{8,0},{9,1},... | collective-permute-start | bytes 1572872 | tf_op jit(solution)/shard_map/ppermute | solution.py:21
  100.7 9.7 %collective-permute-start.7 = (bf16[1,4,2,128,128]{4,3,2,1,0:T(8,128)(2,1)}, bf16[1,4,2,128,128]{4,3,2,1,0:T(8,128)(2,1)S(1)}, u32[]{:S(2)}, u32[]{:S(2)}) collective-permute-start(bf16[1,4,2,128,128]{4,3,2,1,0:T(8,128)(2,1)} %get-tuple-element.61), channel_id=1, source_target_pairs={{0,7},{1,0},{2,1},{3,2},{4,3},{5,4},{6,5},{7,6},{8,15},{9,8},{10,9... | collective-permute-start | bytes 786440 | tf_op jit(solution)/shard_map/ppermute | solution.py:21
  103.9 9.5 %collective-permute-start.8 = (bf16[1,4,2,128,128]{4,3,2,1,0:T(8,128)(2,1)}, bf16[1,4,2,128,128]{4,3,2,1,0:T(8,128)(2,1)}, u32[]{:S(2)}, u32[]{:S(2)}) collective-permute-start(bf16[1,4,2,128,128]{4,3,2,1,0:T(8,128)(2,1)} %get-tuple-element.62), channel_id=1, source_target_pairs={{0,15},{1,8},{2,9},{3,10},{4,11},{5,12},{6,13},{7,14},{8,7},{9,0},... | collective-permute-start | bytes 786440 | tf_op jit(solution)/shard_map/ppermute | solution.py:21
  105.7 13.1 %copy-start.2 = (bf16[2,2,4,128,256]{4,3,2,1,0:T(8,128)(2,1)S(1)}, bf16[2,2,4,128,256]{4,3,2,1,0:T(8,128)(2,1)}, u32[]{:S(2)}) copy-start(bf16[2,2,4,128,256]{4,3,2,1,0:T(8,128)(2,1)} %copy-done.1) | copy-start | bytes 3145732
  114.1 8.2 %copy-start.4 = (bf16[2,4,2,128,128]{4,3,2,1,0:T(8,128)(2,1)S(1)}, bf16[2,4,2,128,128]{4,3,2,1,0:T(8,128)(2,1)}, u32[]{:S(2)}) copy-start(bf16[2,4,2,128,128]{4,3,2,1,0:T(8,128)(2,1)} %copy-done.3) | copy-start | bytes 1572868
  114.1 8.2 %copy-start.6 = (bf16[2,4,2,128,128]{4,3,2,1,0:T(8,128)(2,1)S(1)}, bf16[2,4,2,128,128]{4,3,2,1,0:T(8,128)(2,1)}, u32[]{:S(2)}) copy-start(bf16[2,4,2,128,128]{4,3,2,1,0:T(8,128)(2,1)} %copy-done.5) | copy-start | bytes 1572868
  114.1 8.2 %copy-start.8 = (bf16[2,4,2,128,128]{4,3,2,1,0:T(8,128)(2,1)S(1)}, bf16[2,4,2,128,128]{4,3,2,1,0:T(8,128)(2,1)}, u32[]{:S(2)}) copy-start(bf16[2,4,2,128,128]{4,3,2,1,0:T(8,128)(2,1)} %copy-done.7) | copy-start | bytes 1572868
  114.1 8.2 %copy-start.10 = (bf16[2,4,2,128,128]{4,3,2,1,0:T(8,128)(2,1)S(1)}, bf16[2,4,2,128,128]{4,3,2,1,0:T(8,128)(2,1)}, u32[]{:S(2)}) copy-start(bf16[2,4,2,128,128]{4,3,2,1,0:T(8,128)(2,1)} %copy-done.9) | copy-start | bytes 1572868
  114.1 8.2 %copy-start.12 = (bf16[2,4,2,128,128]{4,3,2,1,0:T(8,128)(2,1)S(1)}, bf16[2,4,2,128,128]{4,3,2,1,0:T(8,128)(2,1)}, u32[]{:S(2)}) copy-start(bf16[2,4,2,128,128]{4,3,2,1,0:T(8,128)(2,1)} %copy-done.11) | copy-start | bytes 1572868
  115.2 10.9 %collective-permute-start.10 = (bf16[1,4,2,128,128]{4,3,2,1,0:T(8,128)(2,1)S(1)}, bf16[1,4,2,128,128]{4,3,2,1,0:T(8,128)(2,1)S(1)}, u32[]{:S(2)}, u32[]{:S(2)}) collective-permute-start(bf16[1,4,2,128,128]{4,3,2,1,0:T(8,128)(2,1)S(1)} %get-tuple-element.67), channel_id=1, source_target_pairs={{0,8},{1,9},{2,10},{3,11},{4,12},{5,13},{6,14},{7,15},{8,0},{9,1},... | collective-permute-start | bytes 786440 | tf_op jit(solution)/shard_map/ppermute | solution.py:21
  119.9 9.4 %collective-permute-start.11 = (bf16[1,4,2,128,128]{4,3,2,1,0:T(8,128)(2,1)S(1)}, bf16[1,4,2,128,128]{4,3,2,1,0:T(8,128)(2,1)S(1)}, u32[]{:S(2)}, u32[]{:S(2)}) collective-permute-start(bf16[1,4,2,128,128]{4,3,2,1,0:T(8,128)(2,1)S(1)} %get-tuple-element.69), channel_id=1, source_target_pairs={{0,1},{1,2},{2,3},{3,4},{4,5},{5,6},{6,7},{7,0},{8,9},{9,10},{10,1... | collective-permute-start | bytes 786440 | tf_op jit(solution)/shard_map/ppermute | solution.py:21
  120.0 11.8 %collective-permute-start.12 = (bf16[1,4,2,128,128]{4,3,2,1,0:T(8,128)(2,1)S(1)}, bf16[1,4,2,128,128]{4,3,2,1,0:T(8,128)(2,1)S(1)}, u32[]{:S(2)}, u32[]{:S(2)}) collective-permute-start(bf16[1,4,2,128,128]{4,3,2,1,0:T(8,128)(2,1)S(1)} %get-tuple-element.70), channel_id=1, source_target_pairs={{0,9},{1,10},{2,11},{3,12},{4,13},{5,14},{6,15},{7,8},{8,1},{9,2},... | collective-permute-start | bytes 786440 | tf_op jit(solution)/shard_map/ppermute | solution.py:21

commit v6 on v5

--- a/solution.py
+++ b/solution.py
@@ -53,48 +53,48 @@
     ).astype(jnp.bfloat16)
 
 
-def visibility_kernel(swaps, own, *refs):
-    partners, (kept, given) = refs[:-2], refs[-2:]
+def visibility_kernel(places, own, *refs):
+    partners, found = refs[:-1], refs[-1]
     for chan in range(own.shape[2]):
-        for block in range(2):
-            real, imag = own[0, block, chan], own[1, block, chan]
-            stacked = jnp.concatenate(
-                [
-                    jnp.concatenate([real, imag], axis=1),
-                    jnp.concatenate([imag, -real], axis=1),
-                ],
-                axis=0,
+        real, imag = own[0, 0, chan], own[1, 0, chan]
+        stacked = jnp.concatenate(
+            [
+                jnp.concatenate([real, imag], axis=1),
+                jnp.concatenate([imag, -real], axis=1),
+            ],
+            axis=0,
+        )
+        tile = real.shape[0]
+        for index, partner in enumerate(partners):
+            moving = jnp.concatenate([partner[0, 0, chan], partner[1, 0, chan]], axis=1)
+            product = lax.dot_general(
+                stacked, moving, (((1,), (1,)), ((), ())), preferred_element_type=jnp.float32
             )
-            tile = real.shape[0]
-            found = kept if block == 0 else given
-            for index, partner in enumerate(partners):
-                other = swaps[index] if block == 0 else 1 - swaps[index]
-                moving = jnp.concatenate([partner[0, other, chan], partner[1, other, chan]], axis=1)
-                product = lax.dot_general(
-                    stacked, moving, (((1,), (1,)), ((), ())), preferred_element_type=jnp.float32
-                )
-                product = (product * (1.0 / SPECTRA)).astype(jnp.bfloat16)
-                found[index, chan, 0] = product[:tile]
-                found[index, chan, 1] = product[tile:]
-
-
-def visibilities(own, partners, swaps):
+            product = (product * (1.0 / SPECTRA)).astype(jnp.bfloat16)
+            found[index, chan, 0] = product[:tile]
+            found[index, chan, 1] = product[tile:]
+
+
+def visibilities(own, partners, swaps, block):
     _, _, chans, tile, spectra = own.shape
     count = len(partners)
-    data = pl.BlockSpec((2, 2, 2, tile, spectra), lambda chan, _: (0, 0, chan, 0, 0))
-    made = pl.BlockSpec((count, 2, 2, tile, tile), lambda chan, _: (0, chan, 0, 0, 0))
-    shape = jax.ShapeDtypeStruct((count, chans, 2, tile, tile), jnp.bfloat16)
+    shape = (2, 1, 2, tile, spectra)
+    places = jnp.stack(swaps).astype(jnp.int32) ^ block
     return pl.pallas_call(
         visibility_kernel,
         grid_spec=pltpu.PrefetchScalarGridSpec(
             num_scalar_prefetch=1,
             grid=(chans // 2,),
-            in_specs=[data] * (1 + count),
-            out_specs=[made, made],
+            in_specs=[pl.BlockSpec(shape, lambda chan, _: (0, block, chan, 0, 0))]
+            + [
+                pl.BlockSpec(shape, lambda chan, at, index=index: (0, at[index], chan, 0, 0))
+                for index in range(count)
+            ],
+            out_specs=pl.BlockSpec((count, 2, 2, tile, tile), lambda chan, _: (0, chan, 0, 0, 0)),
         ),
-        out_shape=[shape, shape],
+        out_shape=jax.ShapeDtypeStruct((count, chans, 2, tile, tile), jnp.bfloat16),
         compiler_params=pltpu.CompilerParams(vmem_limit_bytes=24 * 1024 * 1024),
-    )(jnp.stack(swaps).astype(jnp.int32), own, *partners)
+    )(places, own, *partners)
 
 
 def placement_kernel(column, *refs):
@@ -165,7 +165,8 @@
         swaps = [
             jnp.bool_(True) if at == half else (plane + at) % half > plane for at in partners
         ]
-        mine, theirs = visibilities(blocks[0], sources, swaps)
+        theirs = visibilities(blocks[0], sources, swaps, 1)
+        mine = visibilities(blocks[0], sources, swaps, 0)
         tiles[tuple(half if at == half else -at % half for at in partners)] = (
             mine,
             to_twin(theirs),
@@ -173,7 +174,8 @@
 
     def far(owner, partner):
         swap = (plane + partner) % half > (plane + owner) % half
-        mine, theirs = visibilities(blocks[owner], [blocks[partner]], [swap])
+        theirs = visibilities(blocks[owner], [blocks[partner]], [swap], 1)
+        mine = visibilities(blocks[owner], [blocks[partner]], [swap], 0)
         tiles[((owner - partner) % half,)] = (
             along_ring(mine, owner),
             along_ring(theirs, owner, 1),

time: 136 us -> 135 us (level); the launches traced: 134 us -> 134 us
  Pallas kernels: 20.3 us -> 27.5 us
  waiting for transfers between devices: 65.5 us -> 60.3 us
    pallas_call x6 -> x12, Pallas kernels: 14.3 us -> 21.5 us  [visibilities(): pl.pallas_call(visibility_kernel, grid_spec=pltpu.PrefetchScalarGridSpec(...]
    ppermute x13, waiting for transfers between devices: 49.7 us -> 44.4 us  [along_ring(): return lax.ppermute(value, ('column', 'plane'), pairs)]
    unnamed x26 -> x22, local copies, waits for them, and re-layouts: 4.05 us -> 3.22 us
  transfers between devices with their start and end apart: 14 -> 14, of which waited for: 12 -> 11; matrix products, arithmetic and copies ran while one was open for 0% -> 0% of each run, Pallas kernels for 13% -> 18%
where the time goes in v6:
time: 135 us; the launch traced here: 134 us
  waiting for transfers between devices  60.3 us (45%)
  starting transfers between devices  32.2 us (24%)
  Pallas kernels  27.5 us (20%)
  local copies, waits for them, and re-layouts  6.33 us (5%)
  matrix products  4.59 us (3%)
  other arithmetic  2.55 us (2%)
    ppermute x13, waiting for transfers between devices, along_ring(): return lax.ppermute(value, ('column', 'plane'), pairs)  44.4 us
    ppermute x13, starting transfers between devices, along_ring(): return lax.ppermute(value, ('column', 'plane'), pairs)  24.7 us
    pallas_call x12, Pallas kernels, visibilities(): pl.pallas_call(visibility_kernel, grid_spec=pltpu.PrefetchScalarGridSpec(...  21.5 us
    all_to_all x1, waiting for transfers between devices, body(): lax.all_to_all(voltages, ('freq', 'column'), split_axis=0, concat_axis=0,...  15.8 us
    all_to_all x1, starting transfers between devices, body(): lax.all_to_all(voltages, ('freq', 'column'), split_axis=0, concat_axis=0,...  7.56 us
    pallas_call x2, Pallas kernels, placed(): pl.pallas_call(placement_kernel, grid_spec=pltpu.PrefetchScalarGridSpec(n...  5.99 us
    conv_general_dilated x1, matrix products, channelize(): lax.conv_general_dilated(frames, filters, window_strides=(1,), padding='V...  4.59 us
    unnamed x22, local copies, waits for them, and re-layouts  3.22 us
  transfers between devices with their start and end apart: 14, of which 11 were waited for; matrix products, arithmetic and copies ran while one was open for 0% of the time, Pallas kernels for 18%

profile of v6, /device:TPU:6, one launch (start us, length us, event | category | flops | bytes accessed | tf_op | source)
XLA Modules:
  0.0 134.4 jit_solution(125792654530343217)
XLA Ops:
  0.0 0.7 fusion.17
  1.4 0.1 fusion.9
  1.6 0.8 mul.110
  2.3 1.2 fusion.7
  3.6 0.1 maximum_bitcast_fusion
  3.6 0.1 mul.116
  3.7 4.6 %fusion.3 = bf16[256,8,256]{0,1,2:T(8,128)(2,1)S(1)} fusion(bf16[8,271,256]{2,0,1:T(8,128)(2,1)S(1)} %bitcast.27, f32[256,256]{1,0:T(8,128)S(1)} %mul.116, f32[16,256]{1,0:T(8,128)S(1)} %fusion.9), kind=kOutput, calls=%fused_computation.4 | convolution fusion | flops 4297588736 | bytes 2437120 | tf_op jit(solution)/shard_map/conv_general_dilated | solution.py:46
  8.3 2.0 %copy.6 = bf16[256,8,256]{2,1,0:T(8,128)(2,1)} copy(bf16[256,8,256]{0,1,2:T(8,128)(2,1)S(1)} %fusion.3) | data formatting | bytes 2097152 | tf_op jit(solution)/shard_map/convert_element_type | solution.py:53
  10.4 7.6 %all-to-all-start = ((bf16[32,2,4,8,256]{4,3,2,1,0:T(8,128)(2,1)}), bf16[32,2,4,8,256]{4,3,2,1,0:T(8,128)(2,1)S(1)}, u32[]{:S(2)}, u32[]{:S(2)}) async-start(bf16[32,2,4,8,256]{4,3,2,1,0:T(8,128)(2,1)} %bitcast.5), calls=%async_computation | async-start | bytes 2097152 | tf_op jit(solution)/shard_map/all_to_all | solution.py:151
  18.0 15.8 %all-to-all-done = bf16[32,2,4,8,256]{4,3,2,1,0:T(8,128)(2,1)S(1)} async-done(((bf16[32,2,4,8,256]{4,3,2,1,0:T(8,128)(2,1)}), bf16[32,2,4,8,256]{4,3,2,1,0:T(8,128)(2,1)S(1)}, u32[]{:S(2)}, u32[]{:S(2)}) %all-to-all-start) | async-done | bytes 1048608 | tf_op jit(solution)/shard_map/all_to_all | solution.py:151
  33.8 0.1 constant_dynamic-slice_fusion.1
  33.9 0.1 copy_bitcast_fusion
  34.0 0.1 pad_maximum_fusion.own.refs_0_.refs_1_
  34.1 5.9 %collective-permute-start.2 = (bf16[2,2,4,128,256]{4,3,2,1,0:T(8,128)(2,1)S(1)}, bf16[2,2,4,128,256]{4,3,2,1,0:T(8,128)(2,1)S(1)}, u32[]{:S(2)}, u32[]{:S(2)}) collective-permute-start(bf16[2,2,4,128,256]{4,3,2,1,0:T(8,128)(2,1)S(1)} %pad_maximum_fusion.own.refs_0_.refs_1_), channel_id=1, source_target_pairs={{0,7},{1,0},{2,1},{3,2},{4,3},{5,4},{6,5},{7,6},{8,15},{9,8},{10,9... | collective-permute-start | bytes 3145736 | tf_op jit(solution)/shard_map/ppermute | solution.py:21
  40.1 0.0 collective-permute-start.1
  40.1 0.1 broadcast_xor_fusion.2.places
  40.1 1.6 %shard_map.29 = bf16[2,4,2,128,128]{4,3,2,1,0:T(8,128)(2,1)S(1)} custom-call(s32[2]{0:T(128)S(1)} %broadcast_xor_fusion.2.places, bf16[2,2,4,128,256]{4,3,2,1,0:T(8,128)(2,1)S(1)} %pad_maximum_fusion.own.refs_0_.refs_1_, bf16[2,2,4,128,256]{4,3,2,1,0:T(8,128)(2,1)S(1)} %pad_maximum_fusion.own.refs_0_.refs_1_, ...), custom_call_target="tpu_custom_call" | custom-call | tf_op jit(solution)/shard_map/pallas_call | solution.py:83
  41.8 1.0 collective-permute-start
  42.8 0.1 add_convert_fusion.places
  42.9 1.6 %shard_map.28.refs_0_ = bf16[2,4,2,128,128]{4,3,2,1,0:T(8,128)(2,1)S(1)} custom-call(s32[2]{0:T(128)S(1)} %add_convert_fusion.places, bf16[2,2,4,128,256]{4,3,2,1,0:T(8,128)(2,1)S(1)} %pad_maximum_fusion.own.refs_0_.refs_1_, bf16[2,2,4,128,256]{4,3,2,1,0:T(8,128)(2,1)S(1)} %pad_maximum_fusion.own.refs_0_.refs_1_, ...), custom_call_target="tpu_custom_call" | custom-call | tf_op jit(solution)/shard_map/pallas_call | solution.py:83
  44.5 0.8 copy-done.3
  45.3 11.0 %collective-permute-done.refs_1_ = bf16[2,4,2,128,128]{4,3,2,1,0:T(8,128)(2,1)S(1)} collective-permute-done((bf16[2,4,2,128,128]{4,3,2,1,0:T(8,128)(2,1)S(1)}, bf16[2,4,2,128,128]{4,3,2,1,0:T(8,128)(2,1)S(1)}, u32[]{:S(2)}, u32[]{:S(2)}) %collective-permute-start) | collective-permute-done | bytes 524320 | tf_op jit(solution)/shard_map/ppermute | solution.py:21
  56.3 0.8 copy-done.7
  57.1 4.9 %collective-permute-done.2.refs_1_.own = bf16[2,2,4,128,256]{4,3,2,1,0:T(8,128)(2,1)S(1)} collective-permute-done((bf16[2,2,4,128,256]{4,3,2,1,0:T(8,128)(2,1)S(1)}, bf16[2,2,4,128,256]{4,3,2,1,0:T(8,128)(2,1)S(1)}, u32[]{:S(2)}, u32[]{:S(2)}) %collective-permute-start.2) | collective-permute-done | bytes 1048608 | tf_op jit(solution)/shard_map/ppermute | solution.py:21
  62.0 3.5 %collective-permute-done.1.refs_0_.own = bf16[2,2,4,128,256]{4,3,2,1,0:T(8,128)(2,1)} collective-permute-done((bf16[2,2,4,128,256]{4,3,2,1,0:T(8,128)(2,1)S(1)}, bf16[2,2,4,128,256]{4,3,2,1,0:T(8,128)(2,1)}, u32[]{:S(2)}, u32[]{:S(2)}) %collective-permute-start.1) | collective-permute-done | bytes 1048608 | tf_op jit(solution)/shard_map/ppermute | solution.py:21
  65.6 0.0 collective-permute-start.4
  65.6 3.2 %collective-permute-start.5 = (bf16[2,2,4,128,256]{4,3,2,1,0:T(8,128)(2,1)S(1)}, bf16[2,2,4,128,256]{4,3,2,1,0:T(8,128)(2,1)}, u32[]{:S(2)}, u32[]{:S(2)}) collective-permute-start(bf16[2,2,4,128,256]{4,3,2,1,0:T(8,128)(2,1)S(1)} %collective-permute-done.2.refs_1_.own), channel_id=1, source_target_pairs={{0,7},{1,0},{2,1},{3,2},{4,3},{5,4},{6,5},{7,6},{8,15},{9,8},{10,9... | collective-permute-start | bytes 3145736 | tf_op jit(solution)/shard_map/ppermute | solution.py:21
  68.8 0.1 broadcast_xor_fusion.1
  68.9 2.5 %shard_map.31 = bf16[2,4,2,128,128]{4,3,2,1,0:T(8,128)(2,1)S(1)} custom-call(s32[2]{0:T(128)S(1)} %get-tuple-element.57.places, bf16[2,2,4,128,256]{4,3,2,1,0:T(8,128)(2,1)S(1)} %pad_maximum_fusion.own.refs_0_.refs_1_, bf16[2,2,4,128,256]{4,3,2,1,0:T(8,128)(2,1)} %collective-permute-done.1.refs_0_.own, ...), custom_call_target="tpu_custom_call" | custom-call | tf_op jit(solution)/shard_map/pallas_call | solution.py:83
  71.3 2.0 %collective-permute-start.3 = (bf16[2,4,2,128,128]{4,3,2,1,0:T(8,128)(2,1)S(1)}, bf16[2,4,2,128,128]{4,3,2,1,0:T(8,128)(2,1)S(1)}, u32[]{:S(2)}, u32[]{:S(2)}) collective-permute-start(bf16[2,4,2,128,128]{4,3,2,1,0:T(8,128)(2,1)S(1)} %shard_map.31), channel_id=1, source_target_pairs={{0,8},{1,9},{2,10},{3,11},{4,12},{5,13},{6,14},{7,15},{8,0},{9,1},... | collective-permute-start | bytes 1572872 | tf_op jit(solution)/shard_map/ppermute | solution.py:21
  73.4 2.5 %shard_map.30.refs_2_ = bf16[2,4,2,128,128]{4,3,2,1,0:T(8,128)(2,1)S(1)} custom-call(s32[2]{0:T(128)S(1)} %get-tuple-element.58.places, bf16[2,2,4,128,256]{4,3,2,1,0:T(8,128)(2,1)S(1)} %pad_maximum_fusion.own.refs_0_.refs_1_, bf16[2,2,4,128,256]{4,3,2,1,0:T(8,128)(2,1)} %collective-permute-done.1.refs_0_.own, ...), custom_call_target="tpu_custom_call" | custom-call | tf_op jit(solution)/shard_map/pallas_call | solution.py:83
  75.8 0.0 copy-done.1
  75.8 0.0 copy-start.5
  75.8 0.8 copy-done.5
  76.6 7.9 %collective-permute-done.3.refs_3_ = bf16[2,4,2,128,128]{4,3,2,1,0:T(8,128)(2,1)S(1)} collective-permute-done((bf16[2,4,2,128,128]{4,3,2,1,0:T(8,128)(2,1)S(1)}, bf16[2,4,2,128,128]{4,3,2,1,0:T(8,128)(2,1)S(1)}, u32[]{:S(2)}, u32[]{:S(2)}) %collective-permute-start.3) | collective-permute-done | bytes 524320 | tf_op jit(solution)/shard_map/ppermute | solution.py:21
  84.6 0.8 copy-done.9
  85.4 5.0 %collective-permute-done.4.refs_0_ = bf16[2,2,4,128,256]{4,3,2,1,0:T(8,128)(2,1)} collective-permute-done((bf16[2,2,4,128,256]{4,3,2,1,0:T(8,128)(2,1)}, bf16[2,2,4,128,256]{4,3,2,1,0:T(8,128)(2,1)}, u32[]{:S(2)}, u32[]{:S(2)}) %collective-permute-start.4) | collective-permute-done | bytes 1048608 | tf_op jit(solution)/shard_map/ppermute | solution.py:21
  90.4 0.0 collective-permute-done.5.refs_1_.refs_0_
  90.4 0.0 collective-permute-start.9
  90.4 0.1 broadcast_xor_fusion
  90.4 3.2 %shard_map.33 = bf16[2,4,2,128,128]{4,3,2,1,0:T(8,128)(2,1)} custom-call(s32[2]{0:T(128)S(1)} %get-tuple-element.55.places, bf16[2,2,4,128,256]{4,3,2,1,0:T(8,128)(2,1)S(1)} %pad_maximum_fusion.own.refs_0_.refs_1_, bf16[2,2,4,128,256]{4,3,2,1,0:T(8,128)(2,1)} %collective-permute-done.4.refs_0_, ...), custom_call_target="tpu_custom_call" | custom-call | tf_op jit(solution)/shard_map/pallas_call | solution.py:83
  93.7 2.6 %collective-permute-start.6 = (bf16[2,4,2,128,128]{4,3,2,1,0:T(8,128)(2,1)}, bf16[2,4,2,128,128]{4,3,2,1,0:T(8,128)(2,1)}, u32[]{:S(2)}, u32[]{:S(2)}) collective-permute-start(bf16[2,4,2,128,128]{4,3,2,1,0:T(8,128)(2,1)} %shard_map.33), channel_id=1, source_target_pairs={{0,8},{1,9},{2,10},{3,11},{4,12},{5,13},{6,14},{7,15},{8,0},{9,1},... | collective-permute-start | bytes 1572872 | tf_op jit(solution)/shard_map/ppermute | solution.py:21
  96.3 2.3 %shard_map.34 = bf16[1,4,2,128,128]{4,3,2,1,0:T(8,128)(2,1)} custom-call(s32[1]{0:T(128)} %bitcast.17.places, bf16[2,2,4,128,256]{4,3,2,1,0:T(8,128)(2,1)} %collective-permute-done.1.refs_0_.own, bf16[2,2,4,128,256]{4,3,2,1,0:T(8,128)(2,1)} %collective-permute-done.5.refs_1_.refs_0_), custom_call_target="tpu_custom_call" | custom-call | tf_op jit(solution)/shard_map/pallas_call | solution.py:83
  98.6 2.3 %shard_map.35 = bf16[1,4,2,128,128]{4,3,2,1,0:T(8,128)(2,1)} custom-call(s32[1]{0:T(128)S(6)} %xor.21.places, bf16[2,2,4,128,256]{4,3,2,1,0:T(8,128)(2,1)} %collective-permute-done.1.refs_0_.own, bf16[2,2,4,128,256]{4,3,2,1,0:T(8,128)(2,1)} %collective-permute-done.5.refs_1_.refs_0_), custom_call_target="tpu_custom_call" | custom-call | tf_op jit(solution)/shard_map/pallas_call | solution.py:83
  100.9 3.2 %collective-permute-start.7 = (bf16[1,4,2,128,128]{4,3,2,1,0:T(8,128)(2,1)}, bf16[1,4,2,128,128]{4,3,2,1,0:T(8,128)(2,1)S(1)}, u32[]{:S(2)}, u32[]{:S(2)}) collective-permute-start(bf16[1,4,2,128,128]{4,3,2,1,0:T(8,128)(2,1)} %shard_map.34), channel_id=1, source_target_pairs={{0,7},{1,0},{2,1},{3,2},{4,3},{5,4},{6,5},{7,6},{8,15},{9,8},{10,9... | collective-permute-start | bytes 786440 | tf_op jit(solution)/shard_map/ppermute | solution.py:21
  104.2 1.9 %collective-permute-start.8 = (bf16[1,4,2,128,128]{4,3,2,1,0:T(8,128)(2,1)}, bf16[1,4,2,128,128]{4,3,2,1,0:T(8,128)(2,1)}, u32[]{:S(2)}, u32[]{:S(2)}) collective-permute-start(bf16[1,4,2,128,128]{4,3,2,1,0:T(8,128)(2,1)} %shard_map.35), channel_id=1, source_target_pairs={{0,15},{1,8},{2,9},{3,10},{4,11},{5,12},{6,13},{7,14},{8,7},{9,0},... | collective-permute-start | bytes 786440 | tf_op jit(solution)/shard_map/ppermute | solution.py:21
  106.0 2.5 %shard_map.32.refs_4_ = bf16[2,4,2,128,128]{4,3,2,1,0:T(8,128)(2,1)S(1)} custom-call(s32[2]{0:T(128)S(1)} %get-tuple-element.56.places, bf16[2,2,4,128,256]{4,3,2,1,0:T(8,128)(2,1)S(1)} %pad_maximum_fusion.own.refs_0_.refs_1_, bf16[2,2,4,128,256]{4,3,2,1,0:T(8,128)(2,1)} %collective-permute-done.4.refs_0_, ...), custom_call_target="tpu_custom_call" | custom-call | tf_op jit(solution)/shard_map/pallas_call | solution.py:83
  108.6 2.0 %collective-permute-done.7.refs_4_ = bf16[1,4,2,128,128]{4,3,2,1,0:T(8,128)(2,1)S(1)} collective-permute-done((bf16[1,4,2,128,128]{4,3,2,1,0:T(8,128)(2,1)}, bf16[1,4,2,128,128]{4,3,2,1,0:T(8,128)(2,1)S(1)}, u32[]{:S(2)}, u32[]{:S(2)}) %collective-permute-start.7) | collective-permute-done | bytes 262176 | tf_op jit(solution)/shard_map/ppermute | solution.py:21
  110.6 2.9 %collective-permute-done.8.refs_5_ = bf16[1,4,2,128,128]{4,3,2,1,0:T(8,128)(2,1)} collective-permute-done((bf16[1,4,2,128,128]{4,3,2,1,0:T(8,128)(2,1)}, bf16[1,4,2,128,128]{4,3,2,1,0:T(8,128)(2,1)}, u32[]{:S(2)}, u32[]{:S(2)}) %collective-permute-start.8) | collective-permute-done | bytes 262176 | tf_op jit(solution)/shard_map/ppermute | solution.py:21
  113.6 0.0 collective-permute-done.6.refs_5_
  113.6 0.6 collective-permute-done.9.refs_0_
  114.1 0.7 shard_map.38
  114.9 0.7 shard_map.39
  115.6 0.0 copy-start.4
  115.7 0.3 collective-permute-start.11
  115.9 4.0 %collective-permute-start.12 = (bf16[1,4,2,128,128]{4,3,2,1,0:T(8,128)(2,1)S(1)}, bf16[1,4,2,128,128]{4,3,2,1,0:T(8,128)(2,1)S(1)}, u32[]{:S(2)}, u32[]{:S(2)}) collective-permute-start(bf16[1,4,2,128,128]{4,3,2,1,0:T(8,128)(2,1)S(1)} %shard_map.39), channel_id=1, source_target_pairs={{0,9},{1,10},{2,11},{3,12},{4,13},{5,14},{6,15},{7,8},{8,1},{9,2},... | collective-permute-start | bytes 786440 | tf_op jit(solution)/shard_map/ppermute | solution.py:21
  120.0 0.7 shard_map.37
  120.7 0.4 collective-permute-start.10
  121.1 0.7 shard_map.36.refs_0_
  121.9 3.8 %shard_map.40.refs_6_ = bf16[8,1,9,2,128,128]{5,4,3,2,1,0:T(8,128)(2,1)} custom-call(s32[1]{0:T(128)} %bitcast.column, bf16[2,4,2,128,128]{4,3,2,1,0:T(8,128)(2,1)S(1)} %copy-done.4, bf16[2,4,2,128,128]{4,3,2,1,0:T(8,128)(2,1)S(1)} %copy-done.8, bf16[2,4,2,128,128]{4,3,2,1,0:T(8,128)(2,1)S(1)} %copy-done.6, bf16[2,4,2,128,128]{4,3,2,1,0:T(8,128)(2,1)S(1)} %copy-done.10, ...), custom_call_target="tpu_custom_call" | custom-call | tf_op jit(solution)/shard_map/pallas_call | solution.py:126
  125.7 0.0 collective-permute-done.11.refs_2_
  125.7 5.4 %collective-permute-done.12.refs_3_ = bf16[1,4,2,128,128]{4,3,2,1,0:T(8,128)(2,1)S(1)} collective-permute-done((bf16[1,4,2,128,128]{4,3,2,1,0:T(8,128)(2,1)S(1)}, bf16[1,4,2,128,128]{4,3,2,1,0:T(8,128)(2,1)S(1)}, u32[]{:S(2)}, u32[]{:S(2)}) %collective-permute-start.12) | collective-permute-done | bytes 262176 | tf_op jit(solution)/shard_map/ppermute | solution.py:21
  131.2 1.1 collective-permute-done.10.refs_1_
  132.2 2.2 %shard_map.41 = bf16[8,1,9,2,128,128]{5,4,3,2,1,0:T(8,128)(2,1)} custom-call(s32[1]{0:T(128)} %bitcast.column, bf16[1,4,2,128,128]{4,3,2,1,0:T(8,128)(2,1)S(1)} %shard_map.36.refs_0_, bf16[1,4,2,128,128]{4,3,2,1,0:T(8,128)(2,1)S(1)} %collective-permute-done.10.refs_1_, ...), custom_call_target="tpu_custom_call", output_to_operand_aliasing={{}: (7, {})} | custom-call | tf_op jit(solution)/shard_map/pallas_call | solution.py:126
  (15 shorter events, 0.0 us)
Async XLA Ops:
  0.0 3.7 %copy-start = (bf16[1,8,69376]{2,1,0:T(8,128)(2,1)S(1)}, bf16[1,8,69376]{2,1,0:T(8,128)(2,1)}, u32[]{:S(2)}) copy-start(bf16[1,8,69376]{2,1,0:T(8,128)(2,1)} %param.2) | copy-start | bytes 3330052
  10.4 23.4 %all-to-all-start = ((bf16[32,2,4,8,256]{4,3,2,1,0:T(8,128)(2,1)}), bf16[32,2,4,8,256]{4,3,2,1,0:T(8,128)(2,1)S(1)}, u32[]{:S(2)}, u32[]{:S(2)}) async-start(bf16[32,2,4,8,256]{4,3,2,1,0:T(8,128)(2,1)} %bitcast.5), calls=%async_computation | async-start | bytes 2097152 | tf_op jit(solution)/shard_map/all_to_all | solution.py:151
  34.1 27.9 %collective-permute-start.2 = (bf16[2,2,4,128,256]{4,3,2,1,0:T(8,128)(2,1)S(1)}, bf16[2,2,4,128,256]{4,3,2,1,0:T(8,128)(2,1)S(1)}, u32[]{:S(2)}, u32[]{:S(2)}) collective-permute-start(bf16[2,2,4,128,256]{4,3,2,1,0:T(8,128)(2,1)S(1)} %pad_maximum_fusion.own.refs_0_.refs_1_), channel_id=1, source_target_pairs={{0,7},{1,0},{2,1},{3,2},{4,3},{5,4},{6,5},{7,6},{8,15},{9,8},{10,9... | collective-permute-start | bytes 3145736 | tf_op jit(solution)/shard_map/ppermute | solution.py:21
  40.1 25.5 %collective-permute-start.1 = (bf16[2,2,4,128,256]{4,3,2,1,0:T(8,128)(2,1)S(1)}, bf16[2,2,4,128,256]{4,3,2,1,0:T(8,128)(2,1)}, u32[]{:S(2)}, u32[]{:S(2)}) collective-permute-start(bf16[2,2,4,128,256]{4,3,2,1,0:T(8,128)(2,1)S(1)} %pad_maximum_fusion.own.refs_0_.refs_1_), channel_id=1, source_target_pairs={{0,1},{1,2},{2,3},{3,4},{4,5},{5,6},{6,7},{7,0},{8,9},{9,10},{10,1... | collective-permute-start | bytes 3145736 | tf_op jit(solution)/shard_map/ppermute | solution.py:21
  41.8 14.5 %collective-permute-start = (bf16[2,4,2,128,128]{4,3,2,1,0:T(8,128)(2,1)S(1)}, bf16[2,4,2,128,128]{4,3,2,1,0:T(8,128)(2,1)S(1)}, u32[]{:S(2)}, u32[]{:S(2)}) collective-permute-start(bf16[2,4,2,128,128]{4,3,2,1,0:T(8,128)(2,1)S(1)} %shard_map.29), channel_id=1, source_target_pairs={{0,8},{1,9},{2,10},{3,11},{4,12},{5,13},{6,14},{7,15},{8,0},{9,1},... | collective-permute-start | bytes 1572872 | tf_op jit(solution)/shard_map/ppermute | solution.py:21
  44.5 0.8 copy-start.3
  56.3 0.8 copy-start.7
  62.0 13.8 %copy-start.1 = (bf16[2,2,4,128,256]{4,3,2,1,0:T(8,128)(2,1)}, bf16[2,2,4,128,256]{4,3,2,1,0:T(8,128)(2,1)S(1)}, u32[]{:S(2)}) copy-start(bf16[2,2,4,128,256]{4,3,2,1,0:T(8,128)(2,1)S(1)} %collective-permute-done.2.refs_1_.own) | copy-start | bytes 3145732
  65.6 24.8 %collective-permute-start.4 = (bf16[2,2,4,128,256]{4,3,2,1,0:T(8,128)(2,1)}, bf16[2,2,4,128,256]{4,3,2,1,0:T(8,128)(2,1)}, u32[]{:S(2)}, u32[]{:S(2)}) collective-permute-start(bf16[2,2,4,128,256]{4,3,2,1,0:T(8,128)(2,1)} %collective-permute-done.1.refs_0_.own), channel_id=1, source_target_pairs={{0,1},{1,2},{2,3},{3,4},{4,5},{5,6},{6,7},{7,0},{8,9},{9,10},{10,1... | collective-permute-start | bytes 3145736 | tf_op jit(solution)/shard_map/ppermute | solution.py:21
  65.6 24.8 %collective-permute-start.5 = (bf16[2,2,4,128,256]{4,3,2,1,0:T(8,128)(2,1)S(1)}, bf16[2,2,4,128,256]{4,3,2,1,0:T(8,128)(2,1)}, u32[]{:S(2)}, u32[]{:S(2)}) collective-permute-start(bf16[2,2,4,128,256]{4,3,2,1,0:T(8,128)(2,1)S(1)} %collective-permute-done.2.refs_1_.own), channel_id=1, source_target_pairs={{0,7},{1,0},{2,1},{3,2},{4,3},{5,4},{6,5},{7,6},{8,15},{9,8},{10,9... | collective-permute-start | bytes 3145736 | tf_op jit(solution)/shard_map/ppermute | solution.py:21
  71.3 13.2 %collective-permute-start.3 = (bf16[2,4,2,128,128]{4,3,2,1,0:T(8,128)(2,1)S(1)}, bf16[2,4,2,128,128]{4,3,2,1,0:T(8,128)(2,1)S(1)}, u32[]{:S(2)}, u32[]{:S(2)}) collective-permute-start(bf16[2,4,2,128,128]{4,3,2,1,0:T(8,128)(2,1)S(1)} %shard_map.31), channel_id=1, source_target_pairs={{0,8},{1,9},{2,10},{3,11},{4,12},{5,13},{6,14},{7,15},{8,0},{9,1},... | collective-permute-start | bytes 1572872 | tf_op jit(solution)/shard_map/ppermute | solution.py:21
  75.8 0.8 copy-start.5
  84.6 0.8 copy-start.9
  90.4 23.8 %collective-permute-start.9 = (bf16[2,2,4,128,256]{4,3,2,1,0:T(8,128)(2,1)}, bf16[2,2,4,128,256]{4,3,2,1,0:T(8,128)(2,1)S(1)}, u32[]{:S(2)}, u32[]{:S(2)}) collective-permute-start(bf16[2,2,4,128,256]{4,3,2,1,0:T(8,128)(2,1)} %collective-permute-done.4.refs_0_), channel_id=1, source_target_pairs={{0,1},{1,2},{2,3},{3,4},{4,5},{5,6},{6,7},{7,0},{8,9},{9,10},{10,1... | collective-permute-start | bytes 3145736 | tf_op jit(solution)/shard_map/ppermute | solution.py:21
  93.7 19.9 %collective-permute-start.6 = (bf16[2,4,2,128,128]{4,3,2,1,0:T(8,128)(2,1)}, bf16[2,4,2,128,128]{4,3,2,1,0:T(8,128)(2,1)}, u32[]{:S(2)}, u32[]{:S(2)}) collective-permute-start(bf16[2,4,2,128,128]{4,3,2,1,0:T(8,128)(2,1)} %shard_map.33), channel_id=1, source_target_pairs={{0,8},{1,9},{2,10},{3,11},{4,12},{5,13},{6,14},{7,15},{8,0},{9,1},... | collective-permute-start | bytes 1572872 | tf_op jit(solution)/shard_map/ppermute | solution.py:21
  100.9 9.7 %collective-permute-start.7 = (bf16[1,4,2,128,128]{4,3,2,1,0:T(8,128)(2,1)}, bf16[1,4,2,128,128]{4,3,2,1,0:T(8,128)(2,1)S(1)}, u32[]{:S(2)}, u32[]{:S(2)}) collective-permute-start(bf16[1,4,2,128,128]{4,3,2,1,0:T(8,128)(2,1)} %shard_map.34), channel_id=1, source_target_pairs={{0,7},{1,0},{2,1},{3,2},{4,3},{5,4},{6,5},{7,6},{8,15},{9,8},{10,9... | collective-permute-start | bytes 786440 | tf_op jit(solution)/shard_map/ppermute | solution.py:21
  104.2 9.4 %collective-permute-start.8 = (bf16[1,4,2,128,128]{4,3,2,1,0:T(8,128)(2,1)}, bf16[1,4,2,128,128]{4,3,2,1,0:T(8,128)(2,1)}, u32[]{:S(2)}, u32[]{:S(2)}) collective-permute-start(bf16[1,4,2,128,128]{4,3,2,1,0:T(8,128)(2,1)} %shard_map.35), channel_id=1, source_target_pairs={{0,15},{1,8},{2,9},{3,10},{4,11},{5,12},{6,13},{7,14},{8,7},{9,0},... | collective-permute-start | bytes 786440 | tf_op jit(solution)/shard_map/ppermute | solution.py:21
  106.0 8.1 %copy-start.2 = (bf16[2,2,4,128,256]{4,3,2,1,0:T(8,128)(2,1)S(1)}, bf16[2,2,4,128,256]{4,3,2,1,0:T(8,128)(2,1)}, u32[]{:S(2)}) copy-start(bf16[2,2,4,128,256]{4,3,2,1,0:T(8,128)(2,1)} %copy-done.1) | copy-start | bytes 3145732
  115.6 6.3 %copy-start.4 = (bf16[2,4,2,128,128]{4,3,2,1,0:T(8,128)(2,1)S(1)}, bf16[2,4,2,128,128]{4,3,2,1,0:T(8,128)(2,1)}, u32[]{:S(2)}) copy-start(bf16[2,4,2,128,128]{4,3,2,1,0:T(8,128)(2,1)} %copy-done.3) | copy-start | bytes 1572868
  115.6 6.3 %copy-start.6 = (bf16[2,4,2,128,128]{4,3,2,1,0:T(8,128)(2,1)S(1)}, bf16[2,4,2,128,128]{4,3,2,1,0:T(8,128)(2,1)}, u32[]{:S(2)}) copy-start(bf16[2,4,2,128,128]{4,3,2,1,0:T(8,128)(2,1)} %copy-done.5) | copy-start | bytes 1572868
  115.6 6.3 %copy-start.8 = (bf16[2,4,2,128,128]{4,3,2,1,0:T(8,128)(2,1)S(1)}, bf16[2,4,2,128,128]{4,3,2,1,0:T(8,128)(2,1)}, u32[]{:S(2)}) copy-start(bf16[2,4,2,128,128]{4,3,2,1,0:T(8,128)(2,1)} %copy-done.7) | copy-start | bytes 1572868
  115.6 6.3 %copy-start.10 = (bf16[2,4,2,128,128]{4,3,2,1,0:T(8,128)(2,1)S(1)}, bf16[2,4,2,128,128]{4,3,2,1,0:T(8,128)(2,1)}, u32[]{:S(2)}) copy-start(bf16[2,4,2,128,128]{4,3,2,1,0:T(8,128)(2,1)} %copy-done.9) | copy-start | bytes 1572868
  115.7 10.1 %collective-permute-start.11 = (bf16[1,4,2,128,128]{4,3,2,1,0:T(8,128)(2,1)S(1)}, bf16[1,4,2,128,128]{4,3,2,1,0:T(8,128)(2,1)S(1)}, u32[]{:S(2)}, u32[]{:S(2)}) collective-permute-start(bf16[1,4,2,128,128]{4,3,2,1,0:T(8,128)(2,1)S(1)} %shard_map.38), channel_id=1, source_target_pairs={{0,1},{1,2},{2,3},{3,4},{4,5},{5,6},{6,7},{7,0},{8,9},{9,10},{10,1... | collective-permute-start | bytes 786440 | tf_op jit(solution)/shard_map/ppermute | solution.py:21
  115.9 15.2 %collective-permute-start.12 = (bf16[1,4,2,128,128]{4,3,2,1,0:T(8,128)(2,1)S(1)}, bf16[1,4,2,128,128]{4,3,2,1,0:T(8,128)(2,1)S(1)}, u32[]{:S(2)}, u32[]{:S(2)}) collective-permute-start(bf16[1,4,2,128,128]{4,3,2,1,0:T(8,128)(2,1)S(1)} %shard_map.39), channel_id=1, source_target_pairs={{0,9},{1,10},{2,11},{3,12},{4,13},{5,14},{6,15},{7,8},{8,1},{9,2},... | collective-permute-start | bytes 786440 | tf_op jit(solution)/shard_map/ppermute | solution.py:21
  120.7 11.5 %collective-permute-start.10 = (bf16[1,4,2,128,128]{4,3,2,1,0:T(8,128)(2,1)S(1)}, bf16[1,4,2,128,128]{4,3,2,1,0:T(8,128)(2,1)S(1)}, u32[]{:S(2)}, u32[]{:S(2)}) collective-permute-start(bf16[1,4,2,128,128]{4,3,2,1,0:T(8,128)(2,1)S(1)} %shard_map.37), channel_id=1, source_target_pairs={{0,8},{1,9},{2,10},{3,11},{4,12},{5,13},{6,14},{7,15},{8,0},{9,1},... | collective-permute-start | bytes 786440 | tf_op jit(solution)/shard_map/ppermute | solution.py:21

commit v7 on v6

--- a/solution.py
+++ b/solution.py
@@ -78,19 +78,19 @@
 def visibilities(own, partners, swaps, block):
     _, _, chans, tile, spectra = own.shape
     count = len(partners)
-    shape = (2, 1, 2, tile, spectra)
+    shape = (2, 1, chans, tile, spectra)
     places = jnp.stack(swaps).astype(jnp.int32) ^ block
     return pl.pallas_call(
         visibility_kernel,
         grid_spec=pltpu.PrefetchScalarGridSpec(
             num_scalar_prefetch=1,
-            grid=(chans // 2,),
+            grid=(1,),
             in_specs=[pl.BlockSpec(shape, lambda chan, _: (0, block, chan, 0, 0))]
             + [
                 pl.BlockSpec(shape, lambda chan, at, index=index: (0, at[index], chan, 0, 0))
                 for index in range(count)
             ],
-            out_specs=pl.BlockSpec((count, 2, 2, tile, tile), lambda chan, _: (0, chan, 0, 0, 0)),
+            out_specs=pl.BlockSpec((count, chans, 2, tile, tile), lambda chan, _: (0, chan, 0, 0, 0)),
         ),
         out_shape=jax.ShapeDtypeStruct((count, chans, 2, tile, tile), jnp.bfloat16),
         compiler_params=pltpu.CompilerParams(vmem_limit_bytes=24 * 1024 * 1024),

time: 135 us -> 134 us (level)
  Pallas kernels: 27.5 us -> 25.3 us
  waiting for transfers between devices: 60.3 us -> 61.8 us
    pallas_call x12, Pallas kernels: 21.5 us -> 19.3 us  [visibilities(): pl.pallas_call(visibility_kernel, grid_spec=pltpu.PrefetchScalarGridSpec(...]
    ppermute x13, waiting for transfers between devices: 44.4 us -> 46 us  [along_ring(): return lax.ppermute(value, ('column', 'plane'), pairs)]
  transfers between devices with their start and end apart: 14 -> 14, of which waited for: 11 -> 12; matrix products, arithmetic and copies ran while one was open for 0% -> 0% of each run, Pallas kernels for 18% -> 17%
where the time goes in v7:
time: 134 us
  waiting for transfers between devices  61.8 us (46%)
  starting transfers between devices  32.2 us (24%)
  Pallas kernels  25.3 us (19%)
  local copies, waits for them, and re-layouts  6.33 us (5%)
  matrix products  4.59 us (3%)
  other arithmetic  2.55 us (2%)
    ppermute x13, waiting for transfers between devices, along_ring(): return lax.ppermute(value, ('column', 'plane'), pairs)  46 us
    ppermute x13, starting transfers between devices, along_ring(): return lax.ppermute(value, ('column', 'plane'), pairs)  24.6 us
    pallas_call x12, Pallas kernels, visibilities(): pl.pallas_call(visibility_kernel, grid_spec=pltpu.PrefetchScalarGridSpec(...  19.3 us
    all_to_all x1, waiting for transfers between devices, body(): lax.all_to_all(voltages, ('freq', 'column'), split_axis=0, concat_axis=0,...  15.8 us
    all_to_all x1, starting transfers between devices, body(): lax.all_to_all(voltages, ('freq', 'column'), split_axis=0, concat_axis=0,...  7.56 us
    pallas_call x2, Pallas kernels, placed(): pl.pallas_call(placement_kernel, grid_spec=pltpu.PrefetchScalarGridSpec(n...  5.99 us
    conv_general_dilated x1, matrix products, channelize(): lax.conv_general_dilated(frames, filters, window_strides=(1,), padding='V...  4.59 us
    unnamed x22, local copies, waits for them, and re-layouts  3.22 us
  transfers between devices with their start and end apart: 14, of which 12 were waited for; matrix products, arithmetic and copies ran while one was open for 0% of the time, Pallas kernels for 17%

profile of v7, /device:TPU:6, one launch (start us, length us, event | category | flops | bytes accessed | tf_op | source)
XLA Modules:
  0.0 133.7 jit_solution(6506088007485242378)
XLA Ops:
  0.0 0.7 fusion.17
  1.4 0.1 fusion.9
  1.6 0.8 mul.110
  2.3 1.2 fusion.7
  3.6 0.1 maximum_bitcast_fusion
  3.6 0.1 mul.116
  3.7 4.6 %fusion.3 = bf16[256,8,256]{0,1,2:T(8,128)(2,1)S(1)} fusion(bf16[8,271,256]{2,0,1:T(8,128)(2,1)S(1)} %bitcast.27, f32[256,256]{1,0:T(8,128)S(1)} %mul.116, f32[16,256]{1,0:T(8,128)S(1)} %fusion.9), kind=kOutput, calls=%fused_computation.4 | convolution fusion | flops 4297588736 | bytes 2437120 | tf_op jit(solution)/shard_map/conv_general_dilated | solution.py:46
  8.3 2.0 %copy.6 = bf16[256,8,256]{2,1,0:T(8,128)(2,1)} copy(bf16[256,8,256]{0,1,2:T(8,128)(2,1)S(1)} %fusion.3) | data formatting | bytes 2097152 | tf_op jit(solution)/shard_map/convert_element_type | solution.py:53
  10.4 7.6 %all-to-all-start = ((bf16[32,2,4,8,256]{4,3,2,1,0:T(8,128)(2,1)}), bf16[32,2,4,8,256]{4,3,2,1,0:T(8,128)(2,1)S(1)}, u32[]{:S(2)}, u32[]{:S(2)}) async-start(bf16[32,2,4,8,256]{4,3,2,1,0:T(8,128)(2,1)} %bitcast.5), calls=%async_computation | async-start | bytes 2097152 | tf_op jit(solution)/shard_map/all_to_all | solution.py:151
  18.0 15.8 %all-to-all-done = bf16[32,2,4,8,256]{4,3,2,1,0:T(8,128)(2,1)S(1)} async-done(((bf16[32,2,4,8,256]{4,3,2,1,0:T(8,128)(2,1)}), bf16[32,2,4,8,256]{4,3,2,1,0:T(8,128)(2,1)S(1)}, u32[]{:S(2)}, u32[]{:S(2)}) %all-to-all-start) | async-done | bytes 1048608 | tf_op jit(solution)/shard_map/all_to_all | solution.py:151
  33.8 0.1 constant_dynamic-slice_fusion.1
  33.9 0.1 copy_bitcast_fusion
  34.0 0.1 pad_maximum_fusion.own.refs_0_.refs_1_
  34.1 5.9 %collective-permute-start.2 = (bf16[2,2,4,128,256]{4,3,2,1,0:T(8,128)(2,1)S(1)}, bf16[2,2,4,128,256]{4,3,2,1,0:T(8,128)(2,1)S(1)}, u32[]{:S(2)}, u32[]{:S(2)}) collective-permute-start(bf16[2,2,4,128,256]{4,3,2,1,0:T(8,128)(2,1)S(1)} %pad_maximum_fusion.own.refs_0_.refs_1_), channel_id=1, source_target_pairs={{0,7},{1,0},{2,1},{3,2},{4,3},{5,4},{6,5},{7,6},{8,15},{9,8},{10,9... | collective-permute-start | bytes 3145736 | tf_op jit(solution)/shard_map/ppermute | solution.py:21
  40.1 0.0 collective-permute-start.1
  40.1 0.1 broadcast_xor_fusion.2.places
  40.1 1.2 shard_map.29
  41.4 1.0 collective-permute-start
  42.4 0.1 add_convert_fusion.places
  42.5 1.2 shard_map.28.refs_0_
  43.7 0.8 copy-done.3
  44.5 11.4 %collective-permute-done.refs_1_ = bf16[2,4,2,128,128]{4,3,2,1,0:T(8,128)(2,1)S(1)} collective-permute-done((bf16[2,4,2,128,128]{4,3,2,1,0:T(8,128)(2,1)S(1)}, bf16[2,4,2,128,128]{4,3,2,1,0:T(8,128)(2,1)S(1)}, u32[]{:S(2)}, u32[]{:S(2)}) %collective-permute-start) | collective-permute-done | bytes 524320 | tf_op jit(solution)/shard_map/ppermute | solution.py:21
  55.9 0.8 copy-done.7
  56.7 5.3 %collective-permute-done.2.refs_1_.own = bf16[2,2,4,128,256]{4,3,2,1,0:T(8,128)(2,1)S(1)} collective-permute-done((bf16[2,2,4,128,256]{4,3,2,1,0:T(8,128)(2,1)S(1)}, bf16[2,2,4,128,256]{4,3,2,1,0:T(8,128)(2,1)S(1)}, u32[]{:S(2)}, u32[]{:S(2)}) %collective-permute-start.2) | collective-permute-done | bytes 1048608 | tf_op jit(solution)/shard_map/ppermute | solution.py:21
  62.0 3.5 %collective-permute-done.1.refs_0_.own = bf16[2,2,4,128,256]{4,3,2,1,0:T(8,128)(2,1)} collective-permute-done((bf16[2,2,4,128,256]{4,3,2,1,0:T(8,128)(2,1)S(1)}, bf16[2,2,4,128,256]{4,3,2,1,0:T(8,128)(2,1)}, u32[]{:S(2)}, u32[]{:S(2)}) %collective-permute-start.1) | collective-permute-done | bytes 1048608 | tf_op jit(solution)/shard_map/ppermute | solution.py:21
  65.6 0.0 collective-permute-start.4
  65.6 3.2 %collective-permute-start.5 = (bf16[2,2,4,128,256]{4,3,2,1,0:T(8,128)(2,1)S(1)}, bf16[2,2,4,128,256]{4,3,2,1,0:T(8,128)(2,1)}, u32[]{:S(2)}, u32[]{:S(2)}) collective-permute-start(bf16[2,2,4,128,256]{4,3,2,1,0:T(8,128)(2,1)S(1)} %collective-permute-done.2.refs_1_.own), channel_id=1, source_target_pairs={{0,7},{1,0},{2,1},{3,2},{4,3},{5,4},{6,5},{7,6},{8,15},{9,8},{10,9... | collective-permute-start | bytes 3145736 | tf_op jit(solution)/shard_map/ppermute | solution.py:21
  68.8 0.1 broadcast_xor_fusion.1
  68.9 2.3 %shard_map.31 = bf16[2,4,2,128,128]{4,3,2,1,0:T(8,128)(2,1)S(1)} custom-call(s32[2]{0:T(128)S(1)} %get-tuple-element.57.places, bf16[2,2,4,128,256]{4,3,2,1,0:T(8,128)(2,1)S(1)} %pad_maximum_fusion.own.refs_0_.refs_1_, bf16[2,2,4,128,256]{4,3,2,1,0:T(8,128)(2,1)} %collective-permute-done.1.refs_0_.own, ...), custom_call_target="tpu_custom_call" | custom-call | tf_op jit(solution)/shard_map/pallas_call | solution.py:83
  71.2 1.8 %collective-permute-start.3 = (bf16[2,4,2,128,128]{4,3,2,1,0:T(8,128)(2,1)S(1)}, bf16[2,4,2,128,128]{4,3,2,1,0:T(8,128)(2,1)S(1)}, u32[]{:S(2)}, u32[]{:S(2)}) collective-permute-start(bf16[2,4,2,128,128]{4,3,2,1,0:T(8,128)(2,1)S(1)} %shard_map.31), channel_id=1, source_target_pairs={{0,8},{1,9},{2,10},{3,11},{4,12},{5,13},{6,14},{7,15},{8,0},{9,1},... | collective-permute-start | bytes 1572872 | tf_op jit(solution)/shard_map/ppermute | solution.py:21
  73.0 2.3 %shard_map.30.refs_2_ = bf16[2,4,2,128,128]{4,3,2,1,0:T(8,128)(2,1)S(1)} custom-call(s32[2]{0:T(128)S(1)} %get-tuple-element.58.places, bf16[2,2,4,128,256]{4,3,2,1,0:T(8,128)(2,1)S(1)} %pad_maximum_fusion.own.refs_0_.refs_1_, bf16[2,2,4,128,256]{4,3,2,1,0:T(8,128)(2,1)} %collective-permute-done.1.refs_0_.own, ...), custom_call_target="tpu_custom_call" | custom-call | tf_op jit(solution)/shard_map/pallas_call | solution.py:83
  75.4 0.8 copy-done.5
  76.2 8.1 %collective-permute-done.3.refs_3_ = bf16[2,4,2,128,128]{4,3,2,1,0:T(8,128)(2,1)S(1)} collective-permute-done((bf16[2,4,2,128,128]{4,3,2,1,0:T(8,128)(2,1)S(1)}, bf16[2,4,2,128,128]{4,3,2,1,0:T(8,128)(2,1)S(1)}, u32[]{:S(2)}, u32[]{:S(2)}) %collective-permute-start.3) | collective-permute-done | bytes 524320 | tf_op jit(solution)/shard_map/ppermute | solution.py:21
  84.3 0.8 copy-done.9
  85.1 5.3 %collective-permute-done.4.refs_0_ = bf16[2,2,4,128,256]{4,3,2,1,0:T(8,128)(2,1)} collective-permute-done((bf16[2,2,4,128,256]{4,3,2,1,0:T(8,128)(2,1)}, bf16[2,2,4,128,256]{4,3,2,1,0:T(8,128)(2,1)}, u32[]{:S(2)}, u32[]{:S(2)}) %collective-permute-start.4) | collective-permute-done | bytes 1048608 | tf_op jit(solution)/shard_map/ppermute | solution.py:21
  90.4 0.0 collective-permute-done.5.refs_1_.refs_0_
  90.4 0.0 collective-permute-start.9
  90.4 0.1 broadcast_xor_fusion
  90.4 3.3 %shard_map.33 = bf16[2,4,2,128,128]{4,3,2,1,0:T(8,128)(2,1)} custom-call(s32[2]{0:T(128)S(1)} %get-tuple-element.55.places, bf16[2,2,4,128,256]{4,3,2,1,0:T(8,128)(2,1)S(1)} %pad_maximum_fusion.own.refs_0_.refs_1_, bf16[2,2,4,128,256]{4,3,2,1,0:T(8,128)(2,1)} %collective-permute-done.4.refs_0_, ...), custom_call_target="tpu_custom_call" | custom-call | tf_op jit(solution)/shard_map/pallas_call | solution.py:83
  93.7 2.6 %collective-permute-start.6 = (bf16[2,4,2,128,128]{4,3,2,1,0:T(8,128)(2,1)}, bf16[2,4,2,128,128]{4,3,2,1,0:T(8,128)(2,1)}, u32[]{:S(2)}, u32[]{:S(2)}) collective-permute-start(bf16[2,4,2,128,128]{4,3,2,1,0:T(8,128)(2,1)} %shard_map.33), channel_id=1, source_target_pairs={{0,8},{1,9},{2,10},{3,11},{4,12},{5,13},{6,14},{7,15},{8,0},{9,1},... | collective-permute-start | bytes 1572872 | tf_op jit(solution)/shard_map/ppermute | solution.py:21
  96.4 2.3 %shard_map.34 = bf16[1,4,2,128,128]{4,3,2,1,0:T(8,128)(2,1)} custom-call(s32[1]{0:T(128)} %bitcast.17.places, bf16[2,2,4,128,256]{4,3,2,1,0:T(8,128)(2,1)} %collective-permute-done.1.refs_0_.own, bf16[2,2,4,128,256]{4,3,2,1,0:T(8,128)(2,1)} %collective-permute-done.5.refs_1_.refs_0_), custom_call_target="tpu_custom_call" | custom-call | tf_op jit(solution)/shard_map/pallas_call | solution.py:83
  98.7 2.3 %shard_map.35 = bf16[1,4,2,128,128]{4,3,2,1,0:T(8,128)(2,1)} custom-call(s32[1]{0:T(128)S(6)} %xor.21.places, bf16[2,2,4,128,256]{4,3,2,1,0:T(8,128)(2,1)} %collective-permute-done.1.refs_0_.own, bf16[2,2,4,128,256]{4,3,2,1,0:T(8,128)(2,1)} %collective-permute-done.5.refs_1_.refs_0_), custom_call_target="tpu_custom_call" | custom-call | tf_op jit(solution)/shard_map/pallas_call | solution.py:83
  101.1 3.2 %collective-permute-start.7 = (bf16[1,4,2,128,128]{4,3,2,1,0:T(8,128)(2,1)}, bf16[1,4,2,128,128]{4,3,2,1,0:T(8,128)(2,1)S(1)}, u32[]{:S(2)}, u32[]{:S(2)}) collective-permute-start(bf16[1,4,2,128,128]{4,3,2,1,0:T(8,128)(2,1)} %shard_map.34), channel_id=1, source_target_pairs={{0,7},{1,0},{2,1},{3,2},{4,3},{5,4},{6,5},{7,6},{8,15},{9,8},{10,9... | collective-permute-start | bytes 786440 | tf_op jit(solution)/shard_map/ppermute | solution.py:21
  104.3 1.9 %collective-permute-start.8 = (bf16[1,4,2,128,128]{4,3,2,1,0:T(8,128)(2,1)}, bf16[1,4,2,128,128]{4,3,2,1,0:T(8,128)(2,1)}, u32[]{:S(2)}, u32[]{:S(2)}) collective-permute-start(bf16[1,4,2,128,128]{4,3,2,1,0:T(8,128)(2,1)} %shard_map.35), channel_id=1, source_target_pairs={{0,15},{1,8},{2,9},{3,10},{4,11},{5,12},{6,13},{7,14},{8,7},{9,0},... | collective-permute-start | bytes 786440 | tf_op jit(solution)/shard_map/ppermute | solution.py:21
  106.2 2.5 %shard_map.32.refs_4_ = bf16[2,4,2,128,128]{4,3,2,1,0:T(8,128)(2,1)S(1)} custom-call(s32[2]{0:T(128)S(1)} %get-tuple-element.56.places, bf16[2,2,4,128,256]{4,3,2,1,0:T(8,128)(2,1)S(1)} %pad_maximum_fusion.own.refs_0_.refs_1_, bf16[2,2,4,128,256]{4,3,2,1,0:T(8,128)(2,1)} %collective-permute-done.4.refs_0_, ...), custom_call_target="tpu_custom_call" | custom-call | tf_op jit(solution)/shard_map/pallas_call | solution.py:83
  108.6 2.1 %collective-permute-done.7.refs_4_ = bf16[1,4,2,128,128]{4,3,2,1,0:T(8,128)(2,1)S(1)} collective-permute-done((bf16[1,4,2,128,128]{4,3,2,1,0:T(8,128)(2,1)}, bf16[1,4,2,128,128]{4,3,2,1,0:T(8,128)(2,1)S(1)}, u32[]{:S(2)}, u32[]{:S(2)}) %collective-permute-start.7) | collective-permute-done | bytes 262176 | tf_op jit(solution)/shard_map/ppermute | solution.py:21
  110.8 2.9 %collective-permute-done.8.refs_5_ = bf16[1,4,2,128,128]{4,3,2,1,0:T(8,128)(2,1)} collective-permute-done((bf16[1,4,2,128,128]{4,3,2,1,0:T(8,128)(2,1)}, bf16[1,4,2,128,128]{4,3,2,1,0:T(8,128)(2,1)}, u32[]{:S(2)}, u32[]{:S(2)}) %collective-permute-start.8) | collective-permute-done | bytes 262176 | tf_op jit(solution)/shard_map/ppermute | solution.py:21
  113.7 0.0 collective-permute-done.6.refs_5_
  113.7 0.4 collective-permute-done.9.refs_0_
  114.1 0.4 shard_map.38
  114.6 0.4 shard_map.39
  115.0 0.0 copy-start.4
  115.0 0.0 copy-start.6
  115.0 0.0 copy-start.8
  115.1 0.4 collective-permute-start.11
  115.4 4.0 %collective-permute-start.12 = (bf16[1,4,2,128,128]{4,3,2,1,0:T(8,128)(2,1)S(1)}, bf16[1,4,2,128,128]{4,3,2,1,0:T(8,128)(2,1)S(1)}, u32[]{:S(2)}, u32[]{:S(2)}) collective-permute-start(bf16[1,4,2,128,128]{4,3,2,1,0:T(8,128)(2,1)S(1)} %shard_map.39), channel_id=1, source_target_pairs={{0,9},{1,10},{2,11},{3,12},{4,13},{5,14},{6,15},{7,8},{8,1},{9,2},... | collective-permute-start | bytes 786440 | tf_op jit(solution)/shard_map/ppermute | solution.py:21
  119.5 0.4 shard_map.37
  119.9 0.4 collective-permute-start.10
  120.3 0.4 shard_map.36.refs_0_
  120.8 3.8 %shard_map.40.refs_6_ = bf16[8,1,9,2,128,128]{5,4,3,2,1,0:T(8,128)(2,1)} custom-call(s32[1]{0:T(128)} %bitcast.column, bf16[2,4,2,128,128]{4,3,2,1,0:T(8,128)(2,1)S(1)} %copy-done.4, bf16[2,4,2,128,128]{4,3,2,1,0:T(8,128)(2,1)S(1)} %copy-done.8, bf16[2,4,2,128,128]{4,3,2,1,0:T(8,128)(2,1)S(1)} %copy-done.6, bf16[2,4,2,128,128]{4,3,2,1,0:T(8,128)(2,1)S(1)} %copy-done.10, ...), custom_call_target="tpu_custom_call" | custom-call | tf_op jit(solution)/shard_map/pallas_call | solution.py:126
  124.6 0.3 collective-permute-done.11.refs_2_
  125.0 5.6 %collective-permute-done.12.refs_3_ = bf16[1,4,2,128,128]{4,3,2,1,0:T(8,128)(2,1)S(1)} collective-permute-done((bf16[1,4,2,128,128]{4,3,2,1,0:T(8,128)(2,1)S(1)}, bf16[1,4,2,128,128]{4,3,2,1,0:T(8,128)(2,1)S(1)}, u32[]{:S(2)}, u32[]{:S(2)}) %collective-permute-start.12) | collective-permute-done | bytes 262176 | tf_op jit(solution)/shard_map/ppermute | solution.py:21
  130.6 1.0 collective-permute-done.10.refs_1_
  131.6 2.2 %shard_map.41 = bf16[8,1,9,2,128,128]{5,4,3,2,1,0:T(8,128)(2,1)} custom-call(s32[1]{0:T(128)} %bitcast.column, bf16[1,4,2,128,128]{4,3,2,1,0:T(8,128)(2,1)S(1)} %shard_map.36.refs_0_, bf16[1,4,2,128,128]{4,3,2,1,0:T(8,128)(2,1)S(1)} %collective-permute-done.10.refs_1_, ...), custom_call_target="tpu_custom_call", output_to_operand_aliasing={{}: (7, {})} | custom-call | tf_op jit(solution)/shard_map/pallas_call | solution.py:126
  (15 shorter events, 0.0 us)
Async XLA Ops:
  0.0 3.7 %copy-start = (bf16[1,8,69376]{2,1,0:T(8,128)(2,1)S(1)}, bf16[1,8,69376]{2,1,0:T(8,128)(2,1)}, u32[]{:S(2)}) copy-start(bf16[1,8,69376]{2,1,0:T(8,128)(2,1)} %param.2) | copy-start | bytes 3330052
  10.4 23.4 %all-to-all-start = ((bf16[32,2,4,8,256]{4,3,2,1,0:T(8,128)(2,1)}), bf16[32,2,4,8,256]{4,3,2,1,0:T(8,128)(2,1)S(1)}, u32[]{:S(2)}, u32[]{:S(2)}) async-start(bf16[32,2,4,8,256]{4,3,2,1,0:T(8,128)(2,1)} %bitcast.5), calls=%async_computation | async-start | bytes 2097152 | tf_op jit(solution)/shard_map/all_to_all | solution.py:151
  34.1 27.9 %collective-permute-start.2 = (bf16[2,2,4,128,256]{4,3,2,1,0:T(8,128)(2,1)S(1)}, bf16[2,2,4,128,256]{4,3,2,1,0:T(8,128)(2,1)S(1)}, u32[]{:S(2)}, u32[]{:S(2)}) collective-permute-start(bf16[2,2,4,128,256]{4,3,2,1,0:T(8,128)(2,1)S(1)} %pad_maximum_fusion.own.refs_0_.refs_1_), channel_id=1, source_target_pairs={{0,7},{1,0},{2,1},{3,2},{4,3},{5,4},{6,5},{7,6},{8,15},{9,8},{10,9... | collective-permute-start | bytes 3145736 | tf_op jit(solution)/shard_map/ppermute | solution.py:21
  40.1 25.5 %collective-permute-start.1 = (bf16[2,2,4,128,256]{4,3,2,1,0:T(8,128)(2,1)S(1)}, bf16[2,2,4,128,256]{4,3,2,1,0:T(8,128)(2,1)}, u32[]{:S(2)}, u32[]{:S(2)}) collective-permute-start(bf16[2,2,4,128,256]{4,3,2,1,0:T(8,128)(2,1)S(1)} %pad_maximum_fusion.own.refs_0_.refs_1_), channel_id=1, source_target_pairs={{0,1},{1,2},{2,3},{3,4},{4,5},{5,6},{6,7},{7,0},{8,9},{9,10},{10,1... | collective-permute-start | bytes 3145736 | tf_op jit(solution)/shard_map/ppermute | solution.py:21
  41.4 14.5 %collective-permute-start = (bf16[2,4,2,128,128]{4,3,2,1,0:T(8,128)(2,1)S(1)}, bf16[2,4,2,128,128]{4,3,2,1,0:T(8,128)(2,1)S(1)}, u32[]{:S(2)}, u32[]{:S(2)}) collective-permute-start(bf16[2,4,2,128,128]{4,3,2,1,0:T(8,128)(2,1)S(1)} %shard_map.29), channel_id=1, source_target_pairs={{0,8},{1,9},{2,10},{3,11},{4,12},{5,13},{6,14},{7,15},{8,0},{9,1},... | collective-permute-start | bytes 1572872 | tf_op jit(solution)/shard_map/ppermute | solution.py:21
  43.7 0.8 copy-start.3
  55.9 0.8 copy-start.7
  62.0 13.3 %copy-start.1 = (bf16[2,2,4,128,256]{4,3,2,1,0:T(8,128)(2,1)}, bf16[2,2,4,128,256]{4,3,2,1,0:T(8,128)(2,1)S(1)}, u32[]{:S(2)}) copy-start(bf16[2,2,4,128,256]{4,3,2,1,0:T(8,128)(2,1)S(1)} %collective-permute-done.2.refs_1_.own) | copy-start | bytes 3145732
  65.6 24.8 %collective-permute-start.4 = (bf16[2,2,4,128,256]{4,3,2,1,0:T(8,128)(2,1)}, bf16[2,2,4,128,256]{4,3,2,1,0:T(8,128)(2,1)}, u32[]{:S(2)}, u32[]{:S(2)}) collective-permute-start(bf16[2,2,4,128,256]{4,3,2,1,0:T(8,128)(2,1)} %collective-permute-done.1.refs_0_.own), channel_id=1, source_target_pairs={{0,1},{1,2},{2,3},{3,4},{4,5},{5,6},{6,7},{7,0},{8,9},{9,10},{10,1... | collective-permute-start | bytes 3145736 | tf_op jit(solution)/shard_map/ppermute | solution.py:21
  65.6 24.8 %collective-permute-start.5 = (bf16[2,2,4,128,256]{4,3,2,1,0:T(8,128)(2,1)S(1)}, bf16[2,2,4,128,256]{4,3,2,1,0:T(8,128)(2,1)}, u32[]{:S(2)}, u32[]{:S(2)}) collective-permute-start(bf16[2,2,4,128,256]{4,3,2,1,0:T(8,128)(2,1)S(1)} %collective-permute-done.2.refs_1_.own), channel_id=1, source_target_pairs={{0,7},{1,0},{2,1},{3,2},{4,3},{5,4},{6,5},{7,6},{8,15},{9,8},{10,9... | collective-permute-start | bytes 3145736 | tf_op jit(solution)/shard_map/ppermute | solution.py:21
  71.2 13.1 %collective-permute-start.3 = (bf16[2,4,2,128,128]{4,3,2,1,0:T(8,128)(2,1)S(1)}, bf16[2,4,2,128,128]{4,3,2,1,0:T(8,128)(2,1)S(1)}, u32[]{:S(2)}, u32[]{:S(2)}) collective-permute-start(bf16[2,4,2,128,128]{4,3,2,1,0:T(8,128)(2,1)S(1)} %shard_map.31), channel_id=1, source_target_pairs={{0,8},{1,9},{2,10},{3,11},{4,12},{5,13},{6,14},{7,15},{8,0},{9,1},... | collective-permute-start | bytes 1572872 | tf_op jit(solution)/shard_map/ppermute | solution.py:21
  75.4 0.8 copy-start.5
  84.3 0.8 copy-start.9
  90.4 23.8 %collective-permute-start.9 = (bf16[2,2,4,128,256]{4,3,2,1,0:T(8,128)(2,1)}, bf16[2,2,4,128,256]{4,3,2,1,0:T(8,128)(2,1)S(1)}, u32[]{:S(2)}, u32[]{:S(2)}) collective-permute-start(bf16[2,2,4,128,256]{4,3,2,1,0:T(8,128)(2,1)} %collective-permute-done.4.refs_0_), channel_id=1, source_target_pairs={{0,1},{1,2},{2,3},{3,4},{4,5},{5,6},{6,7},{7,0},{8,9},{9,10},{10,1... | collective-permute-start | bytes 3145736 | tf_op jit(solution)/shard_map/ppermute | solution.py:21
  93.7 20.0 %collective-permute-start.6 = (bf16[2,4,2,128,128]{4,3,2,1,0:T(8,128)(2,1)}, bf16[2,4,2,128,128]{4,3,2,1,0:T(8,128)(2,1)}, u32[]{:S(2)}, u32[]{:S(2)}) collective-permute-start(bf16[2,4,2,128,128]{4,3,2,1,0:T(8,128)(2,1)} %shard_map.33), channel_id=1, source_target_pairs={{0,8},{1,9},{2,10},{3,11},{4,12},{5,13},{6,14},{7,15},{8,0},{9,1},... | collective-permute-start | bytes 1572872 | tf_op jit(solution)/shard_map/ppermute | solution.py:21
  101.1 9.7 %collective-permute-start.7 = (bf16[1,4,2,128,128]{4,3,2,1,0:T(8,128)(2,1)}, bf16[1,4,2,128,128]{4,3,2,1,0:T(8,128)(2,1)S(1)}, u32[]{:S(2)}, u32[]{:S(2)}) collective-permute-start(bf16[1,4,2,128,128]{4,3,2,1,0:T(8,128)(2,1)} %shard_map.34), channel_id=1, source_target_pairs={{0,7},{1,0},{2,1},{3,2},{4,3},{5,4},{6,5},{7,6},{8,15},{9,8},{10,9... | collective-permute-start | bytes 786440 | tf_op jit(solution)/shard_map/ppermute | solution.py:21
  104.3 9.4 %collective-permute-start.8 = (bf16[1,4,2,128,128]{4,3,2,1,0:T(8,128)(2,1)}, bf16[1,4,2,128,128]{4,3,2,1,0:T(8,128)(2,1)}, u32[]{:S(2)}, u32[]{:S(2)}) collective-permute-start(bf16[1,4,2,128,128]{4,3,2,1,0:T(8,128)(2,1)} %shard_map.35), channel_id=1, source_target_pairs={{0,15},{1,8},{2,9},{3,10},{4,11},{5,12},{6,13},{7,14},{8,7},{9,0},... | collective-permute-start | bytes 786440 | tf_op jit(solution)/shard_map/ppermute | solution.py:21
  106.1 8.0 %copy-start.2 = (bf16[2,2,4,128,256]{4,3,2,1,0:T(8,128)(2,1)S(1)}, bf16[2,2,4,128,256]{4,3,2,1,0:T(8,128)(2,1)}, u32[]{:S(2)}) copy-start(bf16[2,2,4,128,256]{4,3,2,1,0:T(8,128)(2,1)} %copy-done.1) | copy-start | bytes 3145732
  115.0 5.8 %copy-start.4 = (bf16[2,4,2,128,128]{4,3,2,1,0:T(8,128)(2,1)S(1)}, bf16[2,4,2,128,128]{4,3,2,1,0:T(8,128)(2,1)}, u32[]{:S(2)}) copy-start(bf16[2,4,2,128,128]{4,3,2,1,0:T(8,128)(2,1)} %copy-done.3) | copy-start | bytes 1572868
  115.0 5.8 %copy-start.6 = (bf16[2,4,2,128,128]{4,3,2,1,0:T(8,128)(2,1)S(1)}, bf16[2,4,2,128,128]{4,3,2,1,0:T(8,128)(2,1)}, u32[]{:S(2)}) copy-start(bf16[2,4,2,128,128]{4,3,2,1,0:T(8,128)(2,1)} %copy-done.5) | copy-start | bytes 1572868
  115.0 5.8 %copy-start.8 = (bf16[2,4,2,128,128]{4,3,2,1,0:T(8,128)(2,1)S(1)}, bf16[2,4,2,128,128]{4,3,2,1,0:T(8,128)(2,1)}, u32[]{:S(2)}) copy-start(bf16[2,4,2,128,128]{4,3,2,1,0:T(8,128)(2,1)} %copy-done.7) | copy-start | bytes 1572868
  115.0 5.8 %copy-start.10 = (bf16[2,4,2,128,128]{4,3,2,1,0:T(8,128)(2,1)S(1)}, bf16[2,4,2,128,128]{4,3,2,1,0:T(8,128)(2,1)}, u32[]{:S(2)}) copy-start(bf16[2,4,2,128,128]{4,3,2,1,0:T(8,128)(2,1)} %copy-done.9) | copy-start | bytes 1572868
  115.1 9.9 %collective-permute-start.11 = (bf16[1,4,2,128,128]{4,3,2,1,0:T(8,128)(2,1)S(1)}, bf16[1,4,2,128,128]{4,3,2,1,0:T(8,128)(2,1)S(1)}, u32[]{:S(2)}, u32[]{:S(2)}) collective-permute-start(bf16[1,4,2,128,128]{4,3,2,1,0:T(8,128)(2,1)S(1)} %shard_map.38), channel_id=1, source_target_pairs={{0,1},{1,2},{2,3},{3,4},{4,5},{5,6},{6,7},{7,0},{8,9},{9,10},{10,1... | collective-permute-start | bytes 786440 | tf_op jit(solution)/shard_map/ppermute | solution.py:21
  115.4 15.2 %collective-permute-start.12 = (bf16[1,4,2,128,128]{4,3,2,1,0:T(8,128)(2,1)S(1)}, bf16[1,4,2,128,128]{4,3,2,1,0:T(8,128)(2,1)S(1)}, u32[]{:S(2)}, u32[]{:S(2)}) collective-permute-start(bf16[1,4,2,128,128]{4,3,2,1,0:T(8,128)(2,1)S(1)} %shard_map.39), channel_id=1, source_target_pairs={{0,9},{1,10},{2,11},{3,12},{4,13},{5,14},{6,15},{7,8},{8,1},{9,2},... | collective-permute-start | bytes 786440 | tf_op jit(solution)/shard_map/ppermute | solution.py:21
  119.9 11.6 %collective-permute-start.10 = (bf16[1,4,2,128,128]{4,3,2,1,0:T(8,128)(2,1)S(1)}, bf16[1,4,2,128,128]{4,3,2,1,0:T(8,128)(2,1)S(1)}, u32[]{:S(2)}, u32[]{:S(2)}) collective-permute-start(bf16[1,4,2,128,128]{4,3,2,1,0:T(8,128)(2,1)S(1)} %shard_map.37), channel_id=1, source_target_pairs={{0,8},{1,9},{2,10},{3,11},{4,12},{5,13},{6,14},{7,15},{8,0},{9,1},... | collective-permute-start | bytes 786440 | tf_op jit(solution)/shard_map/ppermute | solution.py:21
